TPU v7x, 32 devices: a whole 2x2x4 slice. The times are simulated.
32 devices in a mesh: section: 2 (over core), ctx: 4 (over z), wa: 4 (over y, x).
Axes of the slice: x: 2, y: 2, z: 4, core: 2. Of those that a mesh axis runs over, the one named last changes fastest.
Arguments:
- block_input: bfloat16 [2, 2048, 960], P(None, ('ctx', 'wa')), may hold values from -6 to 6
- out_cotangent: bfloat16 [2, 2048, 960], P(None, ('ctx', 'wa')), may hold values from -6 to 6
- block_table: int32 [32], replicated, may hold values from 0 to 31, as said below
- attn_gain: bfloat16 [2, 960], P('section', 'wa'), may hold values from 0.099609375 to 1.8984375
- w_qkv: bfloat16 [2, 960, 1600], P('section', 'wa'), may hold values from -0.1875 to 0.1875
- w_out: bfloat16 [2, 960, 960], P('section', 'wa'), may hold values from -6 to 6
- mlp_gain: bfloat16 [2, 960], P('section', 'wa'), may hold values from 0.099609375 to 1.8984375
- w_gate: bfloat16 [2, 960, 2560], P('section', 'wa'), may hold values from -0.1875 to 0.1875
- w_up: bfloat16 [2, 960, 2560], P('section', 'wa'), may hold values from -0.1875 to 0.1875
- w_down: bfloat16 [2, 2560, 960], P('section', 'wa'), may hold values from -0.125 to 0.125
Outputs:
- layer_outputs: bfloat16 [2, 2, 2048, 960], P('section', None, ('ctx', 'wa'))
- input_grads: bfloat16 [2, 2, 2048, 960], P('section', None, ('ctx', 'wa'))
- attn_gain_grad: float32 [2, 960], P('section', 'wa')
- w_qkv_grad: float32 [2, 960, 1600], P('section', 'wa')
- w_out_grad: float32 [2, 960, 960], P('section', 'wa')
- mlp_gain_grad: float32 [2, 960], P('section', 'wa')
- w_gate_grad: float32 [2, 960, 2560], P('section', 'wa')
- w_up_grad: float32 [2, 960, 2560], P('section', 'wa')
- w_down_grad: float32 [2, 2560, 960], P('section', 'wa')
Inputs may be any that keep to these rules, and one draw needn't show every extreme that they name: `block_table`: stored blocks 2j and 2j+1 hold positional blocks b and 31 - b for some b, in either order; every positional block is held once.
All inputs are finite; a program needn't handle non-finite values.
Results may differ from a plain program's by a relative error of at most 0.015.
Values may be sent and summed in bfloat16 or wider, within the bound.
No kernel may reach another device: no remote copies, remote signals or barrier semaphores. Data moves between devices by JAX's collectives and lax.ppermute only.
A program may use at most 256 MiB of HBM per device.

v0:
```python
import math

import jax
import jax.numpy as jnp
from jax import lax
from jax.sharding import PartitionSpec as P

H = 15
KVH = 5
HD = 64


EPSILON = 1e-05
ROPE_BASE = 100000.0
MASKED = -1e30


def split_up(shard, dim, devices):
    before, after = (shard.shape[:dim], shard.shape[dim + 1 :])
    return jnp.moveaxis(shard.reshape(*before, devices, -1, *after), dim, 0)


def summed_on_arrival(shard, axis, dim):
    devices = lax.axis_size(axis)
    blocks = lax.all_to_all(split_up(shard, dim, devices), axis, 0, 0, tiled=True)
    return jnp.sum(blocks.astype(jnp.float32), axis=0)


def shifted(value, axis, steps):
    count = lax.axis_size(axis)
    leading, last = (max(0, -steps), min(count, count - steps))
    return lax.ppermute(value, axis, [(source, source + steps) for source in range(leading, last)])


def as_sent(shard):
    return jax.tree.map(lambda a: a.astype(jnp.bfloat16) if a.dtype == jnp.float32 else a, shard)


def rotary_tables(positions, head_size):
    half_size = head_size // 2
    inverse = ROPE_BASE ** (-(jnp.arange(half_size, dtype=jnp.float32) * 2.0) / head_size)
    angles = positions.astype(jnp.float32)[:, None] * inverse[None, :]
    return (jnp.cos(angles), jnp.sin(angles))


def rotate(values, cos_table, sin_table):
    half_size = values.shape[-1] // 2
    front_half = values[..., :half_size]
    back_half = values[..., half_size:]
    cos_wide = cos_table[:, None, :]
    sin_wide = sin_table[:, None, :]
    return jnp.concatenate(
        [
            front_half * cos_wide - back_half * sin_wide,
            back_half * cos_wide + front_half * sin_wide,
        ],
        axis=-1,
    )


def norm_back(values, scaling, gain, gradient):
    gain_grad = jnp.sum(gradient * values * scaling, axis=0)
    scaled = gradient * gain.astype(jnp.float32)
    inner = jnp.mean(scaled * values, axis=-1, keepdims=True)
    return (gain_grad, scaling * scaled - values * scaling**3 * inner)


def place_slot(buffer, value, slot_index, micro_count):
    is_valid = (slot_index >= 0) & (slot_index < micro_count)
    clipped = jnp.clip(slot_index, 0, micro_count - 1)
    current = lax.dynamic_index_in_dim(buffer, clipped, 0, keepdims=False)
    updated = jnp.where(is_valid, value, current)
    return lax.dynamic_update_index_in_dim(buffer, updated, clipped, 0)


def per_device(
    block_input, out_cotangent, block_table, attn_gain, w_qkv, w_out, mlp_gain, w_gate, w_up, w_down
):
    sections = lax.axis_size("section")
    section_idx = lax.axis_index("section")
    micro_count, tok_rows, feature_count = block_input.shape
    head_count, kv_heads, head_size = (H, KVH, HD)
    group_size = head_count // kv_heads
    kv_width = kv_heads * head_size
    query_width = head_count * head_size
    block_total = block_table.shape[0]
    half_rows = tok_rows // 2
    seq_rows = block_total * half_rows
    score_scale = head_size ** (-0.5)
    fetched = (
        lax.all_gather(attn_gain, "wa", axis=1, tiled=True),
        lax.all_gather(w_qkv, "wa", axis=1, tiled=True),
        lax.all_gather(w_out, "wa", axis=1, tiled=True),
        lax.all_gather(mlp_gain, "wa", axis=1, tiled=True),
        lax.all_gather(w_gate, "wa", axis=1, tiled=True),
        lax.all_gather(w_up, "wa", axis=1, tiled=True),
        lax.all_gather(w_down, "wa", axis=1, tiled=True),
    )
    gain_one, qkv_full, out_full, gain_two, gate_full, up_full, down_full = [
        member[0] for member in fetched
    ]
    all_pos = jnp.repeat(block_table, half_rows) * half_rows + jnp.tile(
        jnp.arange(half_rows, dtype=jnp.int32), block_total
    )
    device = lax.axis_index(("ctx", "wa"))
    own_pos = lax.dynamic_slice_in_dim(all_pos, device * tok_rows, tok_rows)
    cos_table, sin_table = rotary_tables(own_pos, head_size)
    key_block = math.gcd(seq_rows, 1024)
    key_count = seq_rows // key_block
    key_pos = all_pos.reshape(key_count, key_block)

    def blocks_of(kv_all):
        return kv_all.reshape(key_count, key_block, 2, kv_heads, head_size)

    def scores_of(queries, key_rows, positions):
        raw_scores = (
            jnp.einsum("tkgd,skd->kgts", queries, key_rows, preferred_element_type=jnp.float32)
            * score_scale
        )
        allowed = positions[None, None, None, :] <= own_pos[None, None, :, None]
        return (jnp.where(allowed, raw_scores, MASKED), allowed)

    def softmax_totals(queries, kv_all):

        def advance(carry, inputs):
            running_top, running_sum = carry
            kv_rows, positions = inputs
            raw_scores, allowed = scores_of(queries, kv_rows[:, 0], positions)
            new_top = jnp.maximum(running_top, raw_scores.max(axis=-1))
            fresh = jnp.where(allowed, jnp.exp(raw_scores - new_top[..., None]), 0.0)
            running_sum = running_sum * jnp.exp(running_top - new_top) + jnp.sum(fresh, axis=-1)
            return ((new_top, running_sum), None)

        initial = (
            jnp.full((kv_heads, group_size, tok_rows), MASKED, jnp.float32),
            jnp.zeros((kv_heads, group_size, tok_rows), jnp.float32),
        )
        (running_top, running_sum), _ = lax.scan(advance, initial, (blocks_of(kv_all), key_pos))
        return running_top + jnp.log(running_sum)

    def attend_values(queries, kv_all, log_total):

        def advance(accumulated, inputs):
            kv_rows, positions = inputs
            raw_scores, allowed = scores_of(queries, kv_rows[:, 0], positions)
            probabilities = jnp.exp(raw_scores - log_total[..., None]).astype(jnp.bfloat16)
            return (
                accumulated
                + jnp.einsum(
                    "kgts,skd->tkgd",
                    probabilities,
                    kv_rows[:, 1],
                    preferred_element_type=jnp.float32,
                ),
                None,
            )

        initial = jnp.zeros((tok_rows, kv_heads, group_size, head_size), jnp.float32)
        accumulated, _ = lax.scan(advance, initial, (blocks_of(kv_all), key_pos))
        return accumulated

    tick_count = micro_count + sections - 1
    empty_rows = jnp.zeros((micro_count, tok_rows, feature_count), jnp.bfloat16)
    layer_out = empty_rows
    records = []
    previous = None
    for step_index in range(tick_count):
        first_in = block_input[min(step_index, micro_count - 1)]
        if step_index == 0:
            inflow = first_in
        else:
            passed = shifted(previous, "section", 1)
            inflow = jnp.where(section_idx == 0, first_in, passed)
        forward_residual = inflow.astype(jnp.float32)
        forward_scale_one = lax.rsqrt(
            jnp.mean(forward_residual * forward_residual, axis=-1, keepdims=True) + EPSILON
        )
        forward_normed = (
            forward_residual * forward_scale_one * gain_one.astype(jnp.float32)
        ).astype(jnp.bfloat16)
        mixed_proj = jnp.dot(forward_normed, qkv_full, preferred_element_type=jnp.float32)
        forward_queries = rotate(
            mixed_proj[:, :query_width].reshape(tok_rows, head_count, head_size),
            cos_table,
            sin_table,
        ).astype(jnp.bfloat16)
        key_rot = rotate(
            mixed_proj[:, query_width : query_width + kv_width].reshape(
                tok_rows, kv_heads, head_size
            ),
            cos_table,
            sin_table,
        )
        forward_kv_local = jnp.concatenate(
            [key_rot.reshape(tok_rows, kv_width), mixed_proj[:, query_width + kv_width :]], axis=1
        ).astype(jnp.bfloat16)
        forward_kv_all = lax.all_gather(forward_kv_local, ("ctx", "wa"), axis=0, tiled=True)
        forward_queries = forward_queries.reshape(tok_rows, kv_heads, group_size, head_size)
        forward_log_total = softmax_totals(forward_queries, forward_kv_all)
        forward_attended = attend_values(forward_queries, forward_kv_all, forward_log_total)
        forward_flat_low = forward_attended.reshape(tok_rows, query_width).astype(jnp.bfloat16)
        forward_middle = forward_residual + jnp.dot(
            forward_flat_low, out_full, preferred_element_type=jnp.float32
        )
        forward_scale_two = lax.rsqrt(
            jnp.mean(forward_middle * forward_middle, axis=-1, keepdims=True) + EPSILON
        )
        forward_second = (forward_middle * forward_scale_two * gain_two.astype(jnp.float32)).astype(
            jnp.bfloat16
        )
        forward_gate_proj = jnp.dot(forward_second, gate_full, preferred_element_type=jnp.float32)
        forward_up_proj = jnp.dot(forward_second, up_full, preferred_element_type=jnp.float32)
        forward_hidden = (jax.nn.silu(forward_gate_proj) * forward_up_proj).astype(jnp.bfloat16)
        outflow = (
            forward_middle + jnp.dot(forward_hidden, down_full, preferred_element_type=jnp.float32)
        ).astype(jnp.bfloat16)
        forward_record = (
            forward_residual,
            forward_scale_one,
            forward_normed,
            forward_kv_local,
            None,
            forward_queries,
            forward_log_total,
            forward_attended,
            forward_flat_low,
            forward_middle,
            forward_scale_two,
            forward_second,
            forward_gate_proj,
            forward_up_proj,
            forward_hidden,
        )
        outflow, record = (outflow, forward_record)
        records.append(record)
        layer_out = place_slot(layer_out, outflow, step_index - section_idx, micro_count)
        previous = outflow
    grad_sums = None
    input_grad = empty_rows
    previous = None
    for step_index in range(tick_count):
        record = records[tick_count - 1 - step_index]
        slot_index = micro_count + sections - 2 - step_index - section_idx
        last_in = out_cotangent[max(micro_count - 1 - step_index, 0)]
        if step_index == 0:
            inflow_grad = last_in
        else:
            passed = shifted(previous, "section", -1)
            inflow_grad = jnp.where(section_idx == sections - 1, last_in, passed)
        (
            residual,
            scale_one,
            normed,
            kv_local,
            kept_kv,
            backward_queries,
            backward_log_total,
            attended,
            flat_low,
            middle,
            scale_two,
            second,
            gate_proj,
            up_proj,
            hidden,
        ) = record
        grad_y = inflow_grad.astype(jnp.float32)
        down_grad = jnp.einsum("tf,td->fd", hidden, inflow_grad, preferred_element_type=jnp.float32)
        grad_hidden = jnp.einsum(
            "td,fd->tf", inflow_grad, down_full, preferred_element_type=jnp.float32
        )
        sigmoid_gate = jax.nn.sigmoid(gate_proj)
        silu_gate = gate_proj * sigmoid_gate
        grad_gate = (
            grad_hidden * up_proj * sigmoid_gate * (1.0 + gate_proj * (1.0 - sigmoid_gate))
        ).astype(jnp.bfloat16)
        grad_up = (grad_hidden * silu_gate).astype(jnp.bfloat16)
        gate_grad = jnp.einsum("td,tf->df", second, grad_gate, preferred_element_type=jnp.float32)
        up_grad = jnp.einsum("td,tf->df", second, grad_up, preferred_element_type=jnp.float32)
        grad_second = jnp.einsum(
            "tf,df->td", grad_gate, gate_full, preferred_element_type=jnp.float32
        )
        grad_second = grad_second + jnp.einsum(
            "tf,df->td", grad_up, up_full, preferred_element_type=jnp.float32
        )
        gain_two_grad, grad_norm_two = norm_back(middle, scale_two, gain_two, grad_second)
        grad_middle = grad_y + grad_norm_two
        grad_middle_low = grad_middle.astype(jnp.bfloat16)
        out_grad = jnp.einsum(
            "tq,td->qd", flat_low, grad_middle_low, preferred_element_type=jnp.float32
        )
        backward_grad_attended = jnp.einsum(
            "td,qd->tq", grad_middle_low, out_full, preferred_element_type=jnp.float32
        ).astype(jnp.bfloat16)
        backward_grad_attended = backward_grad_attended.reshape(
            tok_rows, kv_heads, group_size, head_size
        )
        backward_delta_rows = jnp.einsum(
            "tkgd,tkgd->kgt", backward_grad_attended.astype(jnp.float32), attended
        )
        backward_kv_all = lax.all_gather(kv_local, ("ctx", "wa"), axis=0, tiled=True)
        attend_queries = backward_queries
        attend_log_total = backward_log_total
        grad_attended = backward_grad_attended
        delta_rows = backward_delta_rows

        def attend_advance(grad_queries, inputs):
            kv_rows, positions = inputs
            raw_scores, allowed = scores_of(attend_queries, kv_rows[:, 0], positions)
            probabilities = jnp.exp(raw_scores - attend_log_total[..., None])
            prob_low = probabilities.astype(jnp.bfloat16)
            grad_values = jnp.einsum(
                "kgts,tkgd->skd", prob_low, grad_attended, preferred_element_type=jnp.float32
            )
            grad_probs = jnp.einsum(
                "tkgd,skd->kgts", grad_attended, kv_rows[:, 1], preferred_element_type=jnp.float32
            )
            grad_scores = (probabilities * (grad_probs - delta_rows[..., None])).astype(
                jnp.bfloat16
            )
            grad_queries = (
                grad_queries
                + jnp.einsum(
                    "kgts,skd->tkgd", grad_scores, kv_rows[:, 0], preferred_element_type=jnp.float32
                )
                * score_scale
            )
            grad_keys = (
                jnp.einsum(
                    "kgts,tkgd->skd",
                    grad_scores,
                    attend_queries,
                    preferred_element_type=jnp.float32,
                )
                * score_scale
            )
            return (grad_queries, (grad_keys, grad_values))

        attend_initial = jnp.zeros((tok_rows, kv_heads, group_size, head_size), jnp.float32)
        grad_queries, (grad_keys, grad_values) = lax.scan(
            attend_advance, attend_initial, (blocks_of(backward_kv_all), key_pos)
        )
        grad_terms = jnp.concatenate(
            [grad_keys.reshape(seq_rows, kv_width), grad_values.reshape(seq_rows, kv_width)], axis=1
        )
        backward_grad_terms = grad_terms
        grad_kv = summed_on_arrival(backward_grad_terms.astype(jnp.bfloat16), ("ctx", "wa"), 0)
        backward_grad_keys = rotate(
            grad_kv[:, :kv_width].reshape(tok_rows, kv_heads, head_size), cos_table, -sin_table
        ).reshape(tok_rows, kv_width)
        grad_query_raw = rotate(
            grad_queries.reshape(tok_rows, head_count, head_size), cos_table, -sin_table
        ).reshape(tok_rows, query_width)
        grad_mixed = jnp.concatenate(
            [grad_query_raw, backward_grad_keys, grad_kv[:, kv_width:]], axis=1
        ).astype(jnp.bfloat16)
        qkv_grad = jnp.einsum("td,tc->dc", normed, grad_mixed, preferred_element_type=jnp.float32)
        grad_normed = jnp.einsum(
            "tc,dc->td", grad_mixed, qkv_full, preferred_element_type=jnp.float32
        )
        gain_one_grad, grad_norm_one = norm_back(residual, scale_one, gain_one, grad_normed)
        outflow_grad = (grad_middle + grad_norm_one).astype(jnp.bfloat16)
        outflow_grad, grad_terms = (
            outflow_grad,
            (gain_one_grad, qkv_grad, out_grad, gain_two_grad, gate_grad, up_grad, down_grad),
        )
        is_valid = (slot_index >= 0) & (slot_index < micro_count)
        grad_terms = tuple((jnp.where(is_valid, member, 0.0) for member in grad_terms))
        if grad_sums is None:
            grad_sums = grad_terms
        else:
            grad_sums = tuple(
                (left_sum + right_sum for left_sum, right_sum in zip(grad_sums, grad_terms))
            )
        input_grad = place_slot(input_grad, outflow_grad, slot_index, micro_count)
        previous = outflow_grad
    shares = jax.tree.map(
        lambda part: part.astype(jnp.float32),
        lax.psum_scatter(as_sent(grad_sums), "wa", scatter_dimension=0, tiled=True),
    )
    shares = jax.tree.map(lambda part: part.astype(jnp.float32), lax.psum(as_sent(shares), "ctx"))
    return (
        layer_out[None],
        input_grad[None],
        shares[0][None],
        shares[1][None],
        shares[2][None],
        shares[3][None],
        shares[4][None],
        shares[5][None],
        shares[6][None],
    )


def solution(mesh):
    return jax.shard_map(
        per_device,
        mesh=mesh,
        in_specs=(
            P(None, ("ctx", "wa"), None),
            P(None, ("ctx", "wa"), None),
            P(),
            P("section", "wa"),
            P("section", "wa", None),
            P("section", "wa", None),
            P("section", "wa"),
            P("section", "wa", None),
            P("section", "wa", None),
            P("section", "wa", None),
        ),
        out_specs=(
            P("section", None, ("ctx", "wa"), None),
            P("section", None, ("ctx", "wa"), None),
            P("section", "wa"),
            P("section", "wa", None),
            P("section", "wa", None),
            P("section", "wa"),
            P("section", "wa", None),
            P("section", "wa", None),
            P("section", "wa", None),
        ),
        check_vma=False,
    )
```

profile of v0, /device:TPU:1, one launch (start us, length us, event | category | flops | bytes accessed | tf_op | source)
XLA Modules:
  0.0 1388.5 jit_solution(17188675878534255876)
XLA Ops:
  11.8 8.7 all-reduce.6
  23.8 32.5 %all-gather.9.cloned.1.call-done = bf16[1,960,1600]{2,1,0:T(8,128)(2,1)} async-done(((bf16[1,240,1600]{2,1,0:T(8,128)(2,1)}), bf16[1,960,1600]{2,1,0:T(8,128)(2,1)}) %all-gather.9.cloned.1.call-update) | async-done | bytes 3072016 | tf_op jit(solution)/shard_map/all_gather | solution.py:92
  64.0 66.4 %all-gather.11.cloned.1.call-done = bf16[2048,640]{0,1:T(8,128)(2,1)} async-done(((bf16[128,640]{0,1:T(8,128)(2,1)}), bf16[2048,640]{0,1:T(8,128)(2,1)}) %all-gather.11.cloned.1.call-update) | async-done | bytes 2621456 | tf_op jit(solution)/shard_map/all_gather | solution.py:197
  130.4 5.5 reshape.712
  138.5 20.1 %while.117 = (s32[]{:T(128)}, f32[5,3,128]{2,1,0:T(4,128)S(1)}, f32[5,3,128]{2,1,0:T(4,128)S(1)}, s32[2,1024]{1,0:T(2,128)S(1)}, s32[128]{0:T(128)S(1)}, /*index...) while((s32[]{:T(128)}, f32[5,3,128]{2,1,0:T(4,128)S(1)}, ...), condition=%wide.region_4.5_spmd.clone, body=%wide.region_1.4_spmd.clone.sunk | while | flops 267527552 | bytes 19757176 | solution.py:138
  138.8 4.5 fusion.446
  143.4 5.1 select_reduce_fusion.6
  148.9 4.5 fusion.446
  153.4 5.1 select_reduce_fusion.6
  159.2 12.1 while.118
  160.6 4.5 fusion.450
  166.6 4.7 fusion.450
  177.3 48.3 %all-gather.15.cloned.1.call-done = bf16[1,960,2560]{2,1,0:T(8,128)(2,1)} async-done(((bf16[1,240,2560]{2,1,0:T(8,128)(2,1)}), bf16[1,960,2560]{2,1,0:T(8,128)(2,1)}) %all-gather.15.cloned.1.call-update) | async-done | bytes 4915216 | tf_op jit(solution)/shard_map/all_gather | solution.py:95
  229.9 56.1 %all-gather.17.cloned.1.call-done = bf16[1,960,2560]{2,1,0:T(8,128)(2,1)} async-done(((bf16[1,240,2560]{2,1,0:T(8,128)(2,1)}), bf16[1,960,2560]{2,1,0:T(8,128)(2,1)}) %all-gather.17.cloned.1.call-update) | async-done | bytes 4915216 | tf_op jit(solution)/shard_map/all_gather | solution.py:96
  286.0 5.0 multiply_convert_fusion.8
  291.0 55.4 %all-gather.19.cloned.1.call-done = bf16[1,2560,960]{1,2,0:T(8,128)(2,1)} async-done(((bf16[1,640,960]{1,2,0:T(8,128)(2,1)}), bf16[1,2560,960]{1,2,0:T(8,128)(2,1)}) %all-gather.19.cloned.1.call-update) | async-done | bytes 4915216 | tf_op jit(solution)/shard_map/all_gather | solution.py:97
  347.3 5.0 bitcast_dynamic-update-slice_fusion.3
  363.8 66.2 %all-gather.21.cloned.1.call-done = bf16[2048,640]{0,1:T(8,128)(2,1)} async-done(((bf16[128,640]{0,1:T(8,128)(2,1)}), bf16[2048,640]{0,1:T(8,128)(2,1)}) %all-gather.21.cloned.1.call-update) | async-done | bytes 2621456 | tf_op jit(solution)/shard_map/all_gather | solution.py:197
  430.0 5.5 reshape.716
  438.1 20.1 %while.119 = (s32[]{:T(128)}, f32[5,3,128]{2,1,0:T(4,128)S(1)}, f32[5,3,128]{2,1,0:T(4,128)S(1)}, s32[2,1024]{1,0:T(2,128)S(1)}, s32[128]{0:T(128)S(1)}, /*index...) while((s32[]{:T(128)}, f32[5,3,128]{2,1,0:T(4,128)S(1)}, ...), condition=%wide.region_12.13_spmd.clone, body=%wide.region_9.12_spmd.clone.sunk | while | flops 267527552 | bytes 19757176 | solution.py:138
  438.4 4.5 fusion.452
  442.9 5.1 select_reduce_fusion.7
  448.4 4.5 fusion.452
  453.0 5.1 select_reduce_fusion.7
  458.1 12.0 while.120
  459.6 4.5 fusion.456
  465.5 4.6 fusion.456
  478.4 4.9 multiply_convert_fusion.7
  492.4 4.3 fusion.127
  496.8 63.3 %all-gather.23.cloned.1.call-done = bf16[2048,640]{0,1:T(8,128)(2,1)} async-done(((bf16[128,640]{0,1:T(8,128)(2,1)}), bf16[2048,640]{0,1:T(8,128)(2,1)}) %all-gather.23.cloned.1.call-update) | async-done | bytes 2621456 | tf_op jit(solution)/shard_map/all_gather | solution.py:197
  560.2 5.5 reshape.720
  568.2 21.3 %while.121 = (s32[]{:T(128)}, f32[5,3,128]{2,1,0:T(4,128)S(1)}, f32[5,3,128]{2,1,0:T(4,128)}, s32[2,1024]{1,0:T(2,128)S(1)}, s32[128]{0:T(128)S(1)}, /*index=5*/...) while((s32[]{:T(128)}, f32[5,3,128]{2,1,0:T(4,128)S(1)}, ...), condition=%wide.region_20.21_spmd.clone, body=%wide.region_17.20_spmd.clone.sunk | while | flops 267527552 | bytes 19818672 | solution.py:138
  568.6 4.5 fusion.458
  573.1 5.1 select_reduce_fusion.8
  579.2 4.5 fusion.458
  583.7 5.1 select_reduce_fusion.8
  590.2 12.3 while.122
  591.7 4.5 fusion.462
  597.7 4.7 fusion.462
  610.1 5.3 multiply_convert_fusion.5
  623.3 29.6 %while.123 = (s32[]{:T(128)}, f32[128,5,3,64]{0,3,2,1:T(8,128)S(1)}, bf16[2,1024,5,64]{1,3,2,0:T(8,128)(2,1)}, bf16[2,1024,5,64]{1,3,2,0:T(8,128)(2,1)}, bf16[2,...) while((s32[]{:T(128)}, f32[128,5,3,64]{0,3,2,1:T(8,128)S(1)}, ...), condition=%wide.region_26.27_spmd.clone, body=%wide.region_25.26_spmd.clone.sunk | while | flops 1278779392 | bytes 130881888 | solution.py:340
  672.6 50.2 %all-to-all-done = bf16[16,128,640]{1,2,0:T(8,128)(2,1)S(1)} async-done(((bf16[16,128,640]{1,2,0:T(8,128)(2,1)}), bf16[16,128,640]{1,2,0:T(8,128)(2,1)S(1)}, u32[]{:S(2)}, u32[]{:S(2)}) %all-to-all-start) | async-done | bytes 2621472 | tf_op jit(solution)/shard_map/all_to_all | solution.py:25
  728.2 5.1 collective-permute-start.2
  740.8 4.7 multiply_reduce_fusion.1
  749.7 29.4 %while.124 = (s32[]{:T(128)}, f32[128,5,3,64]{0,3,2,1:T(8,128)S(1)}, bf16[2,1024,5,64]{1,3,2,0:T(8,128)(2,1)}, bf16[2,1024,5,64]{1,3,2,0:T(8,128)(2,1)}, bf16[2,...) while((s32[]{:T(128)}, f32[128,5,3,64]{0,3,2,1:T(8,128)S(1)}, ...), condition=%wide.region_31.32_spmd.clone, body=%wide.region_30.31_spmd.clone.sunk | while | flops 1278779392 | bytes 130943392 | solution.py:340
  794.8 12.4 all-to-all-start.1
  807.3 5.1 fusion.286
  814.0 43.6 %all-to-all-done.1 = bf16[16,128,640]{1,2,0:T(8,128)(2,1)} async-done(((bf16[16,128,640]{1,2,0:T(8,128)(2,1)}), bf16[16,128,640]{1,2,0:T(8,128)(2,1)}, u32[]{:S(2)}, u32[]{:S(2)}) %all-to-all-start.1) | async-done | bytes 2621472 | tf_op jit(solution)/shard_map/all_to_all | solution.py:25
  862.8 4.7 collective-permute-start.3
  869.7 4.7 add_convert_fusion
  874.4 7.9 copy.151
  885.2 4.5 multiply_convert_fusion.1
  909.2 5.1 add_convert_fusion.1
  916.8 29.8 %while.125 = (s32[]{:T(128)}, f32[128,5,3,64]{0,3,2,1:T(8,128)S(1)}, bf16[2,1024,5,64]{1,3,2,0:T(8,128)(2,1)}, bf16[2,1024,5,64]{1,3,2,0:T(8,128)(2,1)}, bf16[2,...) while((s32[]{:T(128)}, f32[128,5,3,64]{0,3,2,1:T(8,128)S(1)}, ...), condition=%wide.region_36.37_spmd.clone, body=%wide.region_35.36_spmd.clone.sunk | while | flops 1278779392 | bytes 130943392 | solution.py:340
  962.2 13.6 all-to-all-start.2
  975.9 4.8 fusion.296
  984.6 42.0 %all-to-all-done.2 = bf16[16,128,640]{1,2,0:T(8,128)(2,1)S(1)} async-done(((bf16[16,128,640]{1,2,0:T(8,128)(2,1)}), bf16[16,128,640]{1,2,0:T(8,128)(2,1)S(1)}, u32[]{:S(2)}, u32[]{:S(2)}) %all-to-all-start.2) | async-done | bytes 2621472 | tf_op jit(solution)/shard_map/all_to_all | solution.py:25
  1027.0 8.1 add_convert_fusion.3
  1037.8 39.6 %reduce-scatter.12.cloned.1.call-done = bf16[240,2560]{1,0:T(8,128)(2,1)} async-done(((bf16[960,2560]{1,0:T(8,128)(2,1)}), bf16[240,2560]{1,0:T(8,128)(2,1)}) %reduce-scatter.12.cloned.1.call-update) | async-done | bytes 1228816 | tf_op jit(solution)/shard_map/reduce_scatter | solution.py:379
  1077.3 61.6 %reduce-scatter.14.cloned.1.call-done = bf16[240,2560]{1,0:T(8,128)(2,1)} async-done(((bf16[960,2560]{1,0:T(8,128)(2,1)}), bf16[240,2560]{1,0:T(8,128)(2,1)}) %reduce-scatter.14.cloned.1.call-update) | async-done | bytes 1228816 | tf_op jit(solution)/shard_map/reduce_scatter | solution.py:379
  1139.0 47.7 %reduce-scatter.18.cloned.1.call-done = bf16[240,1600]{1,0:T(8,128)(2,1)} async-done(((bf16[960,1600]{1,0:T(8,128)(2,1)}), bf16[240,1600]{1,0:T(8,128)(2,1)}) %reduce-scatter.18.cloned.1.call-update) | async-done | bytes 768016
  1193.9 7.3 all-reduce.5
  1201.3 10.4 all-reduce.7
  1213.2 158.9 %all-reduce.11.cloned.1.call-done = (bf16[1,240,1600]{2,1,0:T(8,128)(2,1)}, bf16[1,240,960]{2,1,0:T(8,128)(2,1)}, bf16[1,240,2560]{2,1,0:T(8,128)(2,1)}, bf16[1,...) async-done(((bf16[1,240,1600]{2,1,0:T(8,128)(2,1)}, bf16[1,240,960]{2,1,0:T(8,128)(2,1)}, bf16[1,240,2560]{2,1,0:T(8,128)(2,1)}, bf16[1,240,2560]{2,1,0:T(8,128)(2,1)}, ...) | async-done | bytes 4915216 | tf_op jit(solution)/shard_map/psum | solution.py:381
  (751 shorter events, 303.6 us)
Async XLA Ops:
  7.2 49.2 %all-gather.9.cloned.1.call-start = ((), (), s32[]{:S(2)}) async-start(), calls=%async_computation.8 | async-start | bytes 3993600 | tf_op jit(solution)/shard_map/all_gather | solution.py:92
  7.9 122.5 %all-gather.11.cloned.1.call-start = ((), (), s32[]{:S(2)}) async-start(), calls=%async_computation.9 | async-start | bytes 2785280 | tf_op jit(solution)/shard_map/all_gather | solution.py:197
  23.1 39.0 %copy-start.155 = (f32[128]{0:T(128)}, f32[128]{0:T(128)S(1)}, u32[]{:S(2)}) copy-start(f32[128]{0:T(128)S(1)} %get-tuple-element.1132) | copy-start | bytes 1540
  60.8 112.6 %all-gather.13.cloned.1.call-start = ((), (), s32[]{:S(2)}) async-start(), calls=%async_computation.10 | async-start | bytes 2457600 | tf_op jit(solution)/shard_map/all_gather | solution.py:93
  61.5 164.1 %all-gather.15.cloned.1.call-start = ((), (), s32[]{:S(2)}) async-start(), calls=%async_computation.11 | async-start | bytes 6144000 | tf_op jit(solution)/shard_map/all_gather | solution.py:95
  62.1 223.9 %all-gather.17.cloned.1.call-start = ((), (), s32[]{:S(2)}) async-start(), calls=%async_computation.12 | async-start | bytes 6144000 | tf_op jit(solution)/shard_map/all_gather | solution.py:96
  62.7 283.7 %all-gather.19.cloned.1.call-start = ((), (), s32[]{:S(2)}) async-start(), calls=%async_computation.13 | async-start | bytes 6144000 | tf_op jit(solution)/shard_map/all_gather | solution.py:97
  63.3 366.7 %all-gather.21.cloned.1.call-start = ((), (), s32[]{:S(2)}) async-start(), calls=%async_computation.14 | async-start | bytes 2785280 | tf_op jit(solution)/shard_map/all_gather | solution.py:197
  159.2 14.2 %copy-start.54 = (bf16[2,128,960]{1,2,0:T(8,128)(2,1)S(1)}, bf16[2,128,960]{1,2,0:T(8,128)(2,1)}, u32[]{:S(2)}) copy-start(bf16[2,128,960]{1,2,0:T(8,128)(2,1)} %param.28) | copy-start | bytes 1474564
  171.2 58.6 %copy-start.9 = (bf16[2,1024,2,5,64]{1,4,3,2,0:T(8,128)(2,1)}, bf16[2,1024,2,5,64]{1,4,3,2,0:T(8,128)(2,1)S(1)}, u32[]{:S(2)}) copy-start(bf16[2,1024,2,5,64]{1,4,3,2,0:T(8,128)(2,1)S(1)} %get-tuple-element.1940) | copy-start | bytes 7864324
  171.3 58.6 %copy-start.19 = (bf16[128,5,3,64]{0,3,2,1:T(8,128)(2,1)}, bf16[128,5,3,64]{0,3,2,1:T(8,128)(2,1)S(1)}, u32[]{:S(2)}) copy-start(bf16[128,5,3,64]{0,3,2,1:T(8,128)(2,1)S(1)} %get-tuple-element.1949) | copy-start | bytes 737284
  176.8 53.1 %copy-start.151 = (f32[128]{0:T(128)}, f32[128]{0:T(128)S(1)}, u32[]{:S(2)}) copy-start(f32[128]{0:T(128)S(1)} %get-tuple-element.1134) | copy-start | bytes 1540
  177.2 108.8 %copy-start.37 = (bf16[128,960]{0,1:T(8,128)(2,1)}, bf16[128,960]{0,1:T(8,128)(2,1)S(1)}, u32[]{:S(2)}) copy-start(bf16[128,960]{0,1:T(8,128)(2,1)S(1)} %multiply_convert_fusion.11) | copy-start | bytes 737284
  347.3 10.3 copy-start.23
  352.3 3.5 collective-permute-start
  357.0 114.6 %copy-start.51 = (bf16[128,960]{0,1:T(8,128)(2,1)}, bf16[128,960]{0,1:T(8,128)(2,1)S(1)}, u32[]{:S(2)}) copy-start(bf16[128,960]{0,1:T(8,128)(2,1)S(1)} %get-tuple-element.1086) | copy-start | bytes 737284
  360.9 199.3 %all-gather.23.cloned.1.call-start = ((), (), s32[]{:S(2)}) async-start(), calls=%async_computation.15 | async-start | bytes 2785280 | tf_op jit(solution)/shard_map/all_gather | solution.py:197
  470.2 8.2 copy-start.11
  470.2 8.2 copy-start.21
  470.2 8.2 copy-start.139
  474.1 9.2 copy-start.29
  474.9 8.4 slice-start.10
  485.6 3.5 collective-permute-start.1
  606.1 12.9 copy-start.33
  606.4 9.0 slice-start
  606.4 10.5 slice-start.6
  668.3 54.5 %all-to-all-start = ((bf16[16,128,640]{1,2,0:T(8,128)(2,1)}), bf16[16,128,640]{1,2,0:T(8,128)(2,1)S(1)}, u32[]{:S(2)}, u32[]{:S(2)}) async-start(bf16[16,128,640]{1,2,0:T(8,128)(2,1)} %copy.88), calls=%async_computation | async-start | bytes 5242880 | tf_op jit(solution)/shard_map/all_to_all | solution.py:25
  672.5 50.8 %copy-start.49 = (bf16[128,960]{0,1:T(8,128)(2,1)S(1)}, bf16[128,960]{0,1:T(8,128)(2,1)}, u32[]{:S(2)}) copy-start(bf16[128,960]{0,1:T(8,128)(2,1)} %copy-done.48) | copy-start | bytes 737284
  672.5 50.8 %copy-start.146 = (f32[128]{0:T(128)S(1)}, f32[128]{0:T(128)}, u32[]{:S(2)}) copy-start(f32[128]{0:T(128)} %copy-done.145) | copy-start | bytes 1540
  672.6 54.5 %copy-start.110 = (bf16[128,15,64]{0,2,1:T(8,128)(2,1)}, bf16[128,15,64]{0,2,1:T(8,128)(2,1)S(1)}, u32[]{:S(2)}) copy-start(bf16[128,15,64]{0,2,1:T(8,128)(2,1)S(1)} %pad_maximum_fusion.9) | copy-start | bytes 737284
  723.3 11.7 copy-start.62
  723.3 16.0 %slice-start.2 = ((s8[4915200]{0:T(1024)(128)(4,1)}), s8[720896]{0:T(1024)(128)(4,1)S(1)}, s32[]{:S(2)}) async-start(s8[4915200]{0:T(1024)(128)(4,1)} %bitcast.889), calls=%async_computation.24 | async-start | bytes 1441792
  728.2 12.6 copy-start.66
  728.2 5.9 collective-permute-start.2
  735.0 10.5 copy-start.92
  779.0 9.8 copy-start.27
  794.8 12.5 copy-start.76
  794.8 12.5 copy-start.90
  794.8 62.8 %all-to-all-start.1 = ((bf16[16,128,640]{1,2,0:T(8,128)(2,1)}), bf16[16,128,640]{1,2,0:T(8,128)(2,1)}, u32[]{:S(2)}, u32[]{:S(2)}) async-start(bf16[16,128,640]{1,2,0:T(8,128)(2,1)} %copy.92), calls=%async_computation.1 | async-start | bytes 5242880 | tf_op jit(solution)/shard_map/all_to_all | solution.py:25
  807.2 228.0 %reduce-scatter.16.cloned.1.call-start = ((), (), s32[]{:S(2)}) async-start(), calls=%async_computation.19 | async-start | bytes 6553600
  812.4 47.5 %copy-start.25 = (bf16[1,960,1600]{2,1,0:T(8,128)(2,1)S(1)}, bf16[1,960,1600]{2,1,0:T(8,128)(2,1)}, u32[]{:S(2)}) copy-start(bf16[1,960,1600]{2,1,0:T(8,128)(2,1)} %all-gather.9.cloned.1.call-done) | copy-start | bytes 9216004
  812.4 47.5 %copy-start.52 = (bf16[128,960]{0,1:T(8,128)(2,1)S(1)}, bf16[128,960]{0,1:T(8,128)(2,1)}, u32[]{:S(2)}) copy-start(bf16[128,960]{0,1:T(8,128)(2,1)} %copy-done.51) | copy-start | bytes 737284
  812.4 47.5 %copy-start.149 = (f32[128]{0:T(128)S(1)}, f32[128]{0:T(128)}, u32[]{:S(2)}) copy-start(f32[128]{0:T(128)} %copy-done.148) | copy-start | bytes 1540
  859.8 9.9 slice-start.12
  859.9 7.7 copy-start.59
  859.9 7.7 copy-start.93
  859.9 9.8 slice-start.13
  862.8 6.1 collective-permute-start.3
  882.3 155.4 %reduce-scatter.10.cloned.1.call-start = ((), (), s32[]{:S(2)}) async-start(), calls=%async_computation.16 | async-start | bytes 2457600 | tf_op jit(solution)/shard_map/reduce_scatter | solution.py:379
  883.4 7.8 slice-start.8
  896.7 180.6 %reduce-scatter.12.cloned.1.call-start = ((), (), s32[]{:S(2)}) async-start(), calls=%async_computation.17 | async-start | bytes 6144000 | tf_op jit(solution)/shard_map/reduce_scatter | solution.py:379
  903.5 235.5 %reduce-scatter.14.cloned.1.call-start = ((), (), s32[]{:S(2)}) async-start(), calls=%async_computation.18 | async-start | bytes 6144000 | tf_op jit(solution)/shard_map/reduce_scatter | solution.py:379
  962.1 13.7 copy-start.50
  962.1 13.7 copy-start.128
  962.1 13.7 copy-start.147
  962.2 64.4 %all-to-all-start.2 = ((bf16[16,128,640]{1,2,0:T(8,128)(2,1)}), bf16[16,128,640]{1,2,0:T(8,128)(2,1)S(1)}, u32[]{:S(2)}, u32[]{:S(2)}) async-start(bf16[16,128,640]{1,2,0:T(8,128)(2,1)} %copy.96), calls=%async_computation.2 | async-start | bytes 5242880 | tf_op jit(solution)/shard_map/all_to_all | solution.py:25
  975.7 210.9 %reduce-scatter.18.cloned.1.call-start = ((), (), s32[]{:S(2)}) async-start(), calls=%async_computation.20 | async-start | bytes 3993600
  984.5 42.5 %copy-start.156 = (f32[128]{0:T(128)S(1)}, f32[128]{0:T(128)}, u32[]{:S(2)}) copy-start(f32[128]{0:T(128)} %copy-done.155) | copy-start | bytes 1540
  1035.1 337.0 %all-reduce.11.cloned.1.call-start = ((), (), s32[]{:S(2)}) async-start(), calls=%async_computation.21 | async-start | bytes 9953280 | tf_op jit(solution)/shard_map/psum | solution.py:381
  1037.8 150.6 %copy-start.34 = (f32[128,960]{0,1:T(8,128)S(1)}, f32[128,960]{0,1:T(8,128)}, u32[]{:S(2)}) copy-start(f32[128,960]{0,1:T(8,128)} %copy-done.33) | copy-start | bytes 1474564
  1037.8 150.6 %copy-start.91 = (bf16[128,2560]{1,0:T(8,128)(2,1)S(1)}, bf16[128,2560]{1,0:T(8,128)(2,1)}, u32[]{:S(2)}) copy-start(bf16[128,2560]{1,0:T(8,128)(2,1)} %get-tuple-element.1101) | copy-start | bytes 1966084
  1192.6 20.3 %copy-start.47 = (f32[128,960]{0,1:T(8,128)S(1)}, f32[128,960]{0,1:T(8,128)}, u32[]{:S(2)}) copy-start(f32[128,960]{0,1:T(8,128)} %copy-done.45) | copy-start | bytes 1474564
  1192.7 20.3 %copy-start.159 = (f32[128]{0:T(128)S(1)}, f32[128]{0:T(128)}, u32[]{:S(2)}) copy-start(f32[128]{0:T(128)} %get-tuple-element.1131) | copy-start | bytes 1540
  1213.2 165.3 %copy-start.123 = (bf16[1,2,128,960]{2,3,1,0:T(8,128)(2,1)}, bf16[1,2,128,960]{2,3,1,0:T(8,128)(2,1)S(1)}, u32[]{:S(2)}) copy-start(bf16[1,2,128,960]{2,3,1,0:T(8,128)(2,1)S(1)} %fusion.285) | copy-start | bytes 1474564
  (163 other events, 510.4 us)
Sparse Core Ops, SparseCore 0:
  9.9 46.4 all-gather.8
  60.9 69.4 all-gather.10
  132.3 32.8 all-gather.12
  166.8 58.6 all-gather.14
  227.3 58.6 all-gather.16
  287.7 58.6 all-gather.18
  361.0 68.9 all-gather.20
  492.4 67.6 all-gather.22
  882.4 68.0 reduce-scatter.15
  954.0 45.4 reduce-scatter.9
  1002.6 74.7 reduce-scatter.11
  1080.2 58.7 reduce-scatter.13
  1142.0 44.6 reduce-scatter.17
  1190.1 181.9 all-reduce.10
where the time goes:
time: 1390 us
  waiting for transfers between devices  839 us (60%)
  matrix products  271 us (19%)
  local copies, waits for them, and re-layouts  115 us (8%)
  other arithmetic  73.1 us (5%)
  starting transfers between devices  44.4 us (3%)
  blocking collectives  26.4 us (2%)
  between operations  17.8 us (1%)
    all_gather x3, waiting for transfers between devices, per_device(): lax.all_gather(forward_kv_local, ('ctx', 'wa'), axis=0, tiled=True)  196 us
    psum x1, waiting for transfers between devices, per_device(): lax.psum(as_sent(shares), 'ctx')  159 us
    all_to_all x3, waiting for transfers between devices, summed_on_arrival(): lax.all_to_all(split_up(shard, dim, devices), axis, 0, 0, tiled=True)  136 us
    reduce_scatter x3, waiting for transfers between devices, per_device(): lax.psum_scatter(as_sent(grad_sums), 'wa', scatter_dimension=0, tiled=True)  101 us
    all_gather x1, waiting for transfers between devices, per_device(): lax.all_gather(w_up, 'wa', axis=1, tiled=True)  56.1 us
    all_gather x1, waiting for transfers between devices, per_device(): lax.all_gather(w_down, 'wa', axis=1, tiled=True)  55.4 us
    unnamed x16, waiting for transfers between devices  50.8 us
    all_gather x1, waiting for transfers between devices, per_device(): lax.all_gather(w_gate, 'wa', axis=1, tiled=True)  48.3 us
  transfers between devices with their start and end apart: 21, of which 17 were waited for; matrix products, arithmetic and copies ran while one was open for 13% of the time, Pallas kernels for 0%

commit v1 on v0

v1 whole, which is shorter than its diff:
```python
import functools

import jax
import jax.numpy as jnp
from jax import lax
from jax.experimental import pallas as pl
from jax.experimental.pallas import tpu as pltpu
from jax.sharding import PartitionSpec as P

H = 15
KVH = 5
HD = 64
GROUP = H // KVH
QW = H * HD
KW = KVH * HD
LANES = 128
KEY_CHUNK = 512

EPSILON = 1e-05
ROPE_BASE = 100000.0
MASKED = -1e30
SCALE = HD**-0.5
F32 = jnp.float32
BF16 = jnp.bfloat16

WHOLE = pl.BlockSpec(memory_space=pltpu.VMEM)
SCALARS = pl.BlockSpec(memory_space=pltpu.SMEM)


def params(mib):
    return pltpu.CompilerParams(vmem_limit_bytes=mib * 1024 * 1024)


def cost(flops, moved, special=0):
    return pl.CostEstimate(flops=flops, bytes_accessed=moved, transcendentals=special)


def dot_nn(a, b):
    return lax.dot_general(a, b, (((1,), (0,)), ((), ())), preferred_element_type=F32)


def dot_nt(a, b):
    return lax.dot_general(a, b, (((1,), (1,)), ((), ())), preferred_element_type=F32)


def dot_tn(a, b):
    return lax.dot_general(a, b, (((0,), (0,)), ((), ())), preferred_element_type=F32)


def lane_of(shape):
    return lax.broadcasted_iota(jnp.int32, shape, 1)


def swap_halves(block, lane):
    ahead = pltpu.roll(block, LANES - HD // 2, 1)
    behind = pltpu.roll(block, HD // 2, 1)
    return jnp.where(lane % HD < HD // 2, ahead, behind)


def assemble_kernel(index_ref, *refs, shard_rows, step):
    out_ref = refs[-1]
    mine, other = refs[:-2], refs[-2]
    wa, section = index_ref[0], index_ref[1]
    rows = mine[0].shape[0]
    for k, piece in enumerate(mine):
        base = (wa ^ k) * shard_rows
        start = pl.multiple_of(base + section * step, 16)
        out_ref[pl.ds(start, rows), :] = piece[...]
        start = pl.multiple_of(base + (1 - section) * step, 16)
        out_ref[pl.ds(start, rows), :] = other[k]


def assemble(index, mine, other, shard_rows, step):
    width = mine[0].shape[1]
    total = shard_rows * len(mine)
    return pl.pallas_call(
        functools.partial(assemble_kernel, shard_rows=shard_rows, step=step),
        out_shape=jax.ShapeDtypeStruct((total, width), BF16),
        in_specs=[SCALARS] + [WHOLE] * (len(mine) + 1),
        out_specs=WHOLE,
        compiler_params=params(24),
        cost_estimate=cost(0, total * width * 6),
        name="assemble",
    )(index, *mine, other)


def pair_kernel(index_ref, *refs, shard_rows):
    out_ref = refs[-1]
    mine, other = refs[:-2], refs[-2]
    wa, section = index_ref[0], index_ref[1]
    rows, width = mine[0].shape
    left = pl.multiple_of(section * width, LANES)
    right = pl.multiple_of((1 - section) * width, LANES)
    for k, piece in enumerate(mine):
        start = pl.multiple_of((wa ^ k) * shard_rows, 16)
        out_ref[pl.ds(start, rows), pl.ds(left, width)] = piece[...]
        out_ref[pl.ds(start, rows), pl.ds(right, width)] = other[k]


def assemble_pair(index, mine, other):
    shard_rows, width = mine[0].shape
    total = shard_rows * len(mine)
    return pl.pallas_call(
        functools.partial(pair_kernel, shard_rows=shard_rows),
        out_shape=jax.ShapeDtypeStruct((total, 2 * width), BF16),
        in_specs=[SCALARS] + [WHOLE] * (len(mine) + 1),
        out_specs=WHOLE,
        compiler_params=params(24),
        cost_estimate=cost(0, total * width * 8),
        name="assemble_pair",
    )(index, *mine, other)


def project_kernel(u_ref, gain_ref, w_ref, cos_ref, sin_ref, normed_ref, q_ref, kv_ref, mixed_ref):
    u = u_ref[...].astype(F32)
    scale = lax.rsqrt(jnp.mean(u * u, axis=-1, keepdims=True) + EPSILON)
    normed = (u * scale * gain_ref[...].astype(F32)).astype(BF16)
    normed_ref[...] = normed
    mixed_ref[:, : w_ref.shape[1]] = dot_nn(normed, w_ref[...])
    cosine, sine = cos_ref[...], sin_ref[...]
    lane = lane_of(cosine.shape)
    low = lane < HD
    roped = {}

    def unit(h, high):
        j = h // 2
        if j not in roped:
            block = mixed_ref[:, j * LANES : (j + 1) * LANES]
            if h < H + KVH:
                block = block * cosine + swap_halves(block, lane) * sine
            roped[j] = block
        return roped[j] if (h % 2 == 1) == high else pltpu.roll(roped[j], HD, 1)

    for h in range(H):
        padded = jnp.where(low, unit(h, False) * SCALE, 0.0)
        q_ref[:, h * LANES : (h + 1) * LANES] = padded.astype(BF16)
    for g in range(KVH):
        both = jnp.where(low, unit(H + g, False), unit(H + KVH + g, True))
        kv_ref[:, g * LANES : (g + 1) * LANES] = both.astype(BF16)


def project(u, gain, weight, cosine, sine):
    rows, width = u.shape
    columns = weight.shape[1]
    padded = -(-columns // LANES) * LANES
    return pl.pallas_call(
        project_kernel,
        out_shape=(
            jax.ShapeDtypeStruct((rows, width), BF16),
            jax.ShapeDtypeStruct((rows, H * LANES), BF16),
            jax.ShapeDtypeStruct((rows, KVH * LANES), BF16),
        ),
        in_specs=[WHOLE] * 5,
        out_specs=(WHOLE,) * 3,
        scratch_shapes=[pltpu.VMEM((rows, padded), F32)],
        compiler_params=params(24),
        cost_estimate=cost(2 * rows * width * columns, width * columns * 2),
        name="project",
    )(u, gain, weight, cosine, sine)


def stack_heads(ref):
    return jnp.concatenate(
        [ref[:, i * LANES : (i + 1) * LANES] for i in range(GROUP)], axis=0
    )


def attend_kernel(qpos_ref, kpos_ref, q_ref, *refs):
    kv_refs, out_ref = refs[:-1], refs[-1]
    queries = stack_heads(q_ref)
    qpos = jnp.concatenate([qpos_ref[...]] * GROUP, axis=0)
    rows = queries.shape[0]
    top = jnp.full((rows, 1), MASKED, F32)
    total = jnp.zeros((rows, 1), F32)
    acc = jnp.zeros((rows, LANES), F32)
    for k, kv_ref in enumerate(kv_refs):
        for start in range(0, kv_ref.shape[0], KEY_CHUNK):
            size = min(KEY_CHUNK, kv_ref.shape[0] - start)
            kv = kv_ref[start : start + size, :]
            kpos = kpos_ref[k : k + 1, start : start + size]
            scores = jnp.where(kpos <= qpos, dot_nt(queries, kv), MASKED)
            new_top = jnp.maximum(top, jnp.max(scores, axis=-1, keepdims=True))
            fresh = jnp.exp(scores - new_top)
            decay = jnp.exp(top - new_top)
            total = total * decay + jnp.sum(fresh, axis=-1, keepdims=True)
            acc = acc * decay + dot_nn(fresh.astype(BF16), kv)
            top = new_top
    lse = top + jnp.log(total)
    out_ref[...] = jnp.where(lane_of(acc.shape) < HD, lse, acc / total)


def attend(qpos, kpos, queries, groups):
    rows = queries.shape[0]
    keys = groups[0].shape[0]
    pairs = H * rows * keys * len(groups)
    return pl.pallas_call(
        attend_kernel,
        out_shape=jax.ShapeDtypeStruct((H * rows, LANES), F32),
        grid=(KVH,),
        in_specs=[
            pl.BlockSpec((rows, 1), lambda g: (0, 0)),
            pl.BlockSpec(kpos.shape, lambda g: (0, 0)),
            pl.BlockSpec((rows, GROUP * LANES), lambda g: (0, g)),
        ]
        + [pl.BlockSpec((keys, LANES), lambda g: (0, g)) for _ in groups],
        out_specs=pl.BlockSpec((GROUP * rows, LANES), lambda g: (g, 0)),
        compiler_params=params(40),
        cost_estimate=cost(pairs * 512, keys * len(groups) * KVH * 256, pairs),
        name="attend",
    )(qpos, kpos, queries, *groups)


def attend_back_kernel(qpos_ref, kpos_ref, q_ref, g_ref, o_ref, *refs):
    count = (len(refs) - 1) // 2
    kv_refs, dq_ref, dkv_refs = refs[:count], refs[count], refs[count + 1 :]
    queries = stack_heads(q_ref)
    grads = stack_heads(g_ref)
    saved = o_ref[...]
    lse = jnp.transpose(saved)[0:1, :]
    delta = jnp.sum(jnp.transpose(grads.astype(F32) * saved), axis=0, keepdims=True)
    qpos = jnp.concatenate([qpos_ref[...]] * GROUP, axis=1)
    rows = queries.shape[0]
    acc = jnp.zeros((rows, LANES), F32)
    for k, kv_ref in enumerate(kv_refs):
        for start in range(0, kv_ref.shape[0], KEY_CHUNK):
            size = min(KEY_CHUNK, kv_ref.shape[0] - start)
            kv = kv_ref[start : start + size, :]
            kpos = kpos_ref[start : start + size, k : k + 1]
            scores = jnp.where(kpos <= qpos, dot_nt(kv, queries), MASKED)
            probs = jnp.exp(scores - lse)
            grad_probs = dot_nt(kv, grads)
            grad_scores = (probs * (grad_probs - delta)).astype(BF16)
            acc = acc + dot_tn(grad_scores, kv)
            dkv = dot_nn(grad_scores, queries) + dot_nn(probs.astype(BF16), grads)
            dkv_refs[k][start : start + size, :] = dkv.astype(BF16)
    tok = q_ref.shape[0]
    for i in range(GROUP):
        dq_ref[:, i * LANES : (i + 1) * LANES] = acc[i * tok : (i + 1) * tok] * SCALE


def attend_back(qpos_row, kpos_column, queries, grads, saved, groups):
    rows = queries.shape[0]
    keys = groups[0].shape[0]
    pairs = H * rows * keys * len(groups)
    heads = pl.BlockSpec((rows, GROUP * LANES), lambda g: (0, g))
    kv_block = pl.BlockSpec((keys, LANES), lambda g: (0, g))
    result = pl.pallas_call(
        attend_back_kernel,
        out_shape=(jax.ShapeDtypeStruct((rows, H * LANES), F32),)
        + tuple(jax.ShapeDtypeStruct(group.shape, BF16) for group in groups),
        grid=(KVH,),
        in_specs=[
            pl.BlockSpec((1, rows), lambda g: (0, 0)),
            pl.BlockSpec(kpos_column.shape, lambda g: (0, 0)),
            heads,
            heads,
            pl.BlockSpec((GROUP * rows, LANES), lambda g: (g, 0)),
        ]
        + [kv_block for _ in groups],
        out_specs=(heads,) + tuple(kv_block for _ in groups),
        compiler_params=params(40),
        cost_estimate=cost(pairs * 1280, keys * len(groups) * KVH * 512, pairs),
        name="attend_back",
    )(qpos_row, kpos_column, queries, grads, saved, *groups)
    return result[0], result[1:]


def close_kernel(u_ref, saved_ref, w_ref, gain_ref, low_ref, middle_ref, second_ref):
    rows = u_ref.shape[0]
    lane = lane_of((rows, LANES))
    for j in range(H // 2):
        even = pltpu.roll(saved_ref[2 * j * rows : (2 * j + 1) * rows, :], HD, 1)
        odd = saved_ref[(2 * j + 1) * rows : (2 * j + 2) * rows, :]
        low_ref[:, j * LANES : (j + 1) * LANES] = jnp.where(lane < HD, even, odd).astype(BF16)
    last = pltpu.roll(saved_ref[(H - 1) * rows : H * rows, :], HD, 1)
    low_ref[:, (H - 1) * HD : H * HD] = last[:, :HD].astype(BF16)
    middle = u_ref[...].astype(F32) + dot_nn(low_ref[...], w_ref[...])
    middle_ref[...] = middle
    scale = lax.rsqrt(jnp.mean(middle * middle, axis=-1, keepdims=True) + EPSILON)
    second_ref[...] = (middle * scale * gain_ref[...].astype(F32)).astype(BF16)


def close_attention(u, saved, weight, gain):
    rows, width = u.shape
    return pl.pallas_call(
        close_kernel,
        out_shape=(
            jax.ShapeDtypeStruct((rows, QW), BF16),
            jax.ShapeDtypeStruct((rows, width), F32),
            jax.ShapeDtypeStruct((rows, width), BF16),
        ),
        in_specs=[WHOLE] * 4,
        out_specs=(WHOLE,) * 3,
        compiler_params=params(24),
        cost_estimate=cost(2 * rows * QW * width, QW * width * 2),
        name="close_attention",
    )(u, saved, weight, gain)


def mlp_kernel(*refs, count):
    pieces, w_ref, down_ref = refs[:count], refs[count], refs[count + 1]
    wide_ref, hidden_ref = refs[count + 2 : count + 4]
    outs = refs[count + 4 :]
    rows = pieces[0].shape[0]
    second = jnp.concatenate([piece[...] for piece in pieces], axis=0)
    wide = dot_nn(second, w_ref[...])
    wide_ref[...] = wide
    half = wide.shape[1] // 2
    gate, up = wide[:, :half], wide[:, half:]
    hidden = (gate * jax.nn.sigmoid(gate) * up).astype(BF16)
    hidden_ref[...] = hidden
    partial = dot_nn(hidden, down_ref[...])
    for k, out in enumerate(outs):
        out[...] = partial[k * rows : (k + 1) * rows].astype(out.dtype)


def mlp(pieces, weight, down):
    count = len(pieces)
    rows, width = pieces[0].shape
    columns = weight.shape[1]
    result = pl.pallas_call(
        functools.partial(mlp_kernel, count=count),
        out_shape=(
            jax.ShapeDtypeStruct((count * rows, columns), F32),
            jax.ShapeDtypeStruct((count * rows, columns // 2), BF16),
            jax.ShapeDtypeStruct((rows, width), F32),
        )
        + tuple(jax.ShapeDtypeStruct((rows, width), BF16) for _ in range(count - 1)),
        in_specs=[WHOLE] * (count + 2),
        out_specs=(WHOLE,) * (count + 2),
        compiler_params=params(40),
        cost_estimate=cost(3 * count * rows * width * columns, width * columns * 8),
        name="mlp",
    )(*pieces, weight, down)
    return result[0], result[1], result[2:]


def mlp_back_kernel(*refs, count):
    pieces, wide_ref, w_ref, down_ref = refs[:count], *refs[count : count + 3]
    grads_ref, outs = refs[count + 3], refs[count + 4 :]
    rows = pieces[0].shape[0]
    grad_y = jnp.concatenate([piece[...] for piece in pieces], axis=0)
    grad_hidden = dot_nt(grad_y, down_ref[...])
    half = wide_ref.shape[1] // 2
    gate, up = wide_ref[:, :half], wide_ref[:, half:]
    sig = jax.nn.sigmoid(gate)
    grads_ref[:, :half] = (grad_hidden * up * sig * (1.0 + gate * (1.0 - sig))).astype(BF16)
    grads_ref[:, half:] = (grad_hidden * gate * sig).astype(BF16)
    partial = dot_nt(grads_ref[...], w_ref[...])
    for k, out in enumerate(outs):
        out[...] = partial[k * rows : (k + 1) * rows].astype(out.dtype)


def mlp_back(pieces, wide, weight, down):
    count = len(pieces)
    rows, width = pieces[0].shape
    columns = weight.shape[1]
    result = pl.pallas_call(
        functools.partial(mlp_back_kernel, count=count),
        out_shape=(
            jax.ShapeDtypeStruct((count * rows, columns), BF16),
            jax.ShapeDtypeStruct((rows, width), F32),
        )
        + tuple(jax.ShapeDtypeStruct((rows, width), BF16) for _ in range(count - 1)),
        in_specs=[WHOLE] * (count + 3),
        out_specs=(WHOLE,) * (count + 1),
        compiler_params=params(40),
        cost_estimate=cost(3 * count * rows * width * columns, width * columns * 8),
        name="mlp_back",
    )(*pieces, wide, weight, down)
    return result[0], result[1:]


def norm_back(values, gain, gradient):
    scaling = lax.rsqrt(jnp.mean(values * values, axis=-1, keepdims=True) + EPSILON)
    gain_grad = jnp.sum(gradient * values * scaling, axis=0, keepdims=True)
    scaled = gradient * gain.astype(F32)
    inner = jnp.mean(scaled * values, axis=-1, keepdims=True)
    return gain_grad, scaling * scaled - values * (scaling * scaling * scaling) * inner


def open_back_kernel(*refs, count):
    terms = refs[:count]
    middle_ref, gain_ref, y_ref, w_ref = refs[count : count + 4]
    grad_ref, low_ref, padded_ref, gain_grad_ref, wide_ref = refs[count + 4 :]
    gradient = terms[0][...]
    for term in terms[1:]:
        gradient = gradient + term[...].astype(F32)
    gain_grad, through = norm_back(middle_ref[...], gain_ref[...], gradient)
    gain_grad_ref[...] = gain_grad
    grad_middle = y_ref[...].astype(F32) + through
    grad_ref[...] = grad_middle
    low = grad_middle.astype(BF16)
    low_ref[...] = low
    wide_ref[:, :QW] = dot_nt(low, w_ref[...])
    lane = lane_of((low.shape[0], LANES))
    for h in range(H):
        block = wide_ref[:, h // 2 * LANES : (h // 2 + 1) * LANES]
        placed = block if h % 2 else pltpu.roll(block, HD, 1)
        padded_ref[:, h * LANES : (h + 1) * LANES] = jnp.where(lane < HD, 0.0, placed).astype(BF16)


def open_back(terms, middle, gain, grad_y, weight):
    rows, width = middle.shape
    count = len(terms)
    return pl.pallas_call(
        functools.partial(open_back_kernel, count=count),
        out_shape=(
            jax.ShapeDtypeStruct((rows, width), F32),
            jax.ShapeDtypeStruct((rows, width), BF16),
            jax.ShapeDtypeStruct((rows, H * LANES), BF16),
            jax.ShapeDtypeStruct((1, width), F32),
        ),
        in_specs=[WHOLE] * (count + 4),
        out_specs=(WHOLE,) * 4,
        scratch_shapes=[pltpu.VMEM((rows, (H + 1) // 2 * LANES), F32)],
        compiler_params=params(24),
        cost_estimate=cost(2 * rows * QW * width, QW * width * 2),
        name="open_back",
    )(*terms, middle, gain, grad_y, weight)


def project_back_kernel(*refs, count):
    terms = refs[:count]
    dq_ref, cos_ref, sin_ref, w_ref, u_ref, gain_ref, middle_ref = refs[count : count + 7]
    mixed_ref, out_ref, gain_grad_ref, wide_ref = refs[count + 7 :]
    grad_kv = terms[0][...].astype(F32)
    for term in terms[1:]:
        grad_kv = grad_kv + term[...].astype(F32)
    cosine, sine = cos_ref[...], sin_ref[...]
    lane = lane_of(cosine.shape)
    low = lane < HD

    def turned(block):
        return block * cosine - swap_halves(block, lane) * sine

    def unit(h, high):
        if h < H:
            block, at_high = turned(dq_ref[:, h * LANES : (h + 1) * LANES]), False
        elif h < H + KVH:
            g = h - H
            block, at_high = turned(grad_kv[:, g * LANES : (g + 1) * LANES]), False
        else:
            g = h - H - KVH
            block, at_high = grad_kv[:, g * LANES : (g + 1) * LANES], True
        return block if at_high == high else pltpu.roll(block, HD, 1)

    units = H + 2 * KVH
    for j in range((units + 1) // 2):
        block = unit(2 * j, False)
        if 2 * j + 1 < units:
            block = jnp.where(low, block, unit(2 * j + 1, True))
        wide_ref[:, j * LANES : (j + 1) * LANES] = block.astype(BF16)
    grad_mixed = wide_ref[:, : w_ref.shape[1]]
    mixed_ref[...] = grad_mixed
    gradient = dot_nt(grad_mixed, w_ref[...])
    gain_grad, through = norm_back(u_ref[...].astype(F32), gain_ref[...], gradient)
    gain_grad_ref[...] = gain_grad
    out_ref[...] = (middle_ref[...] + through).astype(BF16)


def project_back(terms, dq, cosine, sine, weight, u, gain, grad_middle):
    rows, width = u.shape
    columns = weight.shape[1]
    padded = -(-columns // LANES) * LANES
    count = len(terms)
    return pl.pallas_call(
        functools.partial(project_back_kernel, count=count),
        out_shape=(
            jax.ShapeDtypeStruct((rows, columns), BF16),
            jax.ShapeDtypeStruct((rows, width), BF16),
            jax.ShapeDtypeStruct((1, width), F32),
        ),
        in_specs=[WHOLE] * (count + 7),
        out_specs=(WHOLE,) * 3,
        scratch_shapes=[pltpu.VMEM((rows, padded), BF16)],
        compiler_params=params(24),
        cost_estimate=cost(2 * rows * width * columns, width * columns * 2),
        name="project_back",
    )(*terms, dq, cosine, sine, weight, u, gain, grad_middle)


def to_sibling(value):
    return lax.ppermute(value, "section", [(0, 1), (1, 0)])


def to_peer(value, k):
    count = lax.axis_size("wa")
    return lax.ppermute(value, "wa", [(i, i ^ k) for i in range(count)])


def gather_wa(value):
    return [value] + [to_peer(value, k) for k in range(1, lax.axis_size("wa"))]


def send_wa(pieces):
    return [pieces[0]] + [to_peer(piece, k) for k, piece in enumerate(pieces) if k]


def rotates(count):
    return count <= 4


def gather_ctx(value):
    count = lax.axis_size("ctx")
    if not rotates(count):
        return lax.all_gather(value, "ctx", axis=0, tiled=True)
    pieces = [value]
    for k in range(1, count):
        pieces.append(lax.ppermute(value, "ctx", [(i, (i + k) % count) for i in range(count)]))
    return jnp.concatenate(pieces, axis=0)


def scatter_ctx(value):
    count = lax.axis_size("ctx")
    rows = value.shape[0] // count
    if not rotates(count):
        blocks = value.reshape(count, rows, value.shape[1])
        return list(lax.all_to_all(blocks, "ctx", 0, 0, tiled=True))
    pieces = [value[:rows]]
    for k in range(1, count):
        piece = value[k * rows : (k + 1) * rows]
        pieces.append(lax.ppermute(piece, "ctx", [(i, (i - k) % count) for i in range(count)]))
    return pieces


def at(value, index, size, dim):
    return lax.dynamic_slice_in_dim(value, index * size, size, dim)


def added(terms):
    total = terms[0].astype(F32)
    for term in terms[1:]:
        total = total + term.astype(F32)
    return total


def per_device(
    block_input, out_cotangent, block_table, attn_gain, w_qkv, w_out, mlp_gain, w_gate, w_up, w_down
):
    section = lax.axis_index("section")
    wa = lax.axis_index("wa")
    ctx = lax.axis_index("ctx")
    wa_count = lax.axis_size("wa")
    ctx_count = lax.axis_size("ctx")
    layers = lax.axis_size("section")
    first = section == 0
    peers = range(wa_count)
    index = jnp.stack([wa, section]).astype(jnp.int32)
    micro_count, tok_rows, width = block_input.shape
    half_rows = tok_rows // 2
    shard_rows = w_qkv.shape[1]
    ff_part = w_down.shape[1]
    w_qkv, w_out, w_gate, w_up, w_down = (a[0] for a in (w_qkv, w_out, w_gate, w_up, w_down))

    in_block = jnp.arange(half_rows, dtype=jnp.int32)
    table = block_table.reshape(-1, 2)

    def positions_of(devices):
        return (table[devices][..., None] * half_rows + in_block).reshape(-1)

    own_pos = positions_of((ctx * wa_count + wa)[None])
    steps = jnp.arange(ctx_count)
    sources = (ctx - steps) % ctx_count if rotates(ctx_count) else steps
    key_pos = jnp.stack([positions_of(sources * wa_count + (wa ^ k)) for k in peers])
    key_pos_column = key_pos.T
    qpos_column, qpos_row = own_pos[:, None], own_pos[None, :]
    inverse = ROPE_BASE ** (-(jnp.arange(HD // 2, dtype=F32) * 2.0) / HD)
    angles = own_pos.astype(F32)[:, None] * inverse[None, :]
    cosine = jnp.tile(jnp.cos(angles), (1, 2 * LANES // HD))
    sines = jnp.sin(angles)
    sine = jnp.tile(jnp.concatenate([-sines, sines], axis=1), (1, LANES // HD))

    part_rows = shard_rows // 2 + 8
    part_step = shard_rows - part_rows

    def halves(shard):
        keep = lax.dynamic_slice_in_dim(shard, section * part_step, part_rows, 0)
        other = to_sibling(lax.dynamic_slice_in_dim(shard, (1 - section) * part_step, part_rows, 0))
        return jnp.where(first, keep, other), jnp.where(first, other, keep)

    def fetch_rows(part):
        mine = gather_wa(part)
        return assemble(index, mine, to_sibling(jnp.stack(mine)), shard_rows, part_step)

    def fetch_columns(part):
        mine = send_wa([at(part, wa ^ k, ff_part, 1) for k in peers])
        return assemble_pair(index, mine, to_sibling(jnp.stack(mine)))

    qkv_parts = halves(w_qkv)
    out_parts = halves(w_out)
    crossing = to_sibling(jnp.where(first, w_up, w_gate))
    wide_parts = (jnp.where(first, w_gate, crossing), jnp.where(first, crossing, w_up))
    down_other = to_sibling(w_down)
    downs = (jnp.where(first, w_down, down_other), jnp.where(first, down_other, w_down))
    gains = jnp.concatenate([attn_gain, mlp_gain], axis=0)
    gains = lax.all_gather(gains, ("section", "wa"), axis=0, tiled=False)
    gains = gains.reshape(layers, wa_count, 2, -1).transpose(0, 2, 1, 3).reshape(layers, 2, 1, -1)

    qkvs, outs, wides = [], [], []
    for layer in range(layers):
        qkvs.append(fetch_rows(qkv_parts[layer]))
        outs.append(fetch_rows(out_parts[layer]))
        wides.append(fetch_columns(wide_parts[layer]))

    u = lax.dynamic_index_in_dim(block_input, section, 0, keepdims=False)
    cotangent = lax.dynamic_index_in_dim(out_cotangent, section, 0, keepdims=False)
    records, results = [], []
    for layer in range(layers):
        normed, queries, kv = project(u, gains[layer, 0], qkvs[layer], cosine, sine)
        groups = gather_wa(gather_ctx(kv))
        saved = attend(qpos_column, key_pos, queries, groups)
        low, middle, second = close_attention(u, saved, outs[layer], gains[layer, 1])
        seconds = gather_wa(second)
        wide, hidden, partial = mlp(seconds, wides[layer], downs[layer])
        terms = send_wa(partial)
        result = (middle + added(terms)).astype(BF16)
        records.append((u, normed, queries, groups, saved, low, middle, seconds, wide, hidden))
        results.append(result)
        u = result

    gain_grads, input_grads, weight_grads = [None] * layers, [None] * layers, [None] * layers
    grad_y = cotangent
    for layer in reversed(range(layers)):
        u, normed, queries, groups, saved, low, middle, seconds, wide, hidden = records[layer]
        grad_ys = gather_wa(grad_y)
        grad_wide, partial = mlp_back(grad_ys, wide, wides[layer], downs[layer])
        terms = send_wa(partial)
        grad_middle, grad_low, grad_heads, gain_two_grad = open_back(
            terms, middle, gains[layer, 1], grad_y, outs[layer]
        )
        dq, dkv = attend_back(qpos_row, key_pos_column, queries, grad_heads, saved, groups)
        gathered = added(send_wa(list(dkv))).astype(BF16)
        terms = scatter_ctx(gathered)
        grad_mixed, grad_u, gain_one_grad = project_back(
            terms, dq, cosine, sine, qkvs[layer], u, gains[layer, 0], grad_middle
        )
        gain_grads[layer] = (gain_one_grad, gain_two_grad)
        input_grads[layer] = grad_u

        all_seconds = jnp.concatenate(seconds, axis=0)
        all_grads = jnp.concatenate(grad_ys, axis=0)
        wide_grad = dot_tn(all_seconds, grad_wide).astype(BF16)
        down_grad = dot_tn(hidden, all_grads).astype(BF16)
        out_grad = dot_tn(low, grad_low).astype(BF16)
        qkv_grad = dot_tn(normed, grad_mixed).astype(BF16)

        def over_cores(value, size, dim):
            keep = at(value, section, size, dim)
            other = to_sibling(at(value, 1 - section, size, dim))
            return (keep.astype(F32) + other.astype(F32)).astype(BF16)

        wide_half = over_cores(wide_grad, ff_part, 1)
        pieces = send_wa([at(wide_half, wa ^ k, shard_rows, 0) for k in peers])
        wide_rows = jnp.zeros((shard_rows, wa_count * ff_part), BF16)
        for k in peers:
            wide_rows = lax.dynamic_update_slice_in_dim(
                wide_rows, pieces[k], (wa ^ k) * ff_part, 1
            )
        down_half = over_cores(down_grad, ff_part // 2, 0)

        def rows_over_wa(value):
            columns = value.shape[1]
            blocks = value.reshape(wa_count, 2, shard_rows // 2, columns)
            half = over_cores(blocks, 1, 1)[:, 0]
            pieces = send_wa([at(half, wa ^ k, 1, 0)[0] for k in peers])
            return added(pieces).astype(BF16)

        out_half = rows_over_wa(out_grad)
        qkv_half = rows_over_wa(qkv_grad)
        wide_rows, down_half = lax.psum((wide_rows, down_half), "ctx")
        out_half, qkv_half = lax.psum((out_half, qkv_half), "ctx")
        weight_grads[layer] = (wide_rows, down_half, out_half, qkv_half)
        grad_y = grad_u

    def by_layer(values):
        mine = jnp.where(first, values[0], values[1])
        other = to_sibling(jnp.where(first, values[1], values[0]))
        return jnp.where(first, mine, other), jnp.where(first, other, mine)

    def both(values):
        return jnp.stack(by_layer(values))[None]

    def joined(position):
        parts = by_layer([weight_grads[layer][position] for layer in range(layers)])
        return jnp.concatenate(parts, axis=0).astype(F32)[None]

    gate_grad, up_grad = by_layer([weight_grads[layer][0] for layer in range(layers)])
    gain_sums = lax.psum(
        jnp.concatenate([jnp.concatenate(pair, axis=0) for pair in gain_grads], axis=0),
        ("section", "ctx", "wa"),
    ).reshape(layers, 2, width)
    own_gains = at(lax.dynamic_index_in_dim(gain_sums, section, 0), wa, shard_rows, 2)
    return (
        both(results),
        both(input_grads),
        own_gains[:, 0],
        joined(3),
        joined(2),
        own_gains[:, 1],
        gate_grad.astype(F32)[None],
        up_grad.astype(F32)[None],
        joined(1),
    )


def solution(mesh):
    return jax.shard_map(
        per_device,
        mesh=mesh,
        in_specs=(
            P(None, ("ctx", "wa"), None),
            P(None, ("ctx", "wa"), None),
            P(),
            P("section", "wa"),
            P("section", "wa", None),
            P("section", "wa", None),
            P("section", "wa"),
            P("section", "wa", None),
            P("section", "wa", None),
            P("section", "wa", None),
        ),
        out_specs=(
            P("section", None, ("ctx", "wa"), None),
            P("section", None, ("ctx", "wa"), None),
            P("section", "wa"),
            P("section", "wa", None),
            P("section", "wa", None),
            P("section", "wa"),
            P("section", "wa", None),
            P("section", "wa", None),
            P("section", "wa", None),
        ),
        check_vma=False,
    )
```

time: 1390 us -> 838 us (0.60)
  waiting for transfers between devices: 839 us -> 310 us
  matrix products: 271 us -> 13.3 us
  starting transfers between devices: 44.4 us -> 136 us
  Pallas kernels: 0 us -> 89.3 us
  blocking collectives: 26.4 us -> 63.5 us
  local copies, waits for them, and re-layouts: 115 us -> 132 us
    all_gather x8 -> x0, waiting for transfers between devices: 388 us -> none  [the longest x3 196 us: per_device(): lax.all_gather(forward_kv_local, ('ctx', 'wa'), axis=0, tiled=True)]
    dot_general x87 -> x8, matrix products: 271 us -> 13.3 us  [dot_tn(): lax.dot_general(a, b, (((0,), (0,)), ((), ())), preferred_element_type=F32)]
    ppermute x4 -> x108, waiting for transfers between devices: 4.5 us -> 184 us  [the longest x72 147 us: to_peer(): return lax.ppermute(value, 'wa', [(i, i ^ k) for i in range(count)])]
    all_to_all x3 -> x0, waiting for transfers between devices: 136 us -> none  [summed_on_arrival(): lax.all_to_all(split_up(shard, dim, devices), axis, 0, 0, tiled=True)]
    ppermute x4 -> x108, starting transfers between devices: 13.1 us -> 136 us  [the longest x72 70.8 us: to_peer(): return lax.ppermute(value, 'wa', [(i, i ^ k) for i in range(count)])]
    reduce_scatter x3 -> x0, waiting for transfers between devices: 101 us -> none  [per_device(): lax.psum_scatter(as_sent(grad_sums), 'wa', scatter_dimension=0, tiled=True)]
    pallas_call x0 -> x22, Pallas kernels: none -> 89.3 us  [the longest x2 30.2 us: attend_back(): pl.pallas_call(attend_back_kernel, out_shape=(jax.ShapeDtypeStruct((rows,...]
    unnamed x16 -> x1, waiting for transfers between devices: 50.8 us -> 0.02 us
  transfers between devices with their start and end apart: 21 -> 109, of which waited for: 17 -> 36; matrix products, arithmetic and copies ran while one was open for 13% -> 20% of each run, Pallas kernels for 0% -> 10%
where the time goes in v1:
time: 838 us; the launch traced here: 831 us
  waiting for transfers between devices  310 us (37%)
  starting transfers between devices  136 us (16%)
  local copies, waits for them, and re-layouts  132 us (16%)
  Pallas kernels  89.3 us (11%)
  other arithmetic  71.3 us (9%)
  blocking collectives  63.5 us (8%)
  between operations  15.9 us (2%)
  matrix products  13.3 us (2%)
    ppermute x72, waiting for transfers between devices, to_peer(): return lax.ppermute(value, 'wa', [(i, i ^ k) for i in range(count)])  147 us
    psum x1, waiting for transfers between devices, per_device(): out_half, qkv_half = lax.psum((out_half, qkv_half), 'ctx')  125 us
    ppermute x72, starting transfers between devices, to_peer(): return lax.ppermute(value, 'wa', [(i, i ^ k) for i in range(count)])  70.8 us
    unnamed x327, local copies, waits for them, and re-layouts  54 us
    ppermute x24, starting transfers between devices, to_sibling(): return lax.ppermute(value, 'section', [(0, 1), (1, 0)])  50.7 us
    psum x1, blocking collectives, per_device(): lax.psum(jnp.concatenate([jnp.concatenate(pair, axis=0) for pair in gain_...  43.5 us
    pallas_call x2, Pallas kernels, attend_back(): pl.pallas_call(attend_back_kernel, out_shape=(jax.ShapeDtypeStruct((rows,...  30.2 us
    ppermute x6, waiting for transfers between devices, scatter_ctx(): lax.ppermute(piece, 'ctx', [(i, (i - k) % count) for i in range(count)])  20.9 us
  transfers between devices with their start and end apart: 109, of which 36 were waited for; matrix products, arithmetic and copies ran while one was open for 20% of the time, Pallas kernels for 10%

profile of v1, /device:TPU:1, one launch (start us, length us, event | category | flops | bytes accessed | tf_op | source)
XLA Modules:
  0.0 830.6 jit_solution(3262049707854940132)
XLA Ops:
  10.7 2.5 bitcast_select_fusion.3
  18.6 2.7 collective-permute-start.1
  23.2 8.3 collective-permute-done.1.refs_1_
  31.5 9.0 %collective-permute-done.2.refs_2_ = bf16[128,1600]{1,0:T(8,128)(2,1)S(1)} collective-permute-done((bf16[128,1600]{1,0:T(8,128)(2,1)S(1)}, bf16[128,1600]{1,0:T(8,128)(2,1)S(1)}, u32[]{:S(2)}, u32[]{:S(2)}) %collective-permute-start.2) | collective-permute-done | bytes 409632 | tf_op jit(solution)/shard_map/ppermute | solution.py:489
  43.1 3.6 copy.87
  52.6 20.0 %all-gather.1 = bf16[8,2,240]{2,1,0:T(2,128)(2,1)S(1)} all-gather(bf16[1,2,240]{2,1,0:T(2,128)(2,1)S(1)} %maximum_bitcast_fusion.2), channel_id=2, replica_groups=mesh['section'=2,'ctx'=4,'wa'=4] {'section','wa'}, dimensions={0}, use_global_device_ids=true | all-gather | bytes 8640 | tf_op jit(solution)/shard_map/all_gather | solution.py:597
  77.1 3.4 bitcast_select_fusion.2
  80.5 3.5 copy.88.refs_4_
  101.1 5.4 collective-permute-done.6
  108.5 3.5 collective-permute-done.7
  119.0 2.5 pad_maximum_fusion.2
  122.4 3.9 collective-permute-start.24
  126.4 8.2 collective-permute-start.23
  137.7 2.8 pad_maximum_fusion.1
  140.6 3.6 copy.97
  145.7 3.9 collective-permute-start.31
  168.4 9.8 %attend.2.saved_ref.o_ref = f32[1920,128]{1,0:T(8,128)S(1)} custom-call(s32[128,1]{1,0:T(8,128)S(1)} %copy-done.97, s32[4,512]{1,0:T(4,128)S(1)} %pad_add_fusion.kpos_ref, bf16[128,1920]{1,0:T(8,128)(2,1)S(1)} %copy-done.102, bf16[512,640]{1,0:T(8,128)(2,1)} %constant_dynamic-update-slice_fusion.refs_0_, bf16[512,640]{1,0:T(8,128)(2,1)} %collective-permute-done.8.refs_1_, ...), custom_call_target="tpu_custom_call" | custom-call | flops 2013265920 | bytes 2621440 | tf_op jit(solution)/shard_map/attend/pallas_call | solution.py:196
  183.4 2.4 copy.94
  187.0 2.4 copy.96
  192.2 2.9 bitcast_select_fusion.1
  197.4 10.4 %collective-permute-done.18.refs_3_ = bf16[128,960]{1,0:T(8,128)(2,1)S(1)} collective-permute-done((bf16[128,960]{1,0:T(8,128)(2,1)}, bf16[128,960]{1,0:T(8,128)(2,1)S(1)}, u32[]{:S(2)}, u32[]{:S(2)}) %collective-permute-start.18) | collective-permute-done | bytes 245792 | tf_op jit(solution)/shard_map/ppermute | solution.py:489
  207.8 5.1 mlp.2
  228.9 3.5 copy.98.refs_4_
  240.6 10.3 %collective-permute-done.46.refs_2_ = bf16[240,640]{1,0:T(8,128)(2,1)S(1)} collective-permute-done((bf16[240,640]{1,0:T(8,128)(2,1)S(1)}, bf16[240,640]{1,0:T(8,128)(2,1)S(1)}, u32[]{:S(2)}, u32[]{:S(2)}) %collective-permute-start.46) | collective-permute-done | bytes 307232 | tf_op jit(solution)/shard_map/ppermute | solution.py:489
  251.0 2.4 pad_maximum_fusion.3
  255.2 3.2 collective-permute-start.34
  259.0 5.8 collective-permute-done.33
  276.0 6.5 collective-permute-done.35.refs_1_
  284.2 12.2 %collective-permute-done.37.refs_3_ = bf16[512,640]{1,0:T(8,128)(2,1)} collective-permute-done((bf16[512,640]{1,0:T(8,128)(2,1)}, bf16[512,640]{1,0:T(8,128)(2,1)}, u32[]{:S(2)}, u32[]{:S(2)}) %collective-permute-start.37) | collective-permute-done | bytes 655392 | tf_op jit(solution)/shard_map/ppermute | solution.py:489
  296.5 9.5 %attend.3.saved_ref.o_ref = f32[1920,128]{1,0:T(8,128)S(1)} custom-call(s32[128,1]{1,0:T(8,128)S(1)} %copy-done.98, s32[4,512]{1,0:T(4,128)S(1)} %pad_add_fusion.kpos_ref, bf16[128,1920]{1,0:T(8,128)(2,1)S(1)} %copy-done.105, bf16[512,640]{1,0:T(8,128)(2,1)} %constant_dynamic-update-slice_fusion.4.refs_0_, bf16[512,640]{1,0:T(8,128)(2,1)} %collective-permute-done.35.refs_1_, ...), custom_call_target="tpu_custom_call" | custom-call | flops 2013265920 | bytes 2621440 | tf_op jit(solution)/shard_map/attend/pallas_call | solution.py:196
  324.3 4.3 mlp.3
  333.2 4.5 mlp_back.2
  347.0 4.2 collective-permute-start.106
  356.5 2.4 open_back.2
  359.7 15.3 %attend_back.2 = (f32[128,1920]{1,0:T(8,128)S(1)}, bf16[512,640]{1,0:T(8,128)(2,1)S(1)}, bf16[512,640]{1,0:T(8,128)(2,1)}, bf16[512,640]{1,0:T(8,128)(2,1)}, bf16[512,640]{1,0:T(8,128)(2,1)}) custom-call(s32[1,128]{1,0:T(1,128)S(1)} %add.556.qpos_ref, s32[512,4]{1,0:T(8,128)S(1)} %bitcast.192, bf16[128,1920]{1,0:T(8,128)(2,1)S(1)} %copy-done.106, ...), custom_call_target="tpu_custom_call" | custom-call | flops 5033164800 | bytes 5242880 | tf_op jit(solution)/shard_map/attend_back/pallas_call | solution.py:247
  377.7 2.7 convolution_convert_fusion.2
  381.6 2.5 collective-permute-start.100
  391.0 15.6 %collective-permute-done.60 = bf16[512,640]{1,0:T(8,128)(2,1)} collective-permute-done((bf16[512,640]{1,0:T(8,128)(2,1)}, bf16[512,640]{1,0:T(8,128)(2,1)}, u32[]{:S(2)}, u32[]{:S(2)}) %collective-permute-start.60) | collective-permute-done | bytes 655392 | tf_op jit(solution)/shard_map/ppermute | solution.py:489
  408.9 3.8 collective-permute-start.62
  415.4 11.4 %collective-permute-done.63.refs_2_ = bf16[128,640]{1,0:T(8,128)(2,1)S(1)} collective-permute-done((bf16[128,640]{1,0:T(8,128)(2,1)S(1)}, bf16[128,640]{1,0:T(8,128)(2,1)S(1)}, u32[]{:S(2)}, u32[]{:S(2)}) %collective-permute-start.63) | collective-permute-done | bytes 163872 | tf_op jit(solution)/shard_map/ppermute | solution.py:523
  444.1 3.4 mlp_back.3
  450.2 4.1 convolution_convert_fusion.3
  459.8 2.6 constant_dynamic-slice_fusion.11
  468.2 2.4 open_back.3
  471.4 14.9 %attend_back.3 = (f32[128,1920]{1,0:T(8,128)S(1)}, bf16[512,640]{1,0:T(8,128)(2,1)S(1)}, bf16[512,640]{1,0:T(8,128)(2,1)S(1)}, bf16[512,640]{1,0:T(8,128)(2,1)S(1)}, bf16[512,640]{1,0:T(8,128)(2,1)S(1)}) custom-call(s32[1,128]{1,0:T(1,128)S(1)} %add.556.qpos_ref, s32[512,4]{1,0:T(8,128)S(1)} %bitcast.193, bf16[128,1920]{1,0:T(8,128)(2,1)S(1)} %copy-done.103, ...), custom_call_target="tpu_custom_call" | custom-call | flops 5033164800 | bytes 5242880 | tf_op jit(solution)/shard_map/attend_back/pallas_call | solution.py:247
  491.2 7.4 collective-permute-start.82
  500.9 10.7 %collective-permute-start.96 = (bf16[960,640]{1,0:T(8,128)(2,1)}, bf16[960,640]{1,0:T(8,128)(2,1)}, u32[]{:S(2)}, u32[]{:S(2)}) collective-permute-start(bf16[960,640]{1,0:T(8,128)(2,1)} %constant_dynamic-slice_fusion.11), channel_id=1, source_target_pairs={{0,16},{16,0},{1,17},{17,1},{2,18},{18,2},{3,19},{19,3},{4,20},{20... | collective-permute-start | bytes 3686408 | tf_op jit(solution)/shard_map/ppermute | solution.py:484
  511.6 9.7 %collective-permute-done.72 = bf16[512,640]{1,0:T(8,128)(2,1)S(1)} collective-permute-done((bf16[512,640]{1,0:T(8,128)(2,1)S(1)}, bf16[512,640]{1,0:T(8,128)(2,1)S(1)}, u32[]{:S(2)}, u32[]{:S(2)}) %collective-permute-start.72) | collective-permute-done | bytes 655392 | tf_op jit(solution)/shard_map/ppermute | solution.py:489
  530.9 2.6 add_convert_fusion.7
  533.6 8.7 %collective-permute-done.75.refs_2_ = bf16[128,640]{1,0:T(8,128)(2,1)S(1)} collective-permute-done((bf16[128,640]{1,0:T(8,128)(2,1)}, bf16[128,640]{1,0:T(8,128)(2,1)S(1)}, u32[]{:S(2)}, u32[]{:S(2)}) %collective-permute-start.75) | collective-permute-done | bytes 163872 | tf_op jit(solution)/shard_map/ppermute | solution.py:523
  542.3 2.8 project_back.3
  559.0 4.3 collective-permute-done.89
  566.5 2.5 collective-permute-done.97
  572.4 3.0 collective-permute-done.99
  579.2 4.8 collective-permute-done.85
  585.3 9.5 %collective-permute-done.84 = bf16[120,1600]{1,0:T(8,128)(2,1)S(1)} collective-permute-done((bf16[120,1600]{1,0:T(8,128)(2,1)S(1)}, bf16[120,1600]{1,0:T(8,128)(2,1)S(1)}, u32[]{:S(2)}, u32[]{:S(2)}) %collective-permute-start.84) | collective-permute-done | bytes 384032 | tf_op jit(solution)/shard_map/ppermute | solution.py:489
  595.8 5.3 collective-permute-done.81
  601.1 9.7 %collective-permute-done.80 = bf16[120,1600]{1,0:T(8,128)(2,1)S(1)} collective-permute-done((bf16[120,1600]{1,0:T(8,128)(2,1)S(1)}, bf16[120,1600]{1,0:T(8,128)(2,1)S(1)}, u32[]{:S(2)}, u32[]{:S(2)}) %collective-permute-start.80) | collective-permute-done | bytes 384032 | tf_op jit(solution)/shard_map/ppermute | solution.py:489
  615.4 5.4 collective-permute-done.51
  620.7 6.8 collective-permute-done.50
  631.2 43.5 %psum.63 = f32[2,2,960]{2,1,0:T(2,128)S(1)} all-reduce(f32[2,2,960]{2,1,0:T(2,128)S(1)} %reshape.486), channel_id=1, replica_groups=mesh['section'=2,'ctx'=4,'wa'=4] {'section','ctx','wa'}, use_global_device_ids=true, to_apply=%region_0.1 | all-reduce | flops 3840 | bytes 30720 | tf_op jit(solution)/shard_map/psum | solution.py:689
  676.5 125.4 %all-reduce.3.cloned.1.call-done = (bf16[120,1600]{1,0:T(8,128)(2,1)}, bf16[120,1600]{1,0:T(8,128)(2,1)}, bf16[120,960]{1,0:T(8,128)(2,1)}, bf16[120,960]{1,0:T(...) async-done(((bf16[120,1600]{1,0:T(8,128)(2,1)}, bf16[120,1600]{1,0:T(8,128)(2,1)}, ...) | async-done | bytes 4915216 | tf_op jit(solution)/shard_map/psum | solution.py:672
  805.5 2.6 broadcast_select_fusion
  819.6 3.9 bitcast_convert_fusion
  (661 shorter events, 278.7 us)
Async XLA Ops:
  7.2 794.7 %all-reduce.3.cloned.1.call-start = ((), (), s32[]{:S(2)}) async-start(), calls=%async_computation | async-start | bytes 10444800 | tf_op jit(solution)/shard_map/psum | solution.py:672
  10.2 37.7 %collective-permute-start.11 = (bf16[128,960]{1,0:T(8,128)(2,1)}, bf16[128,960]{1,0:T(8,128)(2,1)}, u32[]{:S(2)}, u32[]{:S(2)}) collective-permute-start(bf16[128,960]{1,0:T(8,128)(2,1)} %dynamic-slice_bitcast_fusion.7), channel_id=1, source_target_pairs={{0,16},{16,0},{1,17},{17,1},{2,18},{18,2},{3,19},{19,3},{4,20},{20... | collective-permute-start | bytes 737288 | tf_op jit(solution)/shard_map/ppermute | solution.py:484
  13.2 63.9 %collective-permute-start.19 = (bf16[240,2560]{1,0:T(8,128)(2,1)}, bf16[240,2560]{1,0:T(8,128)(2,1)}, u32[]{:S(2)}, u32[]{:S(2)}) collective-permute-start(bf16[240,2560]{1,0:T(8,128)(2,1)} %bitcast_select_fusion.3), channel_id=1, source_target_pairs={{0,16},{16,0},{1,17},{17,1},{2,18},{18,2},{3,19},{19,3},{4,20},{20... | collective-permute-start | bytes 3686408 | tf_op jit(solution)/shard_map/ppermute | solution.py:484
  21.3 19.1 %collective-permute-start.2 = (bf16[128,1600]{1,0:T(8,128)(2,1)S(1)}, bf16[128,1600]{1,0:T(8,128)(2,1)S(1)}, u32[]{:S(2)}, u32[]{:S(2)}) collective-permute-start(bf16[128,1600]{1,0:T(8,128)(2,1)S(1)} %get-tuple-element.213.refs_0_), channel_id=1, source_target_pairs={{0,2},{1,3},{2,0},{3,1},{4,6},{5,7},{6,4},{7,5},{8,10},{9,11},{10,... | collective-permute-start | bytes 1228808 | tf_op jit(solution)/shard_map/ppermute | solution.py:489
  22.5 19.1 %collective-permute-start.3 = (bf16[128,1600]{1,0:T(8,128)(2,1)S(1)}, bf16[128,1600]{1,0:T(8,128)(2,1)S(1)}, u32[]{:S(2)}, u32[]{:S(2)}) collective-permute-start(bf16[128,1600]{1,0:T(8,128)(2,1)S(1)} %get-tuple-element.213.refs_0_), channel_id=1, source_target_pairs={{0,3},{1,2},{2,1},{3,0},{4,7},{5,6},{6,5},{7,4},{8,11},{9,10},{10,... | collective-permute-start | bytes 1228808 | tf_op jit(solution)/shard_map/ppermute | solution.py:489
  46.8 33.7 %collective-permute-start.4 = (bf16[4,128,1600]{1,2,0:T(8,128)(2,1)}, bf16[4,128,1600]{1,2,0:T(8,128)(2,1)}, u32[]{:S(2)}, u32[]{:S(2)}) collective-permute-start(bf16[4,128,1600]{1,2,0:T(8,128)(2,1)} %copy.87), channel_id=1, source_target_pairs={{0,16},{16,0},{1,17},{17,1},{2,18},{18,2},{3,19},{19,3},{4,20},{20... | collective-permute-start | bytes 4915208 | tf_op jit(solution)/shard_map/ppermute | solution.py:484
  49.7 23.8 %collective-permute-start.12 = (bf16[128,960]{1,0:T(8,128)(2,1)S(1)}, bf16[128,960]{1,0:T(8,128)(2,1)S(1)}, u32[]{:S(2)}, u32[]{:S(2)}) collective-permute-start(bf16[128,960]{1,0:T(8,128)(2,1)S(1)} %get-tuple-element.227.refs_0_), channel_id=1, source_target_pairs={{0,1},{1,0},{2,3},{3,2},{4,5},{5,4},{6,7},{7,6},{8,9},{9,8},{10,11... | collective-permute-start | bytes 737288 | tf_op jit(solution)/shard_map/ppermute | solution.py:489
  50.6 22.9 %collective-permute-start.13 = (bf16[128,960]{1,0:T(8,128)(2,1)S(1)}, bf16[128,960]{1,0:T(8,128)(2,1)S(1)}, u32[]{:S(2)}, u32[]{:S(2)}) collective-permute-start(bf16[128,960]{1,0:T(8,128)(2,1)S(1)} %get-tuple-element.227.refs_0_), channel_id=1, source_target_pairs={{0,2},{1,3},{2,0},{3,1},{4,6},{5,7},{6,4},{7,5},{8,10},{9,11},{10,... | collective-permute-start | bytes 737288 | tf_op jit(solution)/shard_map/ppermute | solution.py:489
  51.2 22.4 %collective-permute-start.14 = (bf16[128,960]{1,0:T(8,128)(2,1)S(1)}, bf16[128,960]{1,0:T(8,128)(2,1)S(1)}, u32[]{:S(2)}, u32[]{:S(2)}) collective-permute-start(bf16[128,960]{1,0:T(8,128)(2,1)S(1)} %get-tuple-element.227.refs_0_), channel_id=1, source_target_pairs={{0,3},{1,2},{2,1},{3,0},{4,7},{5,6},{6,5},{7,4},{8,11},{9,10},{10,... | collective-permute-start | bytes 737288 | tf_op jit(solution)/shard_map/ppermute | solution.py:489
  77.0 59.8 %collective-permute-start.15 = (bf16[4,128,960]{1,2,0:T(8,128)(2,1)}, bf16[4,128,960]{1,2,0:T(8,128)(2,1)}, u32[]{:S(2)}, u32[]{:S(2)}) collective-permute-start(bf16[4,128,960]{1,2,0:T(8,128)(2,1)} %copy.92), channel_id=1, source_target_pairs={{0,16},{16,0},{1,17},{17,1},{2,18},{18,2},{3,19},{19,3},{4,20},{20... | collective-permute-start | bytes 2949128 | tf_op jit(solution)/shard_map/ppermute | solution.py:484
  95.9 17.8 %collective-permute-start.20 = (bf16[240,640]{1,0:T(8,128)(2,1)S(1)}, bf16[240,640]{1,0:T(8,128)(2,1)}, u32[]{:S(2)}, u32[]{:S(2)}) collective-permute-start(bf16[240,640]{1,0:T(8,128)(2,1)S(1)} %get-tuple-element.210), channel_id=1, source_target_pairs={{0,1},{1,0},{2,3},{3,2},{4,5},{5,4},{6,7},{7,6},{8,9},{9,8},{10,11... | collective-permute-start | bytes 921608 | tf_op jit(solution)/shard_map/ppermute | solution.py:489
  96.9 18.3 %collective-permute-start.21 = (bf16[240,640]{1,0:T(8,128)(2,1)S(1)}, bf16[240,640]{1,0:T(8,128)(2,1)}, u32[]{:S(2)}, u32[]{:S(2)}) collective-permute-start(bf16[240,640]{1,0:T(8,128)(2,1)S(1)} %get-tuple-element.209), channel_id=1, source_target_pairs={{0,2},{1,3},{2,0},{3,1},{4,6},{5,7},{6,4},{7,5},{8,10},{9,11},{10,... | collective-permute-start | bytes 921608 | tf_op jit(solution)/shard_map/ppermute | solution.py:489
  98.8 17.2 %collective-permute-start.22 = (bf16[240,640]{1,0:T(8,128)(2,1)S(1)}, bf16[240,640]{1,0:T(8,128)(2,1)}, u32[]{:S(2)}, u32[]{:S(2)}) collective-permute-start(bf16[240,640]{1,0:T(8,128)(2,1)S(1)} %get-tuple-element.208), channel_id=1, source_target_pairs={{0,3},{1,2},{2,1},{3,0},{4,7},{5,6},{6,5},{7,4},{8,11},{9,10},{10,... | collective-permute-start | bytes 921608 | tf_op jit(solution)/shard_map/ppermute | solution.py:489
  115.1 19.4 %collective-permute-start.30 = (bf16[128,1600]{1,0:T(8,128)(2,1)}, bf16[128,1600]{1,0:T(8,128)(2,1)}, u32[]{:S(2)}, u32[]{:S(2)}) collective-permute-start(bf16[128,1600]{1,0:T(8,128)(2,1)} %get-tuple-element.212.refs_0_), channel_id=1, source_target_pairs={{0,3},{1,2},{2,1},{3,0},{4,7},{5,6},{6,5},{7,4},{8,11},{9,10},{10,... | collective-permute-start | bytes 1228808 | tf_op jit(solution)/shard_map/ppermute | solution.py:489
  116.0 29.6 %collective-permute-start.8 = (bf16[512,640]{1,0:T(8,128)(2,1)}, bf16[512,640]{1,0:T(8,128)(2,1)}, u32[]{:S(2)}, u32[]{:S(2)}) collective-permute-start(bf16[512,640]{1,0:T(8,128)(2,1)} %constant_dynamic-update-slice_fusion.refs_0_), channel_id=1, source_target_pairs={{0,1},{1,0},{2,3},{3,2},{4,5},{5,4},{6,7},{7,6},{8,9},{9,8},{10,11... | collective-permute-start | bytes 1966088 | tf_op jit(solution)/shard_map/ppermute | solution.py:489
  122.4 63.4 %collective-permute-start.24 = (bf16[640,960]{0,1:T(8,128)(2,1)}, bf16[640,960]{0,1:T(8,128)(2,1)}, u32[]{:S(2)}, u32[]{:S(2)}) collective-permute-start(bf16[640,960]{0,1:T(8,128)(2,1)} %bitcast.36), channel_id=1, source_target_pairs={{0,16},{16,0},{1,17},{17,1},{2,18},{18,2},{3,19},{19,3},{4,20},{20... | collective-permute-start | bytes 3686408 | tf_op jit(solution)/shard_map/ppermute | solution.py:484
  126.4 63.0 %collective-permute-start.23 = (bf16[4,240,640]{2,1,0:T(8,128)(2,1)}, bf16[4,240,640]{2,1,0:T(8,128)(2,1)}, u32[]{:S(2)}, u32[]{:S(2)}) collective-permute-start(bf16[4,240,640]{2,1,0:T(8,128)(2,1)} %pad_maximum_fusion.2), channel_id=1, source_target_pairs={{0,16},{16,0},{1,17},{17,1},{2,18},{18,2},{3,19},{19,3},{4,20},{20... | collective-permute-start | bytes 3686408 | tf_op jit(solution)/shard_map/ppermute | solution.py:484
  134.5 33.5 %collective-permute-start.9 = (bf16[512,640]{1,0:T(8,128)(2,1)}, bf16[512,640]{1,0:T(8,128)(2,1)}, u32[]{:S(2)}, u32[]{:S(2)}) collective-permute-start(bf16[512,640]{1,0:T(8,128)(2,1)} %constant_dynamic-update-slice_fusion.refs_0_), channel_id=1, source_target_pairs={{0,2},{1,3},{2,0},{3,1},{4,6},{5,7},{6,4},{7,5},{8,10},{9,11},{10,... | collective-permute-start | bytes 1966088 | tf_op jit(solution)/shard_map/ppermute | solution.py:489
  136.8 31.2 %collective-permute-start.10 = (bf16[512,640]{1,0:T(8,128)(2,1)}, bf16[512,640]{1,0:T(8,128)(2,1)}, u32[]{:S(2)}, u32[]{:S(2)}) collective-permute-start(bf16[512,640]{1,0:T(8,128)(2,1)} %constant_dynamic-update-slice_fusion.refs_0_), channel_id=1, source_target_pairs={{0,3},{1,2},{2,1},{3,0},{4,7},{5,6},{6,5},{7,4},{8,11},{9,10},{10,... | collective-permute-start | bytes 1966088 | tf_op jit(solution)/shard_map/ppermute | solution.py:489
  145.7 82.9 %collective-permute-start.31 = (bf16[4,128,1600]{1,2,0:T(8,128)(2,1)}, bf16[4,128,1600]{1,2,0:T(8,128)(2,1)}, u32[]{:S(2)}, u32[]{:S(2)}) collective-permute-start(bf16[4,128,1600]{1,2,0:T(8,128)(2,1)} %copy.97), channel_id=1, source_target_pairs={{0,16},{16,0},{1,17},{17,1},{2,18},{18,2},{3,19},{19,3},{4,20},{20... | collective-permute-start | bytes 4915208 | tf_op jit(solution)/shard_map/ppermute | solution.py:484
  185.8 30.6 %collective-permute-start.38 = (bf16[128,960]{1,0:T(8,128)(2,1)}, bf16[128,960]{1,0:T(8,128)(2,1)}, u32[]{:S(2)}, u32[]{:S(2)}) collective-permute-start(bf16[128,960]{1,0:T(8,128)(2,1)} %get-tuple-element.226.refs_0_), channel_id=1, source_target_pairs={{0,1},{1,0},{2,3},{3,2},{4,5},{5,4},{6,7},{7,6},{8,9},{9,8},{10,11... | collective-permute-start | bytes 737288 | tf_op jit(solution)/shard_map/ppermute | solution.py:489
  189.4 28.2 %collective-permute-start.39 = (bf16[128,960]{1,0:T(8,128)(2,1)}, bf16[128,960]{1,0:T(8,128)(2,1)S(1)}, u32[]{:S(2)}, u32[]{:S(2)}) collective-permute-start(bf16[128,960]{1,0:T(8,128)(2,1)} %get-tuple-element.226.refs_0_), channel_id=1, source_target_pairs={{0,2},{1,3},{2,0},{3,1},{4,6},{5,7},{6,4},{7,5},{8,10},{9,11},{10,... | collective-permute-start | bytes 737288 | tf_op jit(solution)/shard_map/ppermute | solution.py:489
  189.4 29.4 %collective-permute-start.40 = (bf16[128,960]{1,0:T(8,128)(2,1)}, bf16[128,960]{1,0:T(8,128)(2,1)S(1)}, u32[]{:S(2)}, u32[]{:S(2)}) collective-permute-start(bf16[128,960]{1,0:T(8,128)(2,1)} %get-tuple-element.226.refs_0_), channel_id=1, source_target_pairs={{0,3},{1,2},{2,1},{3,0},{4,7},{5,6},{6,5},{7,4},{8,11},{9,10},{10,... | collective-permute-start | bytes 737288 | tf_op jit(solution)/shard_map/ppermute | solution.py:489
  191.3 16.5 %collective-permute-start.18 = (bf16[128,960]{1,0:T(8,128)(2,1)}, bf16[128,960]{1,0:T(8,128)(2,1)S(1)}, u32[]{:S(2)}, u32[]{:S(2)}) collective-permute-start(bf16[128,960]{1,0:T(8,128)(2,1)} %get-tuple-element.70.refs_0_), channel_id=1, source_target_pairs={{0,3},{1,2},{2,1},{3,0},{4,7},{5,6},{6,5},{7,4},{8,11},{9,10},{10,... | collective-permute-start | bytes 737288 | tf_op jit(solution)/shard_map/ppermute | solution.py:489
  216.1 19.6 %collective-permute-start.27 = (bf16[128,960]{1,0:T(8,128)(2,1)}, bf16[128,960]{1,0:T(8,128)(2,1)}, u32[]{:S(2)}, u32[]{:S(2)}) collective-permute-start(bf16[128,960]{1,0:T(8,128)(2,1)} %get-tuple-element.74), channel_id=1, source_target_pairs={{0,3},{1,2},{2,1},{3,0},{4,7},{5,6},{6,5},{7,4},{8,11},{9,10},{10,... | collective-permute-start | bytes 737288 | tf_op jit(solution)/shard_map/ppermute | solution.py:489
  216.4 19.6 %collective-permute-start.26 = (bf16[128,960]{1,0:T(8,128)(2,1)}, bf16[128,960]{1,0:T(8,128)(2,1)}, u32[]{:S(2)}, u32[]{:S(2)}) collective-permute-start(bf16[128,960]{1,0:T(8,128)(2,1)} %get-tuple-element.73), channel_id=1, source_target_pairs={{0,2},{1,3},{2,0},{3,1},{4,6},{5,7},{6,4},{7,5},{8,10},{9,11},{10,... | collective-permute-start | bytes 737288 | tf_op jit(solution)/shard_map/ppermute | solution.py:489
  217.6 20.5 %collective-permute-start.25 = (bf16[128,960]{1,0:T(8,128)(2,1)}, bf16[128,960]{1,0:T(8,128)(2,1)}, u32[]{:S(2)}, u32[]{:S(2)}) collective-permute-start(bf16[128,960]{1,0:T(8,128)(2,1)} %get-tuple-element.72), channel_id=1, source_target_pairs={{0,1},{1,0},{2,3},{3,2},{4,5},{5,4},{6,7},{7,6},{8,9},{9,8},{10,11... | collective-permute-start | bytes 737288 | tf_op jit(solution)/shard_map/ppermute | solution.py:489
  224.6 44.7 %collective-permute-start.41 = (bf16[4,128,960]{1,2,0:T(8,128)(2,1)}, bf16[4,128,960]{1,2,0:T(8,128)(2,1)}, u32[]{:S(2)}, u32[]{:S(2)}) collective-permute-start(bf16[4,128,960]{1,2,0:T(8,128)(2,1)} %copy.102), channel_id=1, source_target_pairs={{0,16},{16,0},{1,17},{17,1},{2,18},{18,2},{3,19},{19,3},{4,20},{20... | collective-permute-start | bytes 2949128 | tf_op jit(solution)/shard_map/ppermute | solution.py:484
  240.6 17.8 %collective-permute-start.32 = (bf16[128,640]{1,0:T(8,128)(2,1)S(1)}, bf16[128,640]{1,0:T(8,128)(2,1)S(1)}, u32[]{:S(2)}, u32[]{:S(2)}) collective-permute-start(bf16[128,640]{1,0:T(8,128)(2,1)S(1)} %get-tuple-element.76), channel_id=1, source_target_pairs={{0,4},{4,8},{8,12},{12,0},{1,5},{5,9},{9,13},{13,1},{2,6},{6,10},{... | collective-permute-start | bytes 491528 | tf_op jit(solution)/shard_map/ppermute | solution.py:510
  253.4 61.7 %collective-permute-start.48 = (bf16[4,240,640]{2,1,0:T(8,128)(2,1)}, bf16[4,240,640]{2,1,0:T(8,128)(2,1)}, u32[]{:S(2)}, u32[]{:S(2)}) collective-permute-start(bf16[4,240,640]{2,1,0:T(8,128)(2,1)} %pad_maximum_fusion.3), channel_id=1, source_target_pairs={{0,16},{16,0},{1,17},{17,1},{2,18},{18,2},{3,19},{19,3},{4,20},{20... | collective-permute-start | bytes 3686408 | tf_op jit(solution)/shard_map/ppermute | solution.py:484
  266.7 15.8 %collective-permute-start.35 = (bf16[512,640]{1,0:T(8,128)(2,1)}, bf16[512,640]{1,0:T(8,128)(2,1)}, u32[]{:S(2)}, u32[]{:S(2)}) collective-permute-start(bf16[512,640]{1,0:T(8,128)(2,1)} %constant_dynamic-update-slice_fusion.4.refs_0_), channel_id=1, source_target_pairs={{0,1},{1,0},{2,3},{3,2},{4,5},{5,4},{6,7},{7,6},{8,9},{9,8},{10,11... | collective-permute-start | bytes 1966088 | tf_op jit(solution)/shard_map/ppermute | solution.py:489
  267.8 16.4 %collective-permute-start.36 = (bf16[512,640]{1,0:T(8,128)(2,1)}, bf16[512,640]{1,0:T(8,128)(2,1)}, u32[]{:S(2)}, u32[]{:S(2)}) collective-permute-start(bf16[512,640]{1,0:T(8,128)(2,1)} %constant_dynamic-update-slice_fusion.4.refs_0_), channel_id=1, source_target_pairs={{0,2},{1,3},{2,0},{3,1},{4,6},{5,7},{6,4},{7,5},{8,10},{9,11},{10,... | collective-permute-start | bytes 1966088 | tf_op jit(solution)/shard_map/ppermute | solution.py:489
  267.8 28.6 %collective-permute-start.37 = (bf16[512,640]{1,0:T(8,128)(2,1)}, bf16[512,640]{1,0:T(8,128)(2,1)}, u32[]{:S(2)}, u32[]{:S(2)}) collective-permute-start(bf16[512,640]{1,0:T(8,128)(2,1)} %constant_dynamic-update-slice_fusion.4.refs_0_), channel_id=1, source_target_pairs={{0,3},{1,2},{2,1},{3,0},{4,7},{5,6},{6,5},{7,4},{8,11},{9,10},{10,... | collective-permute-start | bytes 1966088 | tf_op jit(solution)/shard_map/ppermute | solution.py:489
  314.1 17.4 %collective-permute-start.53 = (bf16[128,960]{1,0:T(8,128)(2,1)}, bf16[128,960]{1,0:T(8,128)(2,1)}, u32[]{:S(2)}, u32[]{:S(2)}) collective-permute-start(bf16[128,960]{1,0:T(8,128)(2,1)} %bitcast.175), channel_id=1, source_target_pairs={{0,1},{1,0},{2,3},{3,2},{4,5},{5,4},{6,7},{7,6},{8,9},{9,8},{10,11... | collective-permute-start | bytes 737288 | tf_op jit(solution)/shard_map/ppermute | solution.py:489
  315.0 16.4 %collective-permute-start.54 = (bf16[128,960]{1,0:T(8,128)(2,1)}, bf16[128,960]{1,0:T(8,128)(2,1)}, u32[]{:S(2)}, u32[]{:S(2)}) collective-permute-start(bf16[128,960]{1,0:T(8,128)(2,1)} %bitcast.176), channel_id=1, source_target_pairs={{0,2},{1,3},{2,0},{3,1},{4,6},{5,7},{6,4},{7,5},{8,10},{9,11},{10,... | collective-permute-start | bytes 737288 | tf_op jit(solution)/shard_map/ppermute | solution.py:489
  316.5 16.8 %collective-permute-start.55 = (bf16[128,960]{1,0:T(8,128)(2,1)}, bf16[128,960]{1,0:T(8,128)(2,1)}, u32[]{:S(2)}, u32[]{:S(2)}) collective-permute-start(bf16[128,960]{1,0:T(8,128)(2,1)} %bitcast.177), channel_id=1, source_target_pairs={{0,3},{1,2},{2,1},{3,0},{4,7},{5,6},{6,5},{7,4},{8,11},{9,10},{10,... | collective-permute-start | bytes 737288 | tf_op jit(solution)/shard_map/ppermute | solution.py:489
  347.0 40.1 %collective-permute-start.106 = (bf16[320,960]{1,0:T(8,128)(2,1)}, bf16[320,960]{1,0:T(8,128)(2,1)}, u32[]{:S(2)}, u32[]{:S(2)}) collective-permute-start(bf16[320,960]{1,0:T(8,128)(2,1)} %copy.113), channel_id=1, source_target_pairs={{0,16},{16,0},{1,17},{17,1},{2,18},{18,2},{3,19},{19,3},{4,20},{20... | collective-permute-start | bytes 1843208 | tf_op jit(solution)/shard_map/ppermute | solution.py:484
  375.0 16.0 %collective-permute-start.61 = (bf16[512,640]{1,0:T(8,128)(2,1)}, bf16[512,640]{1,0:T(8,128)(2,1)}, u32[]{:S(2)}, u32[]{:S(2)}) collective-permute-start(bf16[512,640]{1,0:T(8,128)(2,1)} %get-tuple-element.92), channel_id=1, source_target_pairs={{0,3},{1,2},{2,1},{3,0},{4,7},{5,6},{6,5},{7,4},{8,11},{9,10},{10,... | collective-permute-start | bytes 1966088 | tf_op jit(solution)/shard_map/ppermute | solution.py:489
  375.8 30.8 %collective-permute-start.60 = (bf16[512,640]{1,0:T(8,128)(2,1)}, bf16[512,640]{1,0:T(8,128)(2,1)}, u32[]{:S(2)}, u32[]{:S(2)}) collective-permute-start(bf16[512,640]{1,0:T(8,128)(2,1)} %get-tuple-element.91), channel_id=1, source_target_pairs={{0,2},{1,3},{2,0},{3,1},{4,6},{5,7},{6,4},{7,5},{8,10},{9,11},{10,... | collective-permute-start | bytes 1966088 | tf_op jit(solution)/shard_map/ppermute | solution.py:489
  376.1 30.6 %collective-permute-start.59 = (bf16[512,640]{1,0:T(8,128)(2,1)}, bf16[512,640]{1,0:T(8,128)(2,1)}, u32[]{:S(2)}, u32[]{:S(2)}) collective-permute-start(bf16[512,640]{1,0:T(8,128)(2,1)} %get-tuple-element.90), channel_id=1, source_target_pairs={{0,1},{1,0},{2,3},{3,2},{4,5},{5,4},{6,7},{7,6},{8,9},{9,8},{10,11... | collective-permute-start | bytes 1966088 | tf_op jit(solution)/shard_map/ppermute | solution.py:489
  381.6 58.1 %collective-permute-start.100 = (bf16[960,640]{1,0:T(8,128)(2,1)}, bf16[960,640]{1,0:T(8,128)(2,1)}, u32[]{:S(2)}, u32[]{:S(2)}) collective-permute-start(bf16[960,640]{1,0:T(8,128)(2,1)} %constant_dynamic-slice_fusion.6), channel_id=1, source_target_pairs={{0,16},{16,0},{1,17},{17,1},{2,18},{18,2},{3,19},{19,3},{4,20},{20... | collective-permute-start | bytes 3686408 | tf_op jit(solution)/shard_map/ppermute | solution.py:484
  387.1 47.6 %collective-permute-start.91 = (bf16[4,1,120,960]{3,2,1,0:T(8,128)(2,1)}, bf16[4,1,120,960]{3,2,1,0:T(8,128)(2,1)}, u32[]{:S(2)}, u32[]{:S(2)}) collective-permute-start(bf16[4,1,120,960]{3,2,1,0:T(8,128)(2,1)} %constant_dynamic-slice_fusion.12), channel_id=1, source_target_pairs={{0,16},{16,0},{1,17},{17,1},{2,18},{18,2},{3,19},{19,3},{4,20},{20... | collective-permute-start | bytes 2764808 | tf_op jit(solution)/shard_map/ppermute | solution.py:484
  428.7 15.4 %collective-permute-start.65 = (bf16[128,960]{1,0:T(8,128)(2,1)S(1)}, bf16[128,960]{1,0:T(8,128)(2,1)S(1)}, u32[]{:S(2)}, u32[]{:S(2)}) collective-permute-start(bf16[128,960]{1,0:T(8,128)(2,1)S(1)} %get-tuple-element.95.refs_0_.refs_6_), channel_id=1, source_target_pairs={{0,1},{1,0},{2,3},{3,2},{4,5},{5,4},{6,7},{7,6},{8,9},{9,8},{10,11... | collective-permute-start | bytes 737288 | tf_op jit(solution)/shard_map/ppermute | solution.py:489
  437.9 48.5 %collective-permute-start.94 = (bf16[120,960]{1,0:T(8,128)(2,1)}, bf16[120,960]{1,0:T(8,128)(2,1)}, u32[]{:S(2)}, u32[]{:S(2)}) collective-permute-start(bf16[120,960]{1,0:T(8,128)(2,1)} %get-tuple-element.220), channel_id=1, source_target_pairs={{0,3},{1,2},{2,1},{3,0},{4,7},{5,6},{6,5},{7,4},{8,11},{9,10},{10,... | collective-permute-start | bytes 691208 | tf_op jit(solution)/shard_map/ppermute | solution.py:489
  439.7 48.4 %collective-permute-start.93 = (bf16[120,960]{1,0:T(8,128)(2,1)}, bf16[120,960]{1,0:T(8,128)(2,1)}, u32[]{:S(2)}, u32[]{:S(2)}) collective-permute-start(bf16[120,960]{1,0:T(8,128)(2,1)} %get-tuple-element.221), channel_id=1, source_target_pairs={{0,2},{1,3},{2,0},{3,1},{4,6},{5,7},{6,4},{7,5},{8,10},{9,11},{10,... | collective-permute-start | bytes 691208 | tf_op jit(solution)/shard_map/ppermute | solution.py:489
  448.1 17.1 %collective-permute-start.69 = (bf16[128,960]{1,0:T(8,128)(2,1)}, bf16[128,960]{1,0:T(8,128)(2,1)}, u32[]{:S(2)}, u32[]{:S(2)}) collective-permute-start(bf16[128,960]{1,0:T(8,128)(2,1)} %get-tuple-element.99), channel_id=1, source_target_pairs={{0,2},{1,3},{2,0},{3,1},{4,6},{5,7},{6,4},{7,5},{8,10},{9,11},{10,... | collective-permute-start | bytes 737288 | tf_op jit(solution)/shard_map/ppermute | solution.py:489
  449.1 17.0 %collective-permute-start.70 = (bf16[128,960]{1,0:T(8,128)(2,1)}, bf16[128,960]{1,0:T(8,128)(2,1)}, u32[]{:S(2)}, u32[]{:S(2)}) collective-permute-start(bf16[128,960]{1,0:T(8,128)(2,1)} %get-tuple-element.100), channel_id=1, source_target_pairs={{0,3},{1,2},{2,1},{3,0},{4,7},{5,6},{6,5},{7,4},{8,11},{9,10},{10,... | collective-permute-start | bytes 737288 | tf_op jit(solution)/shard_map/ppermute | solution.py:489
  462.4 26.5 %collective-permute-start.92 = (bf16[120,960]{1,0:T(8,128)(2,1)}, bf16[120,960]{1,0:T(8,128)(2,1)S(1)}, u32[]{:S(2)}, u32[]{:S(2)}) collective-permute-start(bf16[120,960]{1,0:T(8,128)(2,1)} %get-tuple-element.219), channel_id=1, source_target_pairs={{0,1},{1,0},{2,3},{3,2},{4,5},{5,4},{6,7},{7,6},{8,9},{9,8},{10,11... | collective-permute-start | bytes 691208 | tf_op jit(solution)/shard_map/ppermute | solution.py:489
  465.2 26.0 %collective-permute-start.101 = (bf16[240,640]{1,0:T(8,128)(2,1)}, bf16[240,640]{1,0:T(8,128)(2,1)S(1)}, u32[]{:S(2)}, u32[]{:S(2)}) collective-permute-start(bf16[240,640]{1,0:T(8,128)(2,1)} %get-tuple-element.200), channel_id=1, source_target_pairs={{0,1},{1,0},{2,3},{3,2},{4,5},{5,4},{6,7},{7,6},{8,9},{9,8},{10,11... | collective-permute-start | bytes 921608 | tf_op jit(solution)/shard_map/ppermute | solution.py:489
  466.1 33.2 %collective-permute-start.102 = (bf16[240,640]{1,0:T(8,128)(2,1)}, bf16[240,640]{1,0:T(8,128)(2,1)S(1)}, u32[]{:S(2)}, u32[]{:S(2)}) collective-permute-start(bf16[240,640]{1,0:T(8,128)(2,1)} %get-tuple-element.199), channel_id=1, source_target_pairs={{0,2},{1,3},{2,0},{3,1},{4,6},{5,7},{6,4},{7,5},{8,10},{9,11},{10,... | collective-permute-start | bytes 921608 | tf_op jit(solution)/shard_map/ppermute | solution.py:489
  488.2 33.1 %collective-permute-start.72 = (bf16[512,640]{1,0:T(8,128)(2,1)S(1)}, bf16[512,640]{1,0:T(8,128)(2,1)S(1)}, u32[]{:S(2)}, u32[]{:S(2)}) collective-permute-start(bf16[512,640]{1,0:T(8,128)(2,1)S(1)} %get-tuple-element.104), channel_id=1, source_target_pairs={{0,2},{1,3},{2,0},{3,1},{4,6},{5,7},{6,4},{7,5},{8,10},{9,11},{10,... | collective-permute-start | bytes 1966088 | tf_op jit(solution)/shard_map/ppermute | solution.py:489
  488.9 32.9 %collective-permute-start.71 = (bf16[512,640]{1,0:T(8,128)(2,1)S(1)}, bf16[512,640]{1,0:T(8,128)(2,1)S(1)}, u32[]{:S(2)}, u32[]{:S(2)}) collective-permute-start(bf16[512,640]{1,0:T(8,128)(2,1)S(1)} %get-tuple-element.103), channel_id=1, source_target_pairs={{0,1},{1,0},{2,3},{3,2},{4,5},{5,4},{6,7},{7,6},{8,9},{9,8},{10,11... | collective-permute-start | bytes 1966088 | tf_op jit(solution)/shard_map/ppermute | solution.py:489
  491.2 62.7 %collective-permute-start.82 = (bf16[4,1,120,1600]{3,2,1,0:T(8,128)(2,1)}, bf16[4,1,120,1600]{3,2,1,0:T(8,128)(2,1)}, u32[]{:S(2)}, u32[]{:S(2)}) collective-permute-start(bf16[4,1,120,1600]{3,2,1,0:T(8,128)(2,1)} %constant_dynamic-slice_fusion.14), channel_id=1, source_target_pairs={{0,16},{16,0},{1,17},{17,1},{2,18},{18,2},{3,19},{19,3},{4,20},{20... | collective-permute-start | bytes 4608008 | tf_op jit(solution)/shard_map/ppermute | solution.py:484
  499.3 24.7 %collective-permute-start.103 = (bf16[240,640]{1,0:T(8,128)(2,1)S(1)}, bf16[240,640]{1,0:T(8,128)(2,1)S(1)}, u32[]{:S(2)}, u32[]{:S(2)}) collective-permute-start(bf16[240,640]{1,0:T(8,128)(2,1)S(1)} %copy-done.147), channel_id=1, source_target_pairs={{0,3},{1,2},{2,1},{3,0},{4,7},{5,6},{6,5},{7,4},{8,11},{9,10},{10,... | collective-permute-start | bytes 921608 | tf_op jit(solution)/shard_map/ppermute | solution.py:489
  500.9 50.9 %collective-permute-start.96 = (bf16[960,640]{1,0:T(8,128)(2,1)}, bf16[960,640]{1,0:T(8,128)(2,1)}, u32[]{:S(2)}, u32[]{:S(2)}) collective-permute-start(bf16[960,640]{1,0:T(8,128)(2,1)} %constant_dynamic-slice_fusion.11), channel_id=1, source_target_pairs={{0,16},{16,0},{1,17},{17,1},{2,18},{18,2},{3,19},{19,3},{4,20},{20... | collective-permute-start | bytes 3686408 | tf_op jit(solution)/shard_map/ppermute | solution.py:484
  524.0 23.1 %collective-permute-start.87 = (bf16[4,1,120,960]{3,2,1,0:T(8,128)(2,1)}, bf16[4,1,120,960]{3,2,1,0:T(8,128)(2,1)}, u32[]{:S(2)}, u32[]{:S(2)}) collective-permute-start(bf16[4,1,120,960]{3,2,1,0:T(8,128)(2,1)} %constant_dynamic-slice_fusion.13), channel_id=1, source_target_pairs={{0,16},{16,0},{1,17},{17,1},{2,18},{18,2},{3,19},{19,3},{4,20},{20... | collective-permute-start | bytes 2764808 | tf_op jit(solution)/shard_map/ppermute | solution.py:484
  546.3 29.2 %collective-permute-start.78 = (bf16[4,1,120,1600]{3,2,1,0:T(8,128)(2,1)S(1)}, bf16[4,1,120,1600]{3,2,1,0:T(8,128)(2,1)S(1)}, u32[]{:S(2)}, u32[]{:S(2)}) collective-permute-start(bf16[4,1,120,1600]{3,2,1,0:T(8,128)(2,1)S(1)} %constant_dynamic-slice_fusion.15), channel_id=1, source_target_pairs={{0,16},{16,0},{1,17},{17,1},{2,18},{18,2},{3,19},{19,3},{4,20},{20... | collective-permute-start | bytes 4608008 | tf_op jit(solution)/shard_map/ppermute | solution.py:484
  564.2 19.8 %collective-permute-start.85 = (bf16[120,1600]{1,0:T(8,128)(2,1)S(1)}, bf16[120,1600]{1,0:T(8,128)(2,1)S(1)}, u32[]{:S(2)}, u32[]{:S(2)}) collective-permute-start(bf16[120,1600]{1,0:T(8,128)(2,1)S(1)} %get-tuple-element.192), channel_id=1, source_target_pairs={{0,3},{1,2},{2,1},{3,0},{4,7},{5,6},{6,5},{7,4},{8,11},{9,10},{10,... | collective-permute-start | bytes 1152008 | tf_op jit(solution)/shard_map/ppermute | solution.py:489
  569.1 25.7 %collective-permute-start.84 = (bf16[120,1600]{1,0:T(8,128)(2,1)S(1)}, bf16[120,1600]{1,0:T(8,128)(2,1)S(1)}, u32[]{:S(2)}, u32[]{:S(2)}) collective-permute-start(bf16[120,1600]{1,0:T(8,128)(2,1)S(1)} %get-tuple-element.193), channel_id=1, source_target_pairs={{0,2},{1,3},{2,0},{3,1},{4,6},{5,7},{6,4},{7,5},{8,10},{9,11},{10,... | collective-permute-start | bytes 1152008 | tf_op jit(solution)/shard_map/ppermute | solution.py:489
  571.0 23.7 %collective-permute-start.83 = (bf16[120,1600]{1,0:T(8,128)(2,1)S(1)}, bf16[120,1600]{1,0:T(8,128)(2,1)S(1)}, u32[]{:S(2)}, u32[]{:S(2)}) collective-permute-start(bf16[120,1600]{1,0:T(8,128)(2,1)S(1)} %get-tuple-element.191), channel_id=1, source_target_pairs={{0,1},{1,0},{2,3},{3,2},{4,5},{5,4},{6,7},{7,6},{8,9},{9,8},{10,11... | collective-permute-start | bytes 1152008 | tf_op jit(solution)/shard_map/ppermute | solution.py:489
  576.6 24.5 %collective-permute-start.81 = (bf16[120,1600]{1,0:T(8,128)(2,1)S(1)}, bf16[120,1600]{1,0:T(8,128)(2,1)S(1)}, u32[]{:S(2)}, u32[]{:S(2)}) collective-permute-start(bf16[120,1600]{1,0:T(8,128)(2,1)S(1)} %get-tuple-element.189), channel_id=1, source_target_pairs={{0,3},{1,2},{2,1},{3,0},{4,7},{5,6},{6,5},{7,4},{8,11},{9,10},{10,... | collective-permute-start | bytes 1152008 | tf_op jit(solution)/shard_map/ppermute | solution.py:489
  578.9 31.8 %collective-permute-start.80 = (bf16[120,1600]{1,0:T(8,128)(2,1)S(1)}, bf16[120,1600]{1,0:T(8,128)(2,1)S(1)}, u32[]{:S(2)}, u32[]{:S(2)}) collective-permute-start(bf16[120,1600]{1,0:T(8,128)(2,1)S(1)} %get-tuple-element.190), channel_id=1, source_target_pairs={{0,2},{1,3},{2,0},{3,1},{4,6},{5,7},{6,4},{7,5},{8,10},{9,11},{10,... | collective-permute-start | bytes 1152008 | tf_op jit(solution)/shard_map/ppermute | solution.py:489
  584.0 26.8 %collective-permute-start.79 = (bf16[120,1600]{1,0:T(8,128)(2,1)S(1)}, bf16[120,1600]{1,0:T(8,128)(2,1)S(1)}, u32[]{:S(2)}, u32[]{:S(2)}) collective-permute-start(bf16[120,1600]{1,0:T(8,128)(2,1)S(1)} %get-tuple-element.188), channel_id=1, source_target_pairs={{0,1},{1,0},{2,3},{3,2},{4,5},{5,4},{6,7},{7,6},{8,9},{9,8},{10,11... | collective-permute-start | bytes 1152008 | tf_op jit(solution)/shard_map/ppermute | solution.py:489
  629.7 45.7 %collective-permute-start.77 = (bf16[128,960]{1,0:T(8,128)(2,1)S(1)}, bf16[128,960]{1,0:T(8,128)(2,1)S(1)}, u32[]{:S(2)}, u32[]{:S(2)}) collective-permute-start(bf16[128,960]{1,0:T(8,128)(2,1)S(1)} %broadcast_select_fusion.6), channel_id=1, source_target_pairs={{0,16},{16,0},{1,17},{17,1},{2,18},{18,2},{3,19},{19,3},{4,20},{20... | collective-permute-start | bytes 737288 | tf_op jit(solution)/shard_map/ppermute | solution.py:484
  (204 other events, 1631.2 us)
Sparse Core Ops, SparseCore 0:
  611.9 189.9 all-reduce.2

commit v2 on v1

--- a/solution.py
+++ b/solution.py
@@ -31,8 +31,8 @@
     return pltpu.CompilerParams(vmem_limit_bytes=mib * 1024 * 1024)
 
 
-def cost(flops, moved, special=0):
-    return pl.CostEstimate(flops=flops, bytes_accessed=moved, transcendentals=special)
+def cost(us):
+    return pl.CostEstimate(flops=int(us * 1.15e9), bytes_accessed=0, transcendentals=0)
 
 
 def dot_nn(a, b):
@@ -57,61 +57,86 @@
     return jnp.where(lane % HD < HD // 2, ahead, behind)
 
 
-def assemble_kernel(index_ref, *refs, shard_rows, step):
-    out_ref = refs[-1]
-    mine, other = refs[:-2], refs[-2]
-    wa, section = index_ref[0], index_ref[1]
-    rows = mine[0].shape[0]
-    for k, piece in enumerate(mine):
-        base = (wa ^ k) * shard_rows
-        start = pl.multiple_of(base + section * step, 16)
-        out_ref[pl.ds(start, rows), :] = piece[...]
-        start = pl.multiple_of(base + (1 - section) * step, 16)
-        out_ref[pl.ds(start, rows), :] = other[k]
-
-
-def assemble(index, mine, other, shard_rows, step):
-    width = mine[0].shape[1]
-    total = shard_rows * len(mine)
-    return pl.pallas_call(
-        functools.partial(assemble_kernel, shard_rows=shard_rows, step=step),
-        out_shape=jax.ShapeDtypeStruct((total, width), BF16),
-        in_specs=[SCALARS] + [WHOLE] * (len(mine) + 1),
+def join_kernel(*refs):
+    pieces, out_ref = refs[:-1], refs[-1]
+    rows = pieces[0].shape[0]
+    for k, piece in enumerate(pieces):
+        out_ref[k * rows : (k + 1) * rows, :] = piece[...]
+
+
+def join(pieces):
+    rows, width = pieces[0].shape
+    return pl.pallas_call(
+        join_kernel,
+        out_shape=jax.ShapeDtypeStruct((rows * len(pieces), width), pieces[0].dtype),
+        in_specs=[WHOLE] * len(pieces),
         out_specs=WHOLE,
         compiler_params=params(24),
-        cost_estimate=cost(0, total * width * 6),
+        cost_estimate=cost(1),
+        name="join",
+    )(*pieces)
+
+
+def assemble_kernel(index_ref, mine_ref, other_ref, out_ref, *, relative, rows, shard_rows, step):
+    wa, section = index_ref[0], index_ref[1]
+    count = out_ref.shape[0] // shard_rows
+    part = mine_ref.shape[0] // count
+    for k in range(count):
+        base = ((wa ^ k) if relative else k) * shard_rows
+        start = pl.multiple_of(base + section * step, 16)
+        out_ref[pl.ds(start, rows), :] = mine_ref[k * part : k * part + rows, :]
+        start = pl.multiple_of(base + (1 - section) * step, 16)
+        out_ref[pl.ds(start, rows), :] = other_ref[k * part : k * part + rows, :]
+
+
+def assemble(index, mine, other, count, relative, rows, shard_rows, step):
+    width = mine.shape[1]
+    total = shard_rows * count
+    return pl.pallas_call(
+        functools.partial(
+            assemble_kernel, relative=relative, rows=rows, shard_rows=shard_rows, step=step
+        ),
+        out_shape=jax.ShapeDtypeStruct((total, width), BF16),
+        in_specs=[SCALARS, WHOLE, WHOLE],
+        out_specs=WHOLE,
+        compiler_params=params(24),
+        cost_estimate=cost(2),
         name="assemble",
-    )(index, *mine, other)
-
-
-def pair_kernel(index_ref, *refs, shard_rows):
-    out_ref = refs[-1]
-    mine, other = refs[:-2], refs[-2]
+    )(index, mine, other)
+
+
+def pair_kernel(index_ref, mine_ref, other_ref, out_ref, *, shard_rows):
     wa, section = index_ref[0], index_ref[1]
-    rows, width = mine[0].shape
+    width = mine_ref.shape[1]
     left = pl.multiple_of(section * width, LANES)
     right = pl.multiple_of((1 - section) * width, LANES)
-    for k, piece in enumerate(mine):
-        start = pl.multiple_of((wa ^ k) * shard_rows, 16)
-        out_ref[pl.ds(start, rows), pl.ds(left, width)] = piece[...]
-        out_ref[pl.ds(start, rows), pl.ds(right, width)] = other[k]
-
-
-def assemble_pair(index, mine, other):
-    shard_rows, width = mine[0].shape
-    total = shard_rows * len(mine)
+    for k in range(out_ref.shape[0] // shard_rows):
+        rows = pl.ds(pl.multiple_of((wa ^ k) * shard_rows, 16), shard_rows)
+        piece = slice(k * shard_rows, (k + 1) * shard_rows)
+        out_ref[rows, pl.ds(left, width)] = mine_ref[piece, :]
+        out_ref[rows, pl.ds(right, width)] = other_ref[piece, :]
+
+
+def assemble_pair(index, mine, other, shard_rows):
+    total, width = mine.shape
     return pl.pallas_call(
         functools.partial(pair_kernel, shard_rows=shard_rows),
         out_shape=jax.ShapeDtypeStruct((total, 2 * width), BF16),
-        in_specs=[SCALARS] + [WHOLE] * (len(mine) + 1),
+        in_specs=[SCALARS, WHOLE, WHOLE],
         out_specs=WHOLE,
         compiler_params=params(24),
-        cost_estimate=cost(0, total * width * 8),
+        cost_estimate=cost(2.4),
         name="assemble_pair",
-    )(index, *mine, other)
-
-
-def project_kernel(u_ref, gain_ref, w_ref, cos_ref, sin_ref, normed_ref, q_ref, kv_ref, mixed_ref):
+    )(index, mine, other)
+
+
+def project_kernel(*refs, count):
+    terms, refs = refs[:count], refs[count:]
+    gain_ref, w_ref, cos_ref, sin_ref, u_ref, normed_ref, q_ref, kv_ref, mixed_ref = refs
+    u = terms[0][...].astype(F32)
+    for term in terms[1:]:
+        u = u + term[...].astype(F32)
+    u_ref[...] = u.astype(BF16)
     u = u_ref[...].astype(F32)
     scale = lax.rsqrt(jnp.mean(u * u, axis=-1, keepdims=True) + EPSILON)
     normed = (u * scale * gain_ref[...].astype(F32)).astype(BF16)
@@ -139,24 +164,26 @@
         kv_ref[:, g * LANES : (g + 1) * LANES] = both.astype(BF16)
 
 
-def project(u, gain, weight, cosine, sine):
-    rows, width = u.shape
+def project(terms, gain, weight, cosine, sine):
+    rows, width = terms[0].shape
+    count = len(terms)
     columns = weight.shape[1]
     padded = -(-columns // LANES) * LANES
     return pl.pallas_call(
-        project_kernel,
+        functools.partial(project_kernel, count=count),
         out_shape=(
+            jax.ShapeDtypeStruct((rows, width), BF16),
             jax.ShapeDtypeStruct((rows, width), BF16),
             jax.ShapeDtypeStruct((rows, H * LANES), BF16),
             jax.ShapeDtypeStruct((rows, KVH * LANES), BF16),
         ),
-        in_specs=[WHOLE] * 5,
-        out_specs=(WHOLE,) * 3,
+        in_specs=[WHOLE] * (count + 4),
+        out_specs=(WHOLE,) * 4,
         scratch_shapes=[pltpu.VMEM((rows, padded), F32)],
         compiler_params=params(24),
-        cost_estimate=cost(2 * rows * width * columns, width * columns * 2),
+        cost_estimate=cost(2),
         name="project",
-    )(u, gain, weight, cosine, sine)
+    )(*terms, gain, weight, cosine, sine)
 
 
 def stack_heads(ref):
@@ -205,7 +232,7 @@
         + [pl.BlockSpec((keys, LANES), lambda g: (0, g)) for _ in groups],
         out_specs=pl.BlockSpec((GROUP * rows, LANES), lambda g: (g, 0)),
         compiler_params=params(40),
-        cost_estimate=cost(pairs * 512, keys * len(groups) * KVH * 256, pairs),
+        cost_estimate=cost(9.6),
         name="attend",
     )(qpos, kpos, queries, *groups)
 
@@ -259,7 +286,7 @@
         + [kv_block for _ in groups],
         out_specs=(heads,) + tuple(kv_block for _ in groups),
         compiler_params=params(40),
-        cost_estimate=cost(pairs * 1280, keys * len(groups) * KVH * 512, pairs),
+        cost_estimate=cost(15.2),
         name="attend_back",
     )(qpos_row, kpos_column, queries, grads, saved, *groups)
     return result[0], result[1:]
@@ -292,47 +319,58 @@
         in_specs=[WHOLE] * 4,
         out_specs=(WHOLE,) * 3,
         compiler_params=params(24),
-        cost_estimate=cost(2 * rows * QW * width, QW * width * 2),
+        cost_estimate=cost(1.4),
         name="close_attention",
     )(u, saved, weight, gain)
 
 
-def mlp_kernel(*refs, count):
-    pieces, w_ref, down_ref = refs[:count], refs[count], refs[count + 1]
-    wide_ref, hidden_ref = refs[count + 2 : count + 4]
-    outs = refs[count + 4 :]
-    rows = pieces[0].shape[0]
+def widen_kernel(*refs, count):
+    pieces, w_ref, wide_ref, hidden_ref = refs[:count], *refs[count:]
     second = jnp.concatenate([piece[...] for piece in pieces], axis=0)
     wide = dot_nn(second, w_ref[...])
     wide_ref[...] = wide
     half = wide.shape[1] // 2
     gate, up = wide[:, :half], wide[:, half:]
-    hidden = (gate * jax.nn.sigmoid(gate) * up).astype(BF16)
-    hidden_ref[...] = hidden
-    partial = dot_nn(hidden, down_ref[...])
-    for k, out in enumerate(outs):
-        out[...] = partial[k * rows : (k + 1) * rows].astype(out.dtype)
-
-
-def mlp(pieces, weight, down):
+    hidden_ref[...] = (gate * jax.nn.sigmoid(gate) * up).astype(BF16)
+
+
+def widen(pieces, weight):
     count = len(pieces)
     rows, width = pieces[0].shape
     columns = weight.shape[1]
-    result = pl.pallas_call(
-        functools.partial(mlp_kernel, count=count),
+    return pl.pallas_call(
+        functools.partial(widen_kernel, count=count),
         out_shape=(
             jax.ShapeDtypeStruct((count * rows, columns), F32),
             jax.ShapeDtypeStruct((count * rows, columns // 2), BF16),
-            jax.ShapeDtypeStruct((rows, width), F32),
-        )
+        ),
+        in_specs=[WHOLE] * (count + 1),
+        out_specs=(WHOLE,) * 2,
+        compiler_params=params(40),
+        cost_estimate=cost(2.5),
+        name="widen",
+    )(*pieces, weight)
+
+
+def narrow_kernel(hidden_ref, down_ref, later_ref, *outs):
+    rows = outs[0].shape[0]
+    for k, out in enumerate(outs):
+        part = hidden_ref[k * rows : (k + 1) * rows, :]
+        out[...] = dot_nt(part, down_ref[...]).astype(out.dtype)
+
+
+def narrow(hidden, down, count, later):
+    rows, width = hidden.shape[0] // count, down.shape[0]
+    return pl.pallas_call(
+        narrow_kernel,
+        out_shape=(jax.ShapeDtypeStruct((rows, width), F32),)
         + tuple(jax.ShapeDtypeStruct((rows, width), BF16) for _ in range(count - 1)),
-        in_specs=[WHOLE] * (count + 2),
-        out_specs=(WHOLE,) * (count + 2),
-        compiler_params=params(40),
-        cost_estimate=cost(3 * count * rows * width * columns, width * columns * 8),
-        name="mlp",
-    )(*pieces, weight, down)
-    return result[0], result[1], result[2:]
+        in_specs=[WHOLE, WHOLE, pl.BlockSpec(memory_space=pl.ANY)],
+        out_specs=(WHOLE,) * count,
+        compiler_params=params(24),
+        cost_estimate=cost(1.7),
+        name="narrow",
+    )(hidden, down, later)
 
 
 def mlp_back_kernel(*refs, count):
@@ -340,7 +378,7 @@
     grads_ref, outs = refs[count + 3], refs[count + 4 :]
     rows = pieces[0].shape[0]
     grad_y = jnp.concatenate([piece[...] for piece in pieces], axis=0)
-    grad_hidden = dot_nt(grad_y, down_ref[...])
+    grad_hidden = dot_nn(grad_y, down_ref[...])
     half = wide_ref.shape[1] // 2
     gate, up = wide_ref[:, :half], wide_ref[:, half:]
     sig = jax.nn.sigmoid(gate)
@@ -365,7 +403,7 @@
         in_specs=[WHOLE] * (count + 3),
         out_specs=(WHOLE,) * (count + 1),
         compiler_params=params(40),
-        cost_estimate=cost(3 * count * rows * width * columns, width * columns * 8),
+        cost_estimate=cost(4),
         name="mlp_back",
     )(*pieces, wide, weight, down)
     return result[0], result[1:]
@@ -415,14 +453,48 @@
         out_specs=(WHOLE,) * 4,
         scratch_shapes=[pltpu.VMEM((rows, (H + 1) // 2 * LANES), F32)],
         compiler_params=params(24),
-        cost_estimate=cost(2 * rows * QW * width, QW * width * 2),
+        cost_estimate=cost(2),
         name="open_back",
     )(*terms, middle, gain, grad_y, weight)
 
 
-def project_back_kernel(*refs, count):
+def turned_back(block, cosine, sine, lane):
+    return block * cosine - swap_halves(block, lane) * sine
+
+
+def query_back_kernel(dq_ref, cos_ref, sin_ref, w_ref, mixed_ref, part_ref):
+    cosine, sine = cos_ref[...], sin_ref[...]
+    lane = lane_of(cosine.shape)
+
+    def head(h):
+        return turned_back(dq_ref[:, h * LANES : (h + 1) * LANES], cosine, sine, lane)
+
+    for j in range(H // 2):
+        block = jnp.where(lane < HD, head(2 * j), pltpu.roll(head(2 * j + 1), HD, 1))
+        mixed_ref[:, j * LANES : (j + 1) * LANES] = block.astype(BF16)
+    mixed_ref[:, (H - 1) * HD : QW] = head(H - 1)[:, :HD].astype(BF16)
+    part_ref[...] = dot_nt(mixed_ref[...], w_ref[:, :QW])
+
+
+def query_back(dq, cosine, sine, weight):
+    rows, width = dq.shape[0], weight.shape[0]
+    return pl.pallas_call(
+        query_back_kernel,
+        out_shape=(
+            jax.ShapeDtypeStruct((rows, QW), BF16),
+            jax.ShapeDtypeStruct((rows, width), F32),
+        ),
+        in_specs=[WHOLE] * 4,
+        out_specs=(WHOLE,) * 2,
+        compiler_params=params(24),
+        cost_estimate=cost(1.2),
+        name="query_back",
+    )(dq, cosine, sine, weight)
+
+
+def key_back_kernel(*refs, count):
     terms = refs[:count]
-    dq_ref, cos_ref, sin_ref, w_ref, u_ref, gain_ref, middle_ref = refs[count : count + 7]
+    part_ref, cos_ref, sin_ref, w_ref, u_ref, gain_ref, middle_ref = refs[count : count + 7]
     mixed_ref, out_ref, gain_grad_ref, wide_ref = refs[count + 7 :]
     grad_kv = terms[0][...].astype(F32)
     for term in terms[1:]:
@@ -430,54 +502,71 @@
     cosine, sine = cos_ref[...], sin_ref[...]
     lane = lane_of(cosine.shape)
     low = lane < HD
-
-    def turned(block):
-        return block * cosine - swap_halves(block, lane) * sine
+    blocks = [grad_kv[:, g * LANES : (g + 1) * LANES] for g in range(KVH)]
+    keys = [turned_back(block, cosine, sine, lane) for block in blocks]
 
     def unit(h, high):
-        if h < H:
-            block, at_high = turned(dq_ref[:, h * LANES : (h + 1) * LANES]), False
-        elif h < H + KVH:
-            g = h - H
-            block, at_high = turned(grad_kv[:, g * LANES : (g + 1) * LANES]), False
-        else:
-            g = h - H - KVH
-            block, at_high = grad_kv[:, g * LANES : (g + 1) * LANES], True
+        block, at_high = (keys[h], False) if h < KVH else (blocks[h - KVH], True)
         return block if at_high == high else pltpu.roll(block, HD, 1)
 
-    units = H + 2 * KVH
-    for j in range((units + 1) // 2):
-        block = unit(2 * j, False)
-        if 2 * j + 1 < units:
-            block = jnp.where(low, block, unit(2 * j + 1, True))
+    for j in range(KVH):
+        block = jnp.where(low, unit(2 * j, False), unit(2 * j + 1, True))
+        mixed_ref[:, j * LANES : (j + 1) * LANES] = block.astype(BF16)
+    for j in range(KVH + 1):
+        left = unit(2 * j - 1, False) if j else jnp.zeros(cosine.shape, F32)
+        block = jnp.where(low, left, unit(2 * j, True)) if j < KVH else left
         wide_ref[:, j * LANES : (j + 1) * LANES] = block.astype(BF16)
-    grad_mixed = wide_ref[:, : w_ref.shape[1]]
-    mixed_ref[...] = grad_mixed
-    gradient = dot_nt(grad_mixed, w_ref[...])
+    begin = QW // LANES * LANES
+    columns = w_ref.shape[1] - begin
+    gradient = part_ref[...] + dot_nt(wide_ref[:, :columns], w_ref[:, begin:])
     gain_grad, through = norm_back(u_ref[...].astype(F32), gain_ref[...], gradient)
     gain_grad_ref[...] = gain_grad
     out_ref[...] = (middle_ref[...] + through).astype(BF16)
 
 
-def project_back(terms, dq, cosine, sine, weight, u, gain, grad_middle):
+def key_back(terms, part, cosine, sine, weight, u, gain, grad_middle):
     rows, width = u.shape
-    columns = weight.shape[1]
-    padded = -(-columns // LANES) * LANES
     count = len(terms)
     return pl.pallas_call(
-        functools.partial(project_back_kernel, count=count),
+        functools.partial(key_back_kernel, count=count),
         out_shape=(
-            jax.ShapeDtypeStruct((rows, columns), BF16),
+            jax.ShapeDtypeStruct((rows, 2 * KW), BF16),
             jax.ShapeDtypeStruct((rows, width), BF16),
             jax.ShapeDtypeStruct((1, width), F32),
         ),
         in_specs=[WHOLE] * (count + 7),
         out_specs=(WHOLE,) * 3,
-        scratch_shapes=[pltpu.VMEM((rows, padded), BF16)],
+        scratch_shapes=[pltpu.VMEM((rows, 2 * KW + LANES), BF16)],
         compiler_params=params(24),
-        cost_estimate=cost(2 * rows * width * columns, width * columns * 2),
-        name="project_back",
-    )(*terms, dq, cosine, sine, weight, u, gain, grad_middle)
+        cost_estimate=cost(2),
+        name="key_back",
+    )(*terms, part, cosine, sine, weight, u, gain, grad_middle)
+
+
+def finish_kernel(index_ref, mine_ref, other_ref, gate_ref, up_ref):
+    wa, first = index_ref[0], index_ref[1] == 0
+    rows = gate_ref.shape[0]
+    width = mine_ref.shape[1]
+    for k in range(mine_ref.shape[0] // rows):
+        columns = pl.ds(pl.multiple_of((wa ^ k) * width, LANES), width)
+        piece = slice(k * rows, (k + 1) * rows)
+        mine, other = mine_ref[piece, :].astype(F32), other_ref[piece, :].astype(F32)
+        gate_ref[:, columns] = jnp.where(first, mine, other)
+        up_ref[:, columns] = jnp.where(first, other, mine)
+
+
+def finish(index, mine, other, rows):
+    total, width = mine.shape
+    result = jax.ShapeDtypeStruct((rows, total // rows * width), F32)
+    return pl.pallas_call(
+        finish_kernel,
+        out_shape=(result, result),
+        in_specs=[SCALARS, WHOLE, WHOLE],
+        out_specs=(WHOLE, WHOLE),
+        compiler_params=params(24),
+        cost_estimate=cost(3.3),
+        name="finish",
+    )(index, mine, other)
 
 
 def to_sibling(value):
@@ -508,7 +597,7 @@
     pieces = [value]
     for k in range(1, count):
         pieces.append(lax.ppermute(value, "ctx", [(i, (i + k) % count) for i in range(count)]))
-    return jnp.concatenate(pieces, axis=0)
+    return join(pieces)
 
 
 def scatter_ctx(value):
@@ -526,6 +615,20 @@
 
 def at(value, index, size, dim):
     return lax.dynamic_slice_in_dim(value, index * size, size, dim)
+
+
+def tie(values, after):
+    values, after = tuple(values), tuple(after)
+    anywhere = pl.BlockSpec(memory_space=pl.ANY)
+    return pl.pallas_call(
+        lambda *refs: None,
+        out_shape=tuple(jax.ShapeDtypeStruct(value.shape, value.dtype) for value in values),
+        in_specs=[anywhere] * (len(values) + len(after)),
+        out_specs=(anywhere,) * len(values),
+        input_output_aliases={i: i for i in range(len(values))},
+        cost_estimate=cost(0),
+        name="tie",
+    )(*values, *after)
 
 
 def added(terms):
@@ -552,6 +655,7 @@
     shard_rows = w_qkv.shape[1]
     ff_part = w_down.shape[1]
     w_qkv, w_out, w_gate, w_up, w_down = (a[0] for a in (w_qkv, w_out, w_gate, w_up, w_down))
+    w_down = w_down.T
 
     in_block = jnp.arange(half_rows, dtype=jnp.int32)
     table = block_table.reshape(-1, 2)
@@ -571,136 +675,202 @@
     sines = jnp.sin(angles)
     sine = jnp.tile(jnp.concatenate([-sines, sines], axis=1), (1, LANES // HD))
 
-    part_rows = shard_rows // 2 + 8
-    part_step = shard_rows - part_rows
-
-    def halves(shard):
-        keep = lax.dynamic_slice_in_dim(shard, section * part_step, part_rows, 0)
-        other = to_sibling(lax.dynamic_slice_in_dim(shard, (1 - section) * part_step, part_rows, 0))
+    kept_rows = shard_rows // 2 + 8
+    step = shard_rows - kept_rows
+    own_gains = jnp.concatenate([attn_gain, mlp_gain], axis=0)
+    gain_rows = jnp.pad(own_gains, ((0, 14), (0, w_qkv.shape[1] - shard_rows)))
+
+    def halves(shard, extra=None):
+        def part(half):
+            rows = lax.dynamic_slice_in_dim(shard, half * step, kept_rows, 0)
+            return rows if extra is None else jnp.concatenate([rows, extra], axis=0)
+
+        keep, other = part(section), to_sibling(part(1 - section))
         return jnp.where(first, keep, other), jnp.where(first, other, keep)
 
-    def fetch_rows(part):
-        mine = gather_wa(part)
-        return assemble(index, mine, to_sibling(jnp.stack(mine)), shard_rows, part_step)
-
-    def fetch_columns(part):
-        mine = send_wa([at(part, wa ^ k, ff_part, 1) for k in peers])
-        return assemble_pair(index, mine, to_sibling(jnp.stack(mine)))
-
-    qkv_parts = halves(w_qkv)
+    def fetch_rows(part, after=()):
+        if after:
+            (part,) = tie((part,), after)
+        pieces = gather_wa(part)
+        mine = join(pieces)
+        other = to_sibling(mine)
+        whole = assemble(index, mine, other, wa_count, True, kept_rows, shard_rows, step)
+        return whole, mine, pieces[1:]
+
+    def gains_of(mine):
+        rows = mine.reshape(wa_count, -1, mine.shape[1])[:, kept_rows : kept_rows + 2, :shard_rows]
+        return rows[wa ^ jnp.arange(wa_count)].transpose(1, 0, 2).reshape(2, 1, width)
+
+    def fetch_columns(part, after):
+        pieces = send_wa(tie([at(part, wa ^ k, ff_part, 1) for k in peers], after))
+        mine = join(pieces)
+        return assemble_pair(index, mine, to_sibling(mine), shard_rows), pieces[1:]
+
+    qkv_parts = halves(w_qkv, gain_rows)
+    qkv, mine, pieces = fetch_rows(qkv_parts[0])
     out_parts = halves(w_out)
     crossing = to_sibling(jnp.where(first, w_up, w_gate))
     wide_parts = (jnp.where(first, w_gate, crossing), jnp.where(first, crossing, w_up))
     down_other = to_sibling(w_down)
     downs = (jnp.where(first, w_down, down_other), jnp.where(first, down_other, w_down))
-    gains = jnp.concatenate([attn_gain, mlp_gain], axis=0)
-    gains = lax.all_gather(gains, ("section", "wa"), axis=0, tiled=False)
-    gains = gains.reshape(layers, wa_count, 2, -1).transpose(0, 2, 1, 3).reshape(layers, 2, 1, -1)
-
-    qkvs, outs, wides = [], [], []
+    gains = [gains_of(mine)]
+    out, _, pieces = fetch_rows(out_parts[0], pieces)
+    qkv_last, mine, pieces = fetch_rows(qkv_parts[1], pieces)
+    gains.append(gains_of(mine))
+    qkvs, outs, wides = [qkv, qkv_last], [out], []
+
+    terms = [lax.dynamic_index_in_dim(block_input, section, 0, keepdims=False)]
+    cotangent = lax.dynamic_index_in_dim(out_cotangent, section, 0, keepdims=False)
+    records, inputs = [], []
     for layer in range(layers):
-        qkvs.append(fetch_rows(qkv_parts[layer]))
-        outs.append(fetch_rows(out_parts[layer]))
-        wides.append(fetch_columns(wide_parts[layer]))
-
-    u = lax.dynamic_index_in_dim(block_input, section, 0, keepdims=False)
-    cotangent = lax.dynamic_index_in_dim(out_cotangent, section, 0, keepdims=False)
-    records, results = [], []
-    for layer in range(layers):
-        normed, queries, kv = project(u, gains[layer, 0], qkvs[layer], cosine, sine)
-        groups = gather_wa(gather_ctx(kv))
+        u, normed, queries, kv = project(terms, gains[layer][0], qkvs[layer], cosine, sine)
+        if layer:
+            out, _, pieces = fetch_rows(out_parts[layer], terms[1:])
+            outs.append(out)
+            (grad_y,) = tie((cotangent,), pieces)
+            grad_ys = gather_wa(grad_y)
+            pieces = grad_ys[1:]
+        (group,) = tie((gather_ctx(kv),), pieces)
+        groups = gather_wa(group)
+        weight, pieces = fetch_columns(wide_parts[layer], groups[1:])
+        wides.append(weight)
         saved = attend(qpos_column, key_pos, queries, groups)
-        low, middle, second = close_attention(u, saved, outs[layer], gains[layer, 1])
-        seconds = gather_wa(second)
-        wide, hidden, partial = mlp(seconds, wides[layer], downs[layer])
-        terms = send_wa(partial)
-        result = (middle + added(terms)).astype(BF16)
+        low, middle, second = close_attention(u, saved, outs[layer], gains[layer][1])
+        seconds = gather_wa(*tie((second,), pieces))
+        wide, hidden = widen(seconds, wides[layer])
+        if layer < layers - 1:
+            partial = narrow(hidden, downs[layer], wa_count, index)
+            terms = [middle] + send_wa(partial)
+        inputs.append(u)
         records.append((u, normed, queries, groups, saved, low, middle, seconds, wide, hidden))
-        results.append(result)
-        u = result
-
-    gain_grads, input_grads, weight_grads = [None] * layers, [None] * layers, [None] * layers
-    grad_y = cotangent
+
+    def over_cores(value, size, dim):
+        keep = at(value, section, size, dim)
+        other = to_sibling(at(value, 1 - section, size, dim))
+        return (keep.astype(F32) + other.astype(F32)).astype(BF16)
+
+    def blocked(value):
+        return value.reshape(wa_count, 2, shard_rows // 2, value.shape[1])
+
+    def rows_over_wa(blocks, after):
+        half = over_cores(blocks, 1, 1)[:, 0]
+        pieces = send_wa(tie([at(half, wa ^ k, 1, 0)[0] for k in peers], after))
+        return added(pieces).astype(BF16), pieces[1:]
+
+    def over_ctx(values, after):
+        return lax.psum(tie(values, after) if after else tuple(values), "ctx")
+
+    input_grads, gain_grads = [None] * layers, []
+    sums, pending = {}, ()
+    done = ()
     for layer in reversed(range(layers)):
         u, normed, queries, groups, saved, low, middle, seconds, wide, hidden = records[layer]
-        grad_ys = gather_wa(grad_y)
+        if layer < layers - 1:
+            (grad_y,) = tie((grad_y,), square_pieces)
+            grad_ys = gather_wa(grad_y)
         grad_wide, partial = mlp_back(grad_ys, wide, wides[layer], downs[layer])
+        if layer < layers - 1:
+            partial = tie(partial, (sums["wide", layer + 1],))
         terms = send_wa(partial)
         grad_middle, grad_low, grad_heads, gain_two_grad = open_back(
-            terms, middle, gains[layer, 1], grad_y, outs[layer]
+            terms, middle, gains[layer][1], grad_y, outs[layer]
         )
+
+        wide_grad = dot_tn(jnp.concatenate(seconds, axis=0), grad_wide).astype(BF16)
+        down_grad = dot_tn(jnp.concatenate(grad_ys, axis=0), hidden).astype(BF16)
+        wide_half = over_cores(wide_grad, ff_part, 1)
+        down_half = over_cores(down_grad, width // 2, 0)
+        pieces = [at(wide_half, wa ^ k, shard_rows, 0) for k in peers]
+        pieces = send_wa(tie(pieces, (grad_heads,)))
+        wide_rows = join(pieces)
+        wide_pieces = pieces[1:]
+        if pending:
+            key_half, key_pieces = rows_over_wa(pending[0], (grad_heads,))
+            wide_pieces = wide_pieces + key_pieces
+
         dq, dkv = attend_back(qpos_row, key_pos_column, queries, grad_heads, saved, groups)
-        gathered = added(send_wa(list(dkv))).astype(BF16)
+        dkv = send_wa(tie(dkv, wide_pieces))
+        gathered = added(dkv).astype(BF16)
+        if layer == layers - 1:
+            done = over_ctx((wide_rows,), done)
+            sums["wide", layer] = done[0]
+        else:
+            (gathered,) = tie((gathered,), (sums["square", layer + 1],))
+            done = over_ctx((wide_rows, down_half, key_half), done)
+            sums["wide", layer], sums["down", layer], sums["key", layer + 1] = done
+
         terms = scatter_ctx(gathered)
-        grad_mixed, grad_u, gain_one_grad = project_back(
-            terms, dq, cosine, sine, qkvs[layer], u, gains[layer, 0], grad_middle
+        grad_query, part = query_back(dq, cosine, sine, qkvs[layer])
+        out_grad = dot_tn(low, grad_low).astype(BF16)
+        query_grad = dot_tn(normed, grad_query).astype(BF16)
+        square_grad = jnp.concatenate([blocked(out_grad), blocked(query_grad)], axis=2)
+        square_half, square_pieces = rows_over_wa(square_grad, dkv[1:])
+        if layer == layers - 1:
+            done = over_ctx((down_half, square_half), done)
+            sums["down", layer], sums["square", layer] = done
+        else:
+            done = over_ctx((square_half,), done)
+            sums["square", layer] = done[0]
+
+        grad_key, grad_u, gain_one_grad = key_back(
+            terms, part, cosine, sine, qkvs[layer], u, gains[layer][0], grad_middle
         )
-        gain_grads[layer] = (gain_one_grad, gain_two_grad)
+        key_grad = blocked(dot_tn(normed, grad_key).astype(BF16))
+        pending = (key_grad,)
+        gain_grads = [gain_one_grad, gain_two_grad] + gain_grads
         input_grads[layer] = grad_u
-
-        all_seconds = jnp.concatenate(seconds, axis=0)
-        all_grads = jnp.concatenate(grad_ys, axis=0)
-        wide_grad = dot_tn(all_seconds, grad_wide).astype(BF16)
-        down_grad = dot_tn(hidden, all_grads).astype(BF16)
-        out_grad = dot_tn(low, grad_low).astype(BF16)
-        qkv_grad = dot_tn(normed, grad_mixed).astype(BF16)
-
-        def over_cores(value, size, dim):
-            keep = at(value, section, size, dim)
-            other = to_sibling(at(value, 1 - section, size, dim))
-            return (keep.astype(F32) + other.astype(F32)).astype(BF16)
-
-        wide_half = over_cores(wide_grad, ff_part, 1)
-        pieces = send_wa([at(wide_half, wa ^ k, shard_rows, 0) for k in peers])
-        wide_rows = jnp.zeros((shard_rows, wa_count * ff_part), BF16)
-        for k in peers:
-            wide_rows = lax.dynamic_update_slice_in_dim(
-                wide_rows, pieces[k], (wa ^ k) * ff_part, 1
-            )
-        down_half = over_cores(down_grad, ff_part // 2, 0)
-
-        def rows_over_wa(value):
-            columns = value.shape[1]
-            blocks = value.reshape(wa_count, 2, shard_rows // 2, columns)
-            half = over_cores(blocks, 1, 1)[:, 0]
-            pieces = send_wa([at(half, wa ^ k, 1, 0)[0] for k in peers])
-            return added(pieces).astype(BF16)
-
-        out_half = rows_over_wa(out_grad)
-        qkv_half = rows_over_wa(qkv_grad)
-        wide_rows, down_half = lax.psum((wide_rows, down_half), "ctx")
-        out_half, qkv_half = lax.psum((out_half, qkv_half), "ctx")
-        weight_grads[layer] = (wide_rows, down_half, out_half, qkv_half)
         grad_y = grad_u
 
+    tails = jnp.concatenate(gain_grads, axis=0).reshape(-1, wa_count, 1, shard_rows)
+    tails = jnp.broadcast_to(
+        tails.transpose(1, 2, 0, 3).astype(BF16), (wa_count, 2, 2 * layers, shard_rows)
+    )
+    tails = jnp.pad(tails, ((0, 0), (0, 0), (0, 4), (0, 2 * KW - shard_rows)))
+    packed, pieces = rows_over_wa(jnp.concatenate([key_grad, tails], axis=2), square_pieces)
+    if rotates(ctx_count):
+        key_half = added(jnp.split(gather_ctx(packed), ctx_count, axis=0))
+    else:
+        key_half = lax.psum(packed, "ctx").astype(F32)
+    gain_sums = key_half[shard_rows // 2 : shard_rows // 2 + 2 * layers, :shard_rows]
+    sums["key", 0] = key_half[: shard_rows // 2].astype(BF16)
+
+    hidden, middle = records[-1][-1], records[-1][6]
+    partial = narrow(hidden, downs[-1], wa_count, pieces[-1])
+    last_result = added([middle] + send_wa(partial)).astype(BF16)
+
+    def swapped(values):
+        mine = jnp.where(first, values[0], values[1])
+        return mine, to_sibling(jnp.where(first, values[1], values[0]))
+
     def by_layer(values):
-        mine = jnp.where(first, values[0], values[1])
-        other = to_sibling(jnp.where(first, values[1], values[0]))
+        mine, other = swapped(values)
         return jnp.where(first, mine, other), jnp.where(first, other, mine)
 
     def both(values):
         return jnp.stack(by_layer(values))[None]
 
-    def joined(position):
-        parts = by_layer([weight_grads[layer][position] for layer in range(layers)])
-        return jnp.concatenate(parts, axis=0).astype(F32)[None]
-
-    gate_grad, up_grad = by_layer([weight_grads[layer][0] for layer in range(layers)])
-    gain_sums = lax.psum(
-        jnp.concatenate([jnp.concatenate(pair, axis=0) for pair in gain_grads], axis=0),
-        ("section", "ctx", "wa"),
-    ).reshape(layers, 2, width)
-    own_gains = at(lax.dynamic_index_in_dim(gain_sums, section, 0), wa, shard_rows, 2)
+    def halves_of(name):
+        return [sums[name, layer] for layer in range(layers)]
+
+    down_halves, square_halves, key_halves = (
+        by_layer(halves_of(name)) for name in ("down", "square", "key")
+    )
+    gate_sum, up_sum = finish(index, *swapped(halves_of("wide")), shard_rows)
+    half = shard_rows // 2
+    out_sum = jnp.concatenate([part[:half] for part in square_halves], axis=0)
+    query_sum = jnp.concatenate([part[half:] for part in square_halves], axis=0)
+    qkv_sum = jnp.concatenate([query_sum, jnp.concatenate(key_halves, axis=0)], axis=1)
+    gain_own = lax.dynamic_index_in_dim(gain_sums.reshape(layers, 2, shard_rows), section, 0)
     return (
-        both(results),
+        both([inputs[1], last_result]),
         both(input_grads),
-        own_gains[:, 0],
-        joined(3),
-        joined(2),
-        own_gains[:, 1],
-        gate_grad.astype(F32)[None],
-        up_grad.astype(F32)[None],
-        joined(1),
+        gain_own[:, 0],
+        qkv_sum.astype(F32)[None],
+        out_sum.astype(F32)[None],
+        gain_own[:, 1],
+        gate_sum[None],
+        up_sum[None],
+        jnp.concatenate(down_halves, axis=0).astype(F32).T[None],
     )
 
 

time: 838 us -> 722 us (0.86)
  blocking collectives: 63.5 us -> 0 us
  waiting for transfers between devices: 310 us -> 271 us
  other arithmetic: 71.3 us -> 57 us
    psum x1 -> x4, waiting for transfers between devices: 125 us -> 40.5 us  [over_ctx(): return lax.psum(tie(values, after) if after else tuple(values), 'ctx')]
    psum x1 -> x0, blocking collectives: 43.5 us -> none  [per_device(): lax.psum(jnp.concatenate([jnp.concatenate(pair, axis=0) for pair in gain_...]
    ppermute x72, waiting for transfers between devices: 147 us -> 186 us  [to_peer(): return lax.ppermute(value, 'wa', [(i, i ^ k) for i in range(count)])]
    unnamed x327 -> x501, local copies, waits for them, and re-layouts: 54 us -> 83.5 us
    all_gather x1 -> x0, blocking collectives: 20 us -> none  [per_device(): gains = lax.all_gather(gains, ('section', 'wa'), axis=0, tiled=False)]
    ppermute x8 -> x2, local copies, waits for them, and re-layouts: 20.7 us -> 4.5 us  [to_sibling(): return lax.ppermute(value, 'section', [(0, 1), (1, 0)])]
    pallas_call x10 -> x50, Pallas kernels: 20.5 us -> 35.2 us  [the longest x11 10 us: join(): pl.pallas_call(join_kernel, out_shape=jax.ShapeDtypeStruct((rows * len(pi...]
    another operation x6 -> x0, local copies, waits for them, and re-layouts: 12.9 us -> none  [the longest x4 11.7 us: fetch_rows(): jnp.stack(mine)]
  transfers between devices with their start and end apart: 109 -> 115, of which waited for: 36 -> 46; matrix products, arithmetic and copies ran while one was open for 20% -> 16% of each run, Pallas kernels for 10% -> 12%
where the time goes in v2:
time: 722 us; the launch traced here: 715 us
  waiting for transfers between devices  271 us (38%)
  starting transfers between devices  134 us (19%)
  local copies, waits for them, and re-layouts  125 us (17%)
  Pallas kernels  97.4 us (13%)
  other arithmetic  57 us (8%)
  between operations  16.7 us (2%)
  matrix products  13.4 us (2%)
    ppermute x72, waiting for transfers between devices, to_peer(): return lax.ppermute(value, 'wa', [(i, i ^ k) for i in range(count)])  186 us
    unnamed x501, local copies, waits for them, and re-layouts  83.5 us
    ppermute x72, starting transfers between devices, to_peer(): return lax.ppermute(value, 'wa', [(i, i ^ k) for i in range(count)])  66 us
    ppermute x24, starting transfers between devices, to_sibling(): return lax.ppermute(value, 'section', [(0, 1), (1, 0)])  43.7 us
    psum x4, waiting for transfers between devices, over_ctx(): return lax.psum(tie(values, after) if after else tuple(values), 'ctx')  40.5 us
    pallas_call x2, Pallas kernels, attend_back(): pl.pallas_call(attend_back_kernel, out_shape=(jax.ShapeDtypeStruct((rows,...  29.5 us
    ppermute x9, waiting for transfers between devices, gather_ctx(): lax.ppermute(value, 'ctx', [(i, (i + k) % count) for i in range(count)])  23.5 us
    ppermute x6, waiting for transfers between devices, scatter_ctx(): lax.ppermute(piece, 'ctx', [(i, (i - k) % count) for i in range(count)])  21.4 us
  transfers between devices with their start and end apart: 115, of which 46 were waited for; matrix products, arithmetic and copies ran while one was open for 16% of the time, Pallas kernels for 12%

profile of v2, /device:TPU:1, one launch (start us, length us, event | category | flops | bytes accessed | tf_op | source)
XLA Modules:
  0.0 715.1 jit_solution(5101795022569632917)
XLA Ops:
  15.7 2.7 collective-permute-start.1
  21.4 8.4 %collective-permute-done.1.refs_1_ = bf16[144,1600]{1,0:T(8,128)(2,1)S(1)} collective-permute-done((bf16[144,1600]{1,0:T(8,128)(2,1)S(1)}, bf16[144,1600]{1,0:T(8,128)(2,1)S(1)}, u32[]{:S(2)}, u32[]{:S(2)}) %collective-permute-start.1) | collective-permute-done | bytes 460832 | tf_op jit(solution)/shard_map/ppermute | solution.py:578
  29.7 10.1 %collective-permute-done.2.refs_2_ = bf16[144,1600]{1,0:T(8,128)(2,1)S(1)} collective-permute-done((bf16[144,1600]{1,0:T(8,128)(2,1)S(1)}, bf16[144,1600]{1,0:T(8,128)(2,1)S(1)}, u32[]{:S(2)}, u32[]{:S(2)}) %collective-permute-start.2) | collective-permute-done | bytes 460832 | tf_op jit(solution)/shard_map/ppermute | solution.py:578
  52.2 2.4 assemble.4.refs_2_.w_ref.refs_7_
  59.8 2.3 collective-permute-start.6
  67.2 6.3 collective-permute-done.6.refs_2_
  75.3 4.4 collective-permute-done.7.refs_3_
  91.3 3.3 bitcast_select_fusion
  95.6 9.2 %collective-permute-done.15.refs_1_.refs_4_ = bf16[512,640]{1,0:T(8,128)(2,1)S(1)} collective-permute-done((bf16[512,640]{1,0:T(8,128)(2,1)}, bf16[512,640]{1,0:T(8,128)(2,1)S(1)}, u32[]{:S(2)}, u32[]{:S(2)}) %collective-permute-start.15) | collective-permute-done | bytes 655392 | tf_op jit(solution)/shard_map/ppermute | solution.py:578
  104.8 15.0 %collective-permute-done.17.refs_3_.refs_6_ = bf16[512,640]{1,0:T(8,128)(2,1)S(1)} collective-permute-done((bf16[512,640]{1,0:T(8,128)(2,1)}, bf16[512,640]{1,0:T(8,128)(2,1)S(1)}, u32[]{:S(2)}, u32[]{:S(2)}) %collective-permute-start.17) | collective-permute-done | bytes 655392 | tf_op jit(solution)/shard_map/ppermute | solution.py:578
  136.9 2.7 collective-permute-start.26
  140.4 8.9 %attend.2.saved_ref.o_ref = f32[1920,128]{1,0:T(8,128)S(1)} custom-call(s32[128,1]{1,0:T(8,128)S(1)} %copy.165.qpos_ref, s32[4,512]{1,0:T(4,128)S(1)} %pad_add_fusion.kpos_ref, bf16[128,1920]{1,0:T(8,128)(2,1)S(1)} %copy-done.209, bf16[512,640]{1,0:T(8,128)(2,1)S(1)} %copy-done.48, bf16[512,640]{1,0:T(8,128)(2,1)S(1)} %copy-done.36, ...), custom_call_target="tpu_custom_call" | custom-call | flops 11040000000 | tf_op jit(solution)/shard_map/attend/pallas_call | solution.py:223
  157.0 2.3 collective-permute-done.23.refs_1_
  160.6 5.3 collective-permute-done.25.refs_3_
  174.4 2.4 assemble.6.refs_6_.w_ref.refs_7_
  178.5 2.8 collective-permute-done.30.refs_4_
  197.0 2.6 collective-permute-start.33
  209.1 4.2 collective-permute-done.39.refs_2_
  219.0 6.6 collective-permute-done.41.refs_1_.refs_4_
  227.4 13.5 %collective-permute-done.43.refs_3_.refs_6_ = bf16[512,640]{1,0:T(8,128)(2,1)} collective-permute-done((bf16[512,640]{1,0:T(8,128)(2,1)}, bf16[512,640]{1,0:T(8,128)(2,1)}, u32[]{:S(2)}, u32[]{:S(2)}) %collective-permute-start.43) | collective-permute-done | bytes 655392 | tf_op jit(solution)/shard_map/ppermute | solution.py:578
  251.0 9.3 %collective-permute-start.44 = (bf16[512,960]{0,1:T(8,128)(2,1)}, bf16[512,960]{0,1:T(8,128)(2,1)}, u32[]{:S(2)}, u32[]{:S(2)}) collective-permute-start(bf16[512,960]{0,1:T(8,128)(2,1)} %copy.172), channel_id=1, source_target_pairs={{0,16},{16,0},{1,17},{17,1},{2,18},{18,2},{3,19},{19,3},{4,20},{20... | collective-permute-start | bytes 2949128 | tf_op jit(solution)/shard_map/ppermute | solution.py:573
  260.4 2.4 join.18.mine_ref
  263.2 9.6 %attend.3.saved_ref.o_ref = f32[1920,128]{1,0:T(8,128)S(1)} custom-call(s32[128,1]{1,0:T(8,128)S(1)} %copy-done.128, s32[4,512]{1,0:T(4,128)S(1)} %copy-done.131, bf16[128,1920]{1,0:T(8,128)(2,1)S(1)} %copy-done.202, bf16[512,640]{1,0:T(8,128)(2,1)S(1)} %copy-done.33, bf16[512,640]{1,0:T(8,128)(2,1)} %collective-permute-done.41.refs_1_.refs_4_, ...), custom_call_target="tpu_custom_call" | custom-call | flops 11040000000 | tf_op jit(solution)/shard_map/attend/pallas_call | solution.py:223
  287.4 2.5 collective-permute-done.48.refs_1_
  290.9 6.3 collective-permute-done.50.refs_3_
  298.7 3.6 mlp_back.2
  311.5 2.7 collective-permute-done.54.refs_3_
  316.8 15.3 %attend_back.2 = (f32[128,1920]{1,0:T(8,128)S(1)}, bf16[512,640]{1,0:T(8,128)(2,1)S(1)}, bf16[512,640]{1,0:T(8,128)(2,1)S(1)}, bf16[512,640]{1,0:T(8,128)(2,1)S(1)}, bf16[512,640]{1,0:T(8,128)(2,1)S(1)}) custom-call(s32[1,128]{1,0:T(1,128)S(1)} %copy-done.162, s32[512,4]{1,0:T(8,128)S(1)} %bitcast.139, bf16[128,1920]{1,0:T(8,128)(2,1)S(1)} %copy-done.203, ...), custom_call_target="tpu_custom_call" | custom-call | flops 17479999488 | tf_op jit(solution)/shard_map/attend_back/pallas_call | solution.py:274
  336.9 2.6 collective-permute-start.65
  343.6 6.5 collective-permute-done.56.refs_4_.refs_1_
  351.1 6.6 collective-permute-done.58.refs_6_.refs_3_
  368.1 6.8 collective-permute-done.61.refs_6_
  374.9 15.5 %collective-permute-done.60.refs_5_ = bf16[512,640]{1,0:T(8,128)(2,1)} collective-permute-done((bf16[512,640]{1,0:T(8,128)(2,1)}, bf16[512,640]{1,0:T(8,128)(2,1)}, u32[]{:S(2)}, u32[]{:S(2)}) %collective-permute-start.60) | collective-permute-done | bytes 655392 | tf_op jit(solution)/shard_map/ppermute | solution.py:578
  398.8 2.5 add_convert_fusion.1
  405.4 7.6 %collective-permute-done.63.refs_2_ = bf16[128,640]{1,0:T(8,128)(2,1)S(1)} collective-permute-done((bf16[128,640]{1,0:T(8,128)(2,1)}, bf16[128,640]{1,0:T(8,128)(2,1)S(1)}, u32[]{:S(2)}, u32[]{:S(2)}) %collective-permute-start.63) | collective-permute-done | bytes 163872 | tf_op jit(solution)/shard_map/ppermute | solution.py:612
  424.3 2.5 collective-permute-start.79
  429.5 2.6 add_convert_fusion.11.refs_1_
  435.1 5.8 collective-permute-done.71.refs_3_
  444.4 3.5 mlp_back.3
  455.3 2.8 convolution_convert_fusion
  459.3 2.6 collective-permute-start.75
  481.4 14.2 %attend_back.3 = (f32[128,1920]{1,0:T(8,128)S(1)}, bf16[512,640]{1,0:T(8,128)(2,1)S(1)}, bf16[512,640]{1,0:T(8,128)(2,1)S(1)}, bf16[512,640]{1,0:T(8,128)(2,1)S(1)}, bf16[512,640]{1,0:T(8,128)(2,1)S(1)}) custom-call(s32[1,128]{1,0:T(1,128)S(1)} %copy-done.163, s32[512,4]{1,0:T(8,128)S(1)} %bitcast.140, bf16[128,1920]{1,0:T(8,128)(2,1)S(1)} %copy-done.210, ...), custom_call_target="tpu_custom_call" | custom-call | flops 17479999488 | tf_op jit(solution)/shard_map/attend_back/pallas_call | solution.py:274
  495.7 2.5 add_convert_fusion.2
  508.0 2.5 collective-permute-start.106
  510.5 3.6 collective-permute-done.78.refs_6_.refs_3_
  520.1 3.4 collective-permute-start.91
  525.3 4.4 collective-permute-done.85.refs_6_
  529.7 17.0 %collective-permute-done.84.refs_5_ = bf16[512,640]{1,0:T(8,128)(2,1)S(1)} collective-permute-done((bf16[512,640]{1,0:T(8,128)(2,1)}, bf16[512,640]{1,0:T(8,128)(2,1)S(1)}, u32[]{:S(2)}, u32[]{:S(2)}) %collective-permute-start.84) | collective-permute-done | bytes 655392 | tf_op jit(solution)/shard_map/ppermute | solution.py:578
  557.6 13.2 %collective-permute-done.88.refs_2_ = bf16[128,640]{1,0:T(8,128)(2,1)} collective-permute-done((bf16[128,640]{1,0:T(8,128)(2,1)}, bf16[128,640]{1,0:T(8,128)(2,1)}, u32[]{:S(2)}, u32[]{:S(2)}) %collective-permute-start.88) | collective-permute-done | bytes 163872 | tf_op jit(solution)/shard_map/ppermute | solution.py:612
  578.4 3.2 collective-permute-start.90
  581.8 2.5 add_convert_fusion
  585.6 2.6 collective-permute-start.94
  591.7 5.3 collective-permute-done.92.refs_4_
  597.0 10.5 %collective-permute-done.93.refs_5_ = bf16[240,960]{1,0:T(8,128)(2,1)} collective-permute-done((bf16[240,960]{1,0:T(8,128)(2,1)}, bf16[240,960]{1,0:T(8,128)(2,1)}, u32[]{:S(2)}, u32[]{:S(2)}) %collective-permute-start.93) | collective-permute-done | bytes 460832 | tf_op jit(solution)/shard_map/ppermute | solution.py:578
  610.3 2.4 add_convert_fusion.10.refs_0_
  613.3 3.6 collective-permute-done.102
  617.1 4.8 collective-permute-start.103
  621.8 2.3 collective-permute-start.104
  630.8 11.0 %collective-permute-done.104.refs_2_ = bf16[128,640]{1,0:T(8,128)(2,1)S(1)} collective-permute-done((bf16[128,640]{1,0:T(8,128)(2,1)S(1)}, bf16[128,640]{1,0:T(8,128)(2,1)S(1)}, u32[]{:S(2)}, u32[]{:S(2)}) %collective-permute-start.104) | collective-permute-done | bytes 163872 | tf_op jit(solution)/shard_map/ppermute | solution.py:599
  644.8 4.5 collective-permute-start.99
  649.3 7.6 %all-reduce.13.cloned.1.call-done = (bf16[120,640]{1,0:T(8,128)(2,1)}, bf16[960,640]{1,0:T(8,128)(2,1)}, bf16[480,640]{1,0:T(8,128)(2,1)}) async-done(((bf16[120,640]{1,0:T(8,128)(2,1)}, bf16[960,640]{1,0:T(8,128)(2,1)}, bf16[480,640]{1,0:T(8,128)(2,1)}), (bf16[120,640]{1,0:T(8,128)(2,1)}, bf16[960,640]{1,0:T(8,128)(2,1)}, bf16[480,640]{1,0:T(8,128)(2,1)})) %all-reduce.13.cloned.1.call-update) | async-done | bytes 1996816 | tf_op jit(solution)/shard_map/psum | solution.py:761
  659.3 2.6 broadcast_select_fusion
  665.7 31.5 %all-reduce.11.cloned.1.call-done = bf16[240,960]{1,0:T(8,128)(2,1)} async-done(((bf16[240,960]{1,0:T(8,128)(2,1)}), bf16[240,960]{1,0:T(8,128)(2,1)}) %all-reduce.11.cloned.1.call-update) | async-done | bytes 460816 | tf_op jit(solution)/shard_map/psum | solution.py:761
  704.7 3.3 finish.1
  (884 shorter events, 305.0 us)
Async XLA Ops:
  7.2 426.4 %all-reduce.9.cloned.1.call-start = ((), (), s32[]{:S(2)}) async-start(), calls=%async_computation | async-start | bytes 2457600 | tf_op jit(solution)/shard_map/psum | solution.py:761
  10.9 35.3 %collective-permute-start.8 = (bf16[128,960]{1,0:T(8,128)(2,1)}, bf16[128,960]{1,0:T(8,128)(2,1)}, u32[]{:S(2)}, u32[]{:S(2)}) collective-permute-start(bf16[128,960]{1,0:T(8,128)(2,1)} %dynamic-slice_bitcast_fusion.10), channel_id=1, source_target_pairs={{0,16},{16,0},{1,17},{17,1},{2,18},{18,2},{3,19},{19,3},{4,20},{20... | collective-permute-start | bytes 737288 | tf_op jit(solution)/shard_map/ppermute | solution.py:573
  12.6 77.6 %collective-permute-start.19 = (bf16[240,2560]{1,0:T(8,128)(2,1)}, bf16[240,2560]{1,0:T(8,128)(2,1)}, u32[]{:S(2)}, u32[]{:S(2)}) collective-permute-start(bf16[240,2560]{1,0:T(8,128)(2,1)} %bitcast_select_fusion.1), channel_id=1, source_target_pairs={{0,16},{16,0},{1,17},{17,1},{2,18},{18,2},{3,19},{19,3},{4,20},{20... | collective-permute-start | bytes 3686408 | tf_op jit(solution)/shard_map/ppermute | solution.py:573
  15.7 14.0 %collective-permute-start.1 = (bf16[144,1600]{1,0:T(8,128)(2,1)S(1)}, bf16[144,1600]{1,0:T(8,128)(2,1)S(1)}, u32[]{:S(2)}, u32[]{:S(2)}) collective-permute-start(bf16[144,1600]{1,0:T(8,128)(2,1)S(1)} %get-tuple-element.341.refs_0_), channel_id=1, source_target_pairs={{0,1},{1,0},{2,3},{3,2},{4,5},{5,4},{6,7},{7,6},{8,9},{9,8},{10,11... | collective-permute-start | bytes 1382408 | tf_op jit(solution)/shard_map/ppermute | solution.py:578
  18.4 21.4 %collective-permute-start.2 = (bf16[144,1600]{1,0:T(8,128)(2,1)S(1)}, bf16[144,1600]{1,0:T(8,128)(2,1)S(1)}, u32[]{:S(2)}, u32[]{:S(2)}) collective-permute-start(bf16[144,1600]{1,0:T(8,128)(2,1)S(1)} %get-tuple-element.341.refs_0_), channel_id=1, source_target_pairs={{0,2},{1,3},{2,0},{3,1},{4,6},{5,7},{6,4},{7,5},{8,10},{9,11},{10,... | collective-permute-start | bytes 1382408 | tf_op jit(solution)/shard_map/ppermute | solution.py:578
  19.6 21.4 %collective-permute-start.3 = (bf16[144,1600]{1,0:T(8,128)(2,1)S(1)}, bf16[144,1600]{1,0:T(8,128)(2,1)S(1)}, u32[]{:S(2)}, u32[]{:S(2)}) collective-permute-start(bf16[144,1600]{1,0:T(8,128)(2,1)S(1)} %get-tuple-element.341.refs_0_), channel_id=1, source_target_pairs={{0,3},{1,2},{2,1},{3,0},{4,7},{5,6},{6,5},{7,4},{8,11},{9,10},{10,... | collective-permute-start | bytes 1382408 | tf_op jit(solution)/shard_map/ppermute | solution.py:578
  59.8 13.7 %collective-permute-start.6 = (bf16[128,640]{1,0:T(8,128)(2,1)S(1)}, bf16[128,640]{1,0:T(8,128)(2,1)S(1)}, u32[]{:S(2)}, u32[]{:S(2)}) collective-permute-start(bf16[128,640]{1,0:T(8,128)(2,1)S(1)} %get-tuple-element.126.refs_0_), channel_id=1, source_target_pairs={{0,8},{4,12},{8,0},{12,4},{1,9},{5,13},{9,1},{13,5},{2,10},{6,14},... | collective-permute-start | bytes 491528 | tf_op jit(solution)/shard_map/ppermute | solution.py:599
  63.5 23.4 %collective-permute-start.12 = (bf16[144,1600]{1,0:T(8,128)(2,1)}, bf16[144,1600]{1,0:T(8,128)(2,1)S(1)}, u32[]{:S(2)}, u32[]{:S(2)}) collective-permute-start(bf16[144,1600]{1,0:T(8,128)(2,1)} %tie.25.refs_0_), channel_id=1, source_target_pairs={{0,1},{1,0},{2,3},{3,2},{4,5},{5,4},{6,7},{7,6},{8,9},{9,8},{10,11... | collective-permute-start | bytes 1382408 | tf_op jit(solution)/shard_map/ppermute | solution.py:578
  63.8 23.1 %collective-permute-start.13 = (bf16[144,1600]{1,0:T(8,128)(2,1)}, bf16[144,1600]{1,0:T(8,128)(2,1)S(1)}, u32[]{:S(2)}, u32[]{:S(2)}) collective-permute-start(bf16[144,1600]{1,0:T(8,128)(2,1)} %tie.25.refs_0_), channel_id=1, source_target_pairs={{0,2},{1,3},{2,0},{3,1},{4,6},{5,7},{6,4},{7,5},{8,10},{9,11},{10,... | collective-permute-start | bytes 1382408 | tf_op jit(solution)/shard_map/ppermute | solution.py:578
  66.0 20.9 %collective-permute-start.14 = (bf16[144,1600]{1,0:T(8,128)(2,1)}, bf16[144,1600]{1,0:T(8,128)(2,1)S(1)}, u32[]{:S(2)}, u32[]{:S(2)}) collective-permute-start(bf16[144,1600]{1,0:T(8,128)(2,1)} %tie.25.refs_0_), channel_id=1, source_target_pairs={{0,3},{1,2},{2,1},{3,0},{4,7},{5,6},{6,5},{7,4},{8,11},{9,10},{10,... | collective-permute-start | bytes 1382408 | tf_op jit(solution)/shard_map/ppermute | solution.py:578
  79.6 43.8 %collective-permute-start.27 = (bf16[960,640]{1,0:T(8,128)(2,1)}, bf16[960,640]{1,0:T(8,128)(2,1)}, u32[]{:S(2)}, u32[]{:S(2)}) collective-permute-start(bf16[960,640]{1,0:T(8,128)(2,1)} %bitcast.153), channel_id=1, source_target_pairs={{0,16},{16,0},{1,17},{17,1},{2,18},{18,2},{3,19},{19,3},{4,20},{20... | collective-permute-start | bytes 3686408 | tf_op jit(solution)/shard_map/ppermute | solution.py:573
  86.9 43.1 %collective-permute-start.18 = (bf16[512,960]{0,1:T(8,128)(2,1)}, bf16[512,960]{0,1:T(8,128)(2,1)}, u32[]{:S(2)}, u32[]{:S(2)}) collective-permute-start(bf16[512,960]{0,1:T(8,128)(2,1)} %copy.166), channel_id=1, source_target_pairs={{0,16},{16,0},{1,17},{17,1},{2,18},{18,2},{3,19},{19,3},{4,20},{20... | collective-permute-start | bytes 2949128 | tf_op jit(solution)/shard_map/ppermute | solution.py:573
  88.6 16.2 %collective-permute-start.15 = (bf16[512,640]{1,0:T(8,128)(2,1)}, bf16[512,640]{1,0:T(8,128)(2,1)S(1)}, u32[]{:S(2)}, u32[]{:S(2)}) collective-permute-start(bf16[512,640]{1,0:T(8,128)(2,1)} %tie.26.refs_0_), channel_id=1, source_target_pairs={{0,1},{1,0},{2,3},{3,2},{4,5},{5,4},{6,7},{7,6},{8,9},{9,8},{10,11... | collective-permute-start | bytes 1966088 | tf_op jit(solution)/shard_map/ppermute | solution.py:578
  89.5 15.3 %collective-permute-start.16 = (bf16[512,640]{1,0:T(8,128)(2,1)}, bf16[512,640]{1,0:T(8,128)(2,1)S(1)}, u32[]{:S(2)}, u32[]{:S(2)}) collective-permute-start(bf16[512,640]{1,0:T(8,128)(2,1)} %tie.26.refs_0_), channel_id=1, source_target_pairs={{0,2},{1,3},{2,0},{3,1},{4,6},{5,7},{6,4},{7,5},{8,10},{9,11},{10,... | collective-permute-start | bytes 1966088 | tf_op jit(solution)/shard_map/ppermute | solution.py:578
  90.1 29.7 %collective-permute-start.17 = (bf16[512,640]{1,0:T(8,128)(2,1)}, bf16[512,640]{1,0:T(8,128)(2,1)S(1)}, u32[]{:S(2)}, u32[]{:S(2)}) collective-permute-start(bf16[512,640]{1,0:T(8,128)(2,1)} %tie.26.refs_0_), channel_id=1, source_target_pairs={{0,3},{1,2},{2,1},{3,0},{4,7},{5,6},{6,5},{7,4},{8,11},{9,10},{10,... | collective-permute-start | bytes 1966088 | tf_op jit(solution)/shard_map/ppermute | solution.py:578
  126.7 47.6 %collective-permute-start.31 = (bf16[576,1600]{1,0:T(8,128)(2,1)}, bf16[576,1600]{1,0:T(8,128)(2,1)}, u32[]{:S(2)}, u32[]{:S(2)}) collective-permute-start(bf16[576,1600]{1,0:T(8,128)(2,1)} %join.15.mine_ref), channel_id=1, source_target_pairs={{0,16},{16,0},{1,17},{17,1},{2,18},{18,2},{3,19},{19,3},{4,20},{20... | collective-permute-start | bytes 5529608 | tf_op jit(solution)/shard_map/ppermute | solution.py:573
  136.9 18.2 %collective-permute-start.26 = (bf16[960,640]{1,0:T(8,128)(2,1)}, bf16[960,640]{1,0:T(8,128)(2,1)}, u32[]{:S(2)}, u32[]{:S(2)}) collective-permute-start(bf16[960,640]{1,0:T(8,128)(2,1)} %join.14.mine_ref), channel_id=1, source_target_pairs={{0,16},{16,0},{1,17},{17,1},{2,18},{18,2},{3,19},{19,3},{4,20},{20... | collective-permute-start | bytes 3686408 | tf_op jit(solution)/shard_map/ppermute | solution.py:573
  182.0 17.6 %collective-permute-start.35 = (bf16[128,960]{1,0:T(8,128)(2,1)}, bf16[128,960]{1,0:T(8,128)(2,1)S(1)}, u32[]{:S(2)}, u32[]{:S(2)}) collective-permute-start(bf16[128,960]{1,0:T(8,128)(2,1)} %tie.29.refs_0_), channel_id=1, source_target_pairs={{0,1},{1,0},{2,3},{3,2},{4,5},{5,4},{6,7},{7,6},{8,9},{9,8},{10,11... | collective-permute-start | bytes 737288 | tf_op jit(solution)/shard_map/ppermute | solution.py:578
  184.0 18.5 %collective-permute-start.36 = (bf16[128,960]{1,0:T(8,128)(2,1)}, bf16[128,960]{1,0:T(8,128)(2,1)S(1)}, u32[]{:S(2)}, u32[]{:S(2)}) collective-permute-start(bf16[128,960]{1,0:T(8,128)(2,1)} %tie.29.refs_0_), channel_id=1, source_target_pairs={{0,2},{1,3},{2,0},{3,1},{4,6},{5,7},{6,4},{7,5},{8,10},{9,11},{10,... | collective-permute-start | bytes 737288 | tf_op jit(solution)/shard_map/ppermute | solution.py:578
  184.3 18.2 %collective-permute-start.37 = (bf16[128,960]{1,0:T(8,128)(2,1)}, bf16[128,960]{1,0:T(8,128)(2,1)}, u32[]{:S(2)}, u32[]{:S(2)}) collective-permute-start(bf16[128,960]{1,0:T(8,128)(2,1)} %tie.29.refs_0_), channel_id=1, source_target_pairs={{0,3},{1,2},{2,1},{3,0},{4,7},{5,6},{6,5},{7,4},{8,11},{9,10},{10,... | collective-permute-start | bytes 737288 | tf_op jit(solution)/shard_map/ppermute | solution.py:578
  214.0 13.5 %collective-permute-start.42 = (bf16[512,640]{1,0:T(8,128)(2,1)}, bf16[512,640]{1,0:T(8,128)(2,1)}, u32[]{:S(2)}, u32[]{:S(2)}) collective-permute-start(bf16[512,640]{1,0:T(8,128)(2,1)} %tie.31.refs_0_), channel_id=1, source_target_pairs={{0,2},{1,3},{2,0},{3,1},{4,6},{5,7},{6,4},{7,5},{8,10},{9,11},{10,... | collective-permute-start | bytes 1966088 | tf_op jit(solution)/shard_map/ppermute | solution.py:578
  214.6 26.3 %collective-permute-start.43 = (bf16[512,640]{1,0:T(8,128)(2,1)}, bf16[512,640]{1,0:T(8,128)(2,1)}, u32[]{:S(2)}, u32[]{:S(2)}) collective-permute-start(bf16[512,640]{1,0:T(8,128)(2,1)} %tie.31.refs_0_), channel_id=1, source_target_pairs={{0,3},{1,2},{2,1},{3,0},{4,7},{5,6},{6,5},{7,4},{8,11},{9,10},{10,... | collective-permute-start | bytes 1966088 | tf_op jit(solution)/shard_map/ppermute | solution.py:578
  240.9 19.5 %collective-permute-start.45 = (bf16[240,640]{1,0:T(8,128)(2,1)}, bf16[240,640]{1,0:T(8,128)(2,1)}, u32[]{:S(2)}, u32[]{:S(2)}) collective-permute-start(bf16[240,640]{1,0:T(8,128)(2,1)} %get-tuple-element.143), channel_id=1, source_target_pairs={{0,1},{1,0},{2,3},{3,2},{4,5},{5,4},{6,7},{7,6},{8,9},{9,8},{10,11... | collective-permute-start | bytes 921608 | tf_op jit(solution)/shard_map/ppermute | solution.py:578
  240.9 19.5 %collective-permute-start.46 = (bf16[240,640]{1,0:T(8,128)(2,1)}, bf16[240,640]{1,0:T(8,128)(2,1)}, u32[]{:S(2)}, u32[]{:S(2)}) collective-permute-start(bf16[240,640]{1,0:T(8,128)(2,1)} %get-tuple-element.144), channel_id=1, source_target_pairs={{0,2},{1,3},{2,0},{3,1},{4,6},{5,7},{6,4},{7,5},{8,10},{9,11},{10,... | collective-permute-start | bytes 921608 | tf_op jit(solution)/shard_map/ppermute | solution.py:578
  242.7 17.7 %collective-permute-start.47 = (bf16[240,640]{1,0:T(8,128)(2,1)}, bf16[240,640]{1,0:T(8,128)(2,1)}, u32[]{:S(2)}, u32[]{:S(2)}) collective-permute-start(bf16[240,640]{1,0:T(8,128)(2,1)} %get-tuple-element.145), channel_id=1, source_target_pairs={{0,3},{1,2},{2,1},{3,0},{4,7},{5,6},{6,5},{7,4},{8,11},{9,10},{10,... | collective-permute-start | bytes 921608 | tf_op jit(solution)/shard_map/ppermute | solution.py:578
  251.0 22.7 %collective-permute-start.44 = (bf16[512,960]{0,1:T(8,128)(2,1)}, bf16[512,960]{0,1:T(8,128)(2,1)}, u32[]{:S(2)}, u32[]{:S(2)}) collective-permute-start(bf16[512,960]{0,1:T(8,128)(2,1)} %copy.172), channel_id=1, source_target_pairs={{0,16},{16,0},{1,17},{17,1},{2,18},{18,2},{3,19},{19,3},{4,20},{20... | collective-permute-start | bytes 2949128 | tf_op jit(solution)/shard_map/ppermute | solution.py:573
  262.8 22.0 %collective-permute-start.51 = (bf16[960,640]{1,0:T(8,128)(2,1)}, bf16[960,640]{1,0:T(8,128)(2,1)}, u32[]{:S(2)}, u32[]{:S(2)}) collective-permute-start(bf16[960,640]{1,0:T(8,128)(2,1)} %join.18.mine_ref), channel_id=1, source_target_pairs={{0,16},{16,0},{1,17},{17,1},{2,18},{18,2},{3,19},{19,3},{4,20},{20... | collective-permute-start | bytes 3686408 | tf_op jit(solution)/shard_map/ppermute | solution.py:573
  306.6 32.9 %collective-permute-start.55 = (bf16[960,640]{1,0:T(8,128)(2,1)S(1)}, bf16[960,640]{1,0:T(8,128)(2,1)S(1)}, u32[]{:S(2)}, u32[]{:S(2)}) collective-permute-start(bf16[960,640]{1,0:T(8,128)(2,1)S(1)} %constant_dynamic-slice_fusion.16), channel_id=1, source_target_pairs={{0,16},{16,0},{1,17},{17,1},{2,18},{18,2},{3,19},{19,3},{4,20},{20... | collective-permute-start | bytes 3686408 | tf_op jit(solution)/shard_map/ppermute | solution.py:573
  311.4 50.4 %collective-permute-start.86 = (bf16[480,640]{1,0:T(8,128)(2,1)}, bf16[480,640]{1,0:T(8,128)(2,1)}, u32[]{:S(2)}, u32[]{:S(2)}) collective-permute-start(bf16[480,640]{1,0:T(8,128)(2,1)} %constant_dynamic-slice_fusion.5), channel_id=1, source_target_pairs={{0,16},{16,0},{1,17},{17,1},{2,18},{18,2},{3,19},{19,3},{4,20},{20... | collective-permute-start | bytes 1843208 | tf_op jit(solution)/shard_map/ppermute | solution.py:573
  336.9 61.9 %collective-permute-start.65 = (bf16[4,1,240,960]{3,2,1,0:T(8,128)(2,1)}, bf16[4,1,240,960]{3,2,1,0:T(8,128)(2,1)}, u32[]{:S(2)}, u32[]{:S(2)}) collective-permute-start(bf16[4,1,240,960]{3,2,1,0:T(8,128)(2,1)} %fusion.3), channel_id=1, source_target_pairs={{0,16},{16,0},{1,17},{17,1},{2,18},{18,2},{3,19},{19,3},{4,20},{20... | collective-permute-start | bytes 5529608 | tf_op jit(solution)/shard_map/ppermute | solution.py:573
  342.4 15.4 %collective-permute-start.58 = (bf16[240,640]{1,0:T(8,128)(2,1)}, bf16[240,640]{1,0:T(8,128)(2,1)S(1)}, u32[]{:S(2)}, u32[]{:S(2)}) collective-permute-start(bf16[240,640]{1,0:T(8,128)(2,1)} %get-tuple-element.162), channel_id=1, source_target_pairs={{0,3},{1,2},{2,1},{3,0},{4,7},{5,6},{6,5},{7,4},{8,11},{9,10},{10,... | collective-permute-start | bytes 921608 | tf_op jit(solution)/shard_map/ppermute | solution.py:578
  358.5 16.5 %collective-permute-start.61 = (bf16[512,640]{1,0:T(8,128)(2,1)}, bf16[512,640]{1,0:T(8,128)(2,1)}, u32[]{:S(2)}, u32[]{:S(2)}) collective-permute-start(bf16[512,640]{1,0:T(8,128)(2,1)} %get-tuple-element.166), channel_id=1, source_target_pairs={{0,3},{1,2},{2,1},{3,0},{4,7},{5,6},{6,5},{7,4},{8,11},{9,10},{10,... | collective-permute-start | bytes 1966088 | tf_op jit(solution)/shard_map/ppermute | solution.py:578
  359.8 30.7 %collective-permute-start.60 = (bf16[512,640]{1,0:T(8,128)(2,1)}, bf16[512,640]{1,0:T(8,128)(2,1)}, u32[]{:S(2)}, u32[]{:S(2)}) collective-permute-start(bf16[512,640]{1,0:T(8,128)(2,1)} %get-tuple-element.165), channel_id=1, source_target_pairs={{0,2},{1,3},{2,0},{3,1},{4,6},{5,7},{6,4},{7,5},{8,10},{9,11},{10,... | collective-permute-start | bytes 1966088 | tf_op jit(solution)/shard_map/ppermute | solution.py:578
  359.8 30.7 %collective-permute-start.59 = (bf16[512,640]{1,0:T(8,128)(2,1)}, bf16[512,640]{1,0:T(8,128)(2,1)}, u32[]{:S(2)}, u32[]{:S(2)}) collective-permute-start(bf16[512,640]{1,0:T(8,128)(2,1)} %get-tuple-element.164), channel_id=1, source_target_pairs={{0,1},{1,0},{2,3},{3,2},{4,5},{5,4},{6,7},{7,6},{8,9},{9,8},{10,11... | collective-permute-start | bytes 1966088 | tf_op jit(solution)/shard_map/ppermute | solution.py:578
  368.1 180.9 %all-reduce.15.cloned.1.call-start = ((), (), s32[]{:S(2)}) async-start(), calls=%async_computation.3 | async-start | bytes 2211840 | tf_op jit(solution)/shard_map/psum | solution.py:761
  395.2 17.8 %collective-permute-start.63 = (bf16[128,640]{1,0:T(8,128)(2,1)}, bf16[128,640]{1,0:T(8,128)(2,1)S(1)}, u32[]{:S(2)}, u32[]{:S(2)}) collective-permute-start(bf16[128,640]{1,0:T(8,128)(2,1)} %get-tuple-element.359), channel_id=1, source_target_pairs={{0,8},{4,12},{8,0},{12,4},{1,9},{5,13},{9,1},{13,5},{2,10},{6,14},... | collective-permute-start | bytes 491528 | tf_op jit(solution)/shard_map/ppermute | solution.py:612
  397.4 16.3 %collective-permute-start.64 = (bf16[128,640]{1,0:T(8,128)(2,1)}, bf16[128,640]{1,0:T(8,128)(2,1)}, u32[]{:S(2)}, u32[]{:S(2)}) collective-permute-start(bf16[128,640]{1,0:T(8,128)(2,1)} %get-tuple-element.358), channel_id=1, source_target_pairs={{0,4},{4,8},{8,12},{12,0},{1,5},{5,9},{9,13},{13,1},{2,6},{6,10},{... | collective-permute-start | bytes 491528 | tf_op jit(solution)/shard_map/ppermute | solution.py:612
  402.7 24.1 %collective-permute-start.66 = (bf16[240,960]{1,0:T(8,128)(2,1)}, bf16[240,960]{1,0:T(8,128)(2,1)}, u32[]{:S(2)}, u32[]{:S(2)}) collective-permute-start(bf16[240,960]{1,0:T(8,128)(2,1)} %get-tuple-element.175), channel_id=1, source_target_pairs={{0,1},{1,0},{2,3},{3,2},{4,5},{5,4},{6,7},{7,6},{8,9},{9,8},{10,11... | collective-permute-start | bytes 1382408 | tf_op jit(solution)/shard_map/ppermute | solution.py:578
  404.2 22.6 %collective-permute-start.67 = (bf16[240,960]{1,0:T(8,128)(2,1)}, bf16[240,960]{1,0:T(8,128)(2,1)}, u32[]{:S(2)}, u32[]{:S(2)}) collective-permute-start(bf16[240,960]{1,0:T(8,128)(2,1)} %get-tuple-element.176), channel_id=1, source_target_pairs={{0,2},{1,3},{2,0},{3,1},{4,6},{5,7},{6,4},{7,5},{8,10},{9,11},{10,... | collective-permute-start | bytes 1382408 | tf_op jit(solution)/shard_map/ppermute | solution.py:578
  404.2 22.6 %collective-permute-start.68 = (bf16[240,960]{1,0:T(8,128)(2,1)}, bf16[240,960]{1,0:T(8,128)(2,1)}, u32[]{:S(2)}, u32[]{:S(2)}) collective-permute-start(bf16[240,960]{1,0:T(8,128)(2,1)} %get-tuple-element.177), channel_id=1, source_target_pairs={{0,3},{1,2},{2,1},{3,0},{4,7},{5,6},{6,5},{7,4},{8,11},{9,10},{10,... | collective-permute-start | bytes 1382408 | tf_op jit(solution)/shard_map/ppermute | solution.py:578
  424.3 40.6 %collective-permute-start.79 = (bf16[4,1,120,640]{3,2,1,0:T(8,128)(2,1)}, bf16[4,1,120,640]{3,2,1,0:T(8,128)(2,1)}, u32[]{:S(2)}, u32[]{:S(2)}) collective-permute-start(bf16[4,1,120,640]{3,2,1,0:T(8,128)(2,1)} %constant_dynamic-slice_fusion.6), channel_id=1, source_target_pairs={{0,16},{16,0},{1,17},{17,1},{2,18},{18,2},{3,19},{19,3},{4,20},{20... | collective-permute-start | bytes 1843208 | tf_op jit(solution)/shard_map/ppermute | solution.py:573
  433.6 223.3 %all-reduce.13.cloned.1.call-start = ((), (), s32[]{:S(2)}) async-start(), calls=%async_computation.2 | async-start | bytes 3993600 | tf_op jit(solution)/shard_map/psum | solution.py:761
  452.6 15.0 %collective-permute-start.72 = (bf16[128,960]{1,0:T(8,128)(2,1)}, bf16[128,960]{1,0:T(8,128)(2,1)S(1)}, u32[]{:S(2)}, u32[]{:S(2)}) collective-permute-start(bf16[128,960]{1,0:T(8,128)(2,1)} %get-tuple-element.185), channel_id=1, source_target_pairs={{0,1},{1,0},{2,3},{3,2},{4,5},{5,4},{6,7},{7,6},{8,9},{9,8},{10,11... | collective-permute-start | bytes 737288 | tf_op jit(solution)/shard_map/ppermute | solution.py:578
  453.2 14.5 %collective-permute-start.73 = (bf16[128,960]{1,0:T(8,128)(2,1)}, bf16[128,960]{1,0:T(8,128)(2,1)S(1)}, u32[]{:S(2)}, u32[]{:S(2)}) collective-permute-start(bf16[128,960]{1,0:T(8,128)(2,1)} %get-tuple-element.186), channel_id=1, source_target_pairs={{0,2},{1,3},{2,0},{3,1},{4,6},{5,7},{6,4},{7,5},{8,10},{9,11},{10,... | collective-permute-start | bytes 737288 | tf_op jit(solution)/shard_map/ppermute | solution.py:578
  459.3 36.4 %collective-permute-start.75 = (bf16[960,640]{1,0:T(8,128)(2,1)}, bf16[960,640]{1,0:T(8,128)(2,1)}, u32[]{:S(2)}, u32[]{:S(2)}) collective-permute-start(bf16[960,640]{1,0:T(8,128)(2,1)} %constant_dynamic-slice_fusion.11), channel_id=1, source_target_pairs={{0,16},{16,0},{1,17},{17,1},{2,18},{18,2},{3,19},{19,3},{4,20},{20... | collective-permute-start | bytes 3686408 | tf_op jit(solution)/shard_map/ppermute | solution.py:573
  471.1 29.9 %collective-permute-start.80 = (bf16[120,640]{1,0:T(8,128)(2,1)}, bf16[120,640]{1,0:T(8,128)(2,1)}, u32[]{:S(2)}, u32[]{:S(2)}) collective-permute-start(bf16[120,640]{1,0:T(8,128)(2,1)} %get-tuple-element.198), channel_id=1, source_target_pairs={{0,1},{1,0},{2,3},{3,2},{4,5},{5,4},{6,7},{7,6},{8,9},{9,8},{10,11... | collective-permute-start | bytes 460808 | tf_op jit(solution)/shard_map/ppermute | solution.py:578
  471.8 36.2 %collective-permute-start.81 = (bf16[120,640]{1,0:T(8,128)(2,1)}, bf16[120,640]{1,0:T(8,128)(2,1)}, u32[]{:S(2)}, u32[]{:S(2)}) collective-permute-start(bf16[120,640]{1,0:T(8,128)(2,1)} %get-tuple-element.199), channel_id=1, source_target_pairs={{0,2},{1,3},{2,0},{3,1},{4,6},{5,7},{6,4},{7,5},{8,10},{9,11},{10,... | collective-permute-start | bytes 460808 | tf_op jit(solution)/shard_map/ppermute | solution.py:578
  472.6 37.9 %collective-permute-start.82 = (bf16[120,640]{1,0:T(8,128)(2,1)}, bf16[120,640]{1,0:T(8,128)(2,1)}, u32[]{:S(2)}, u32[]{:S(2)}) collective-permute-start(bf16[120,640]{1,0:T(8,128)(2,1)} %get-tuple-element.200), channel_id=1, source_target_pairs={{0,3},{1,2},{2,1},{3,0},{4,7},{5,6},{6,5},{7,4},{8,11},{9,10},{10,... | collective-permute-start | bytes 460808 | tf_op jit(solution)/shard_map/ppermute | solution.py:578
  508.0 44.5 %collective-permute-start.106 = (bf16[480,640]{1,0:T(8,128)(2,1)}, bf16[480,640]{1,0:T(8,128)(2,1)}, u32[]{:S(2)}, u32[]{:S(2)}) collective-permute-start(bf16[480,640]{1,0:T(8,128)(2,1)} %constant_dynamic-slice_fusion.1), channel_id=1, source_target_pairs={{0,16},{16,0},{1,17},{17,1},{2,18},{18,2},{3,19},{19,3},{4,20},{20... | collective-permute-start | bytes 1843208 | tf_op jit(solution)/shard_map/ppermute | solution.py:573
  514.8 14.9 %collective-permute-start.85 = (bf16[512,640]{1,0:T(8,128)(2,1)}, bf16[512,640]{1,0:T(8,128)(2,1)S(1)}, u32[]{:S(2)}, u32[]{:S(2)}) collective-permute-start(bf16[512,640]{1,0:T(8,128)(2,1)} %get-tuple-element.204), channel_id=1, source_target_pairs={{0,3},{1,2},{2,1},{3,0},{4,7},{5,6},{6,5},{7,4},{8,11},{9,10},{10,... | collective-permute-start | bytes 1966088 | tf_op jit(solution)/shard_map/ppermute | solution.py:578
  515.8 30.8 %collective-permute-start.84 = (bf16[512,640]{1,0:T(8,128)(2,1)}, bf16[512,640]{1,0:T(8,128)(2,1)S(1)}, u32[]{:S(2)}, u32[]{:S(2)}) collective-permute-start(bf16[512,640]{1,0:T(8,128)(2,1)} %get-tuple-element.203), channel_id=1, source_target_pairs={{0,2},{1,3},{2,0},{3,1},{4,6},{5,7},{6,4},{7,5},{8,10},{9,11},{10,... | collective-permute-start | bytes 1966088 | tf_op jit(solution)/shard_map/ppermute | solution.py:578
  516.6 30.1 %collective-permute-start.83 = (bf16[512,640]{1,0:T(8,128)(2,1)}, bf16[512,640]{1,0:T(8,128)(2,1)S(1)}, u32[]{:S(2)}, u32[]{:S(2)}) collective-permute-start(bf16[512,640]{1,0:T(8,128)(2,1)} %get-tuple-element.202), channel_id=1, source_target_pairs={{0,1},{1,0},{2,3},{3,2},{4,5},{5,4},{6,7},{7,6},{8,9},{9,8},{10,11... | collective-permute-start | bytes 1966088 | tf_op jit(solution)/shard_map/ppermute | solution.py:578
  520.1 61.6 %collective-permute-start.91 = (bf16[4,1,240,960]{3,2,1,0:T(8,128)(2,1)}, bf16[4,1,240,960]{3,2,1,0:T(8,128)(2,1)}, u32[]{:S(2)}, u32[]{:S(2)}) collective-permute-start(bf16[4,1,240,960]{3,2,1,0:T(8,128)(2,1)} %fusion.1), channel_id=1, source_target_pairs={{0,16},{16,0},{1,17},{17,1},{2,18},{18,2},{3,19},{19,3},{4,20},{20... | collective-permute-start | bytes 5529608 | tf_op jit(solution)/shard_map/ppermute | solution.py:573
  552.0 18.8 %collective-permute-start.88 = (bf16[128,640]{1,0:T(8,128)(2,1)}, bf16[128,640]{1,0:T(8,128)(2,1)}, u32[]{:S(2)}, u32[]{:S(2)}) collective-permute-start(bf16[128,640]{1,0:T(8,128)(2,1)} %get-tuple-element.355), channel_id=1, source_target_pairs={{0,8},{4,12},{8,0},{12,4},{1,9},{5,13},{9,1},{13,5},{2,10},{6,14},... | collective-permute-start | bytes 491528 | tf_op jit(solution)/shard_map/ppermute | solution.py:612
  552.0 18.8 %collective-permute-start.89 = (bf16[128,640]{1,0:T(8,128)(2,1)}, bf16[128,640]{1,0:T(8,128)(2,1)}, u32[]{:S(2)}, u32[]{:S(2)}) collective-permute-start(bf16[128,640]{1,0:T(8,128)(2,1)} %get-tuple-element.354), channel_id=1, source_target_pairs={{0,4},{4,8},{8,12},{12,0},{1,5},{5,9},{9,13},{13,1},{2,6},{6,10},{... | collective-permute-start | bytes 491528 | tf_op jit(solution)/shard_map/ppermute | solution.py:612
  556.0 141.3 %all-reduce.11.cloned.1.call-start = ((), (), s32[]{:S(2)}) async-start(), calls=%async_computation.1 | async-start | bytes 983040 | tf_op jit(solution)/shard_map/psum | solution.py:761
  585.6 21.9 %collective-permute-start.93 = (bf16[240,960]{1,0:T(8,128)(2,1)}, bf16[240,960]{1,0:T(8,128)(2,1)}, u32[]{:S(2)}, u32[]{:S(2)}) collective-permute-start(bf16[240,960]{1,0:T(8,128)(2,1)} %get-tuple-element.219), channel_id=1, source_target_pairs={{0,2},{1,3},{2,0},{3,1},{4,6},{5,7},{6,4},{7,5},{8,10},{9,11},{10,... | collective-permute-start | bytes 1382408 | tf_op jit(solution)/shard_map/ppermute | solution.py:578
  585.6 21.9 %collective-permute-start.94 = (bf16[240,960]{1,0:T(8,128)(2,1)}, bf16[240,960]{1,0:T(8,128)(2,1)}, u32[]{:S(2)}, u32[]{:S(2)}) collective-permute-start(bf16[240,960]{1,0:T(8,128)(2,1)} %get-tuple-element.220), channel_id=1, source_target_pairs={{0,3},{1,2},{2,1},{3,0},{4,7},{5,6},{6,5},{7,4},{8,11},{9,10},{10,... | collective-permute-start | bytes 1382408 | tf_op jit(solution)/shard_map/ppermute | solution.py:578
  621.8 20.0 %collective-permute-start.104 = (bf16[128,640]{1,0:T(8,128)(2,1)S(1)}, bf16[128,640]{1,0:T(8,128)(2,1)S(1)}, u32[]{:S(2)}, u32[]{:S(2)}) collective-permute-start(bf16[128,640]{1,0:T(8,128)(2,1)S(1)} %add_convert_fusion.13.refs_0_), channel_id=1, source_target_pairs={{0,8},{4,12},{8,0},{12,4},{1,9},{5,13},{9,1},{13,5},{2,10},{6,14},... | collective-permute-start | bytes 491528 | tf_op jit(solution)/shard_map/ppermute | solution.py:599
  624.2 17.8 %collective-permute-start.105 = (bf16[128,640]{1,0:T(8,128)(2,1)S(1)}, bf16[128,640]{1,0:T(8,128)(2,1)S(1)}, u32[]{:S(2)}, u32[]{:S(2)}) collective-permute-start(bf16[128,640]{1,0:T(8,128)(2,1)S(1)} %add_convert_fusion.13.refs_0_), channel_id=1, source_target_pairs={{0,12},{4,0},{8,4},{12,8},{1,13},{5,1},{9,5},{13,9},{2,14},{6,2},{... | collective-permute-start | bytes 491528 | tf_op jit(solution)/shard_map/ppermute | solution.py:599
  628.1 14.7 %collective-permute-start.98 = (bf16[128,960]{1,0:T(8,128)(2,1)S(1)}, bf16[128,960]{1,0:T(8,128)(2,1)S(1)}, u32[]{:S(2)}, u32[]{:S(2)}) collective-permute-start(bf16[128,960]{1,0:T(8,128)(2,1)S(1)} %get-tuple-element.225), channel_id=1, source_target_pairs={{0,3},{1,2},{2,1},{3,0},{4,7},{5,6},{6,5},{7,4},{8,11},{9,10},{10,... | collective-permute-start | bytes 737288 | tf_op jit(solution)/shard_map/ppermute | solution.py:578
  644.8 18.6 %collective-permute-start.99 = (bf16[128,960]{1,0:T(8,128)(2,1)S(1)}, bf16[128,960]{1,0:T(8,128)(2,1)S(1)}, u32[]{:S(2)}, u32[]{:S(2)}) collective-permute-start(bf16[128,960]{1,0:T(8,128)(2,1)S(1)} %get-tuple-element.304), channel_id=1, source_target_pairs={{0,16},{16,0},{1,17},{17,1},{2,18},{18,2},{3,19},{19,3},{4,20},{20... | collective-permute-start | bytes 737288 | tf_op jit(solution)/shard_map/ppermute | solution.py:573
  662.0 42.7 %collective-permute-start.109 = (bf16[960,640]{1,0:T(8,128)(2,1)}, bf16[960,640]{1,0:T(8,128)(2,1)S(1)}, u32[]{:S(2)}, u32[]{:S(2)}) collective-permute-start(bf16[960,640]{1,0:T(8,128)(2,1)} %get-tuple-element.306), channel_id=1, source_target_pairs={{0,16},{16,0},{1,17},{17,1},{2,18},{18,2},{3,19},{19,3},{4,20},{20... | collective-permute-start | bytes 3686408 | tf_op jit(solution)/shard_map/ppermute | solution.py:573
  662.9 36.1 %collective-permute-start.110 = (bf16[480,640]{1,0:T(8,128)(2,1)}, bf16[480,640]{1,0:T(8,128)(2,1)}, u32[]{:S(2)}, u32[]{:S(2)}) collective-permute-start(bf16[480,640]{1,0:T(8,128)(2,1)} %broadcast_select_fusion.6), channel_id=1, source_target_pairs={{0,16},{16,0},{1,17},{17,1},{2,18},{18,2},{3,19},{19,3},{4,20},{20... | collective-permute-start | bytes 1843208 | tf_op jit(solution)/shard_map/ppermute | solution.py:573
  (300 other events, 2232.6 us)
Sparse Core Ops, SparseCore 0:
  368.2 65.3 all-reduce.8
  436.2 52.7 all-reduce.14
  556.1 100.7 all-reduce.12
  659.8 37.3 all-reduce.10

commit v3 on v2

--- a/solution.py
+++ b/solution.py
@@ -19,6 +19,7 @@
 EPSILON = 1e-05
 ROPE_BASE = 100000.0
 MASKED = -1e30
+FLOPS_PER_US = 1.15e9
 SCALE = HD**-0.5
 F32 = jnp.float32
 BF16 = jnp.bfloat16
@@ -32,7 +33,7 @@
 
 
 def cost(us):
-    return pl.CostEstimate(flops=int(us * 1.15e9), bytes_accessed=0, transcendentals=0)
+    return pl.CostEstimate(flops=int(us * FLOPS_PER_US), bytes_accessed=0, transcendentals=0)
 
 
 def dot_nn(a, b):
@@ -57,40 +58,43 @@
     return jnp.where(lane % HD < HD // 2, ahead, behind)
 
 
-def join_kernel(*refs):
-    pieces, out_ref = refs[:-1], refs[-1]
-    rows = pieces[0].shape[0]
+def join_kernel(*refs, count):
+    pieces, out_ref = refs[:count], refs[-1]
+    rows, width = pieces[0].shape
     for k, piece in enumerate(pieces):
-        out_ref[k * rows : (k + 1) * rows, :] = piece[...]
-
-
-def join(pieces):
+        out_ref[k * rows : (k + 1) * rows, :width] = piece[...]
+    if out_ref.shape[1] > width:
+        out_ref[:, width:] = jnp.zeros((out_ref.shape[0], out_ref.shape[1] - width), out_ref.dtype)
+
+
+def join(pieces, after=()):
     rows, width = pieces[0].shape
-    return pl.pallas_call(
-        join_kernel,
-        out_shape=jax.ShapeDtypeStruct((rows * len(pieces), width), pieces[0].dtype),
-        in_specs=[WHOLE] * len(pieces),
+    padded = -(-width // LANES) * LANES
+    return pl.pallas_call(
+        functools.partial(join_kernel, count=len(pieces)),
+        out_shape=jax.ShapeDtypeStruct((rows * len(pieces), padded), pieces[0].dtype),
+        in_specs=[WHOLE] * len(pieces) + [pl.BlockSpec(memory_space=pl.ANY)] * len(after),
         out_specs=WHOLE,
         compiler_params=params(24),
         cost_estimate=cost(1),
         name="join",
-    )(*pieces)
+    )(*pieces, *after)
 
 
 def assemble_kernel(index_ref, mine_ref, other_ref, out_ref, *, relative, rows, shard_rows, step):
     wa, section = index_ref[0], index_ref[1]
     count = out_ref.shape[0] // shard_rows
     part = mine_ref.shape[0] // count
+    width = out_ref.shape[1]
     for k in range(count):
         base = ((wa ^ k) if relative else k) * shard_rows
         start = pl.multiple_of(base + section * step, 16)
-        out_ref[pl.ds(start, rows), :] = mine_ref[k * part : k * part + rows, :]
+        out_ref[pl.ds(start, rows), :] = mine_ref[k * part : k * part + rows, :width]
         start = pl.multiple_of(base + (1 - section) * step, 16)
-        out_ref[pl.ds(start, rows), :] = other_ref[k * part : k * part + rows, :]
-
-
-def assemble(index, mine, other, count, relative, rows, shard_rows, step):
-    width = mine.shape[1]
+        out_ref[pl.ds(start, rows), :] = other_ref[k * part : k * part + rows, :width]
+
+
+def assemble(index, mine, other, width, count, relative, rows, shard_rows, step):
     total = shard_rows * count
     return pl.pallas_call(
         functools.partial(
@@ -237,9 +241,8 @@
     )(qpos, kpos, queries, *groups)
 
 
-def attend_back_kernel(qpos_ref, kpos_ref, q_ref, g_ref, o_ref, *refs):
-    count = (len(refs) - 1) // 2
-    kv_refs, dq_ref, dkv_refs = refs[:count], refs[count], refs[count + 1 :]
+def attend_back_kernel(qpos_ref, kpos_ref, q_ref, g_ref, o_ref, *refs, count):
+    kv_refs, dq_ref, dkv_refs = refs[:count], refs[-count - 1], refs[-count:]
     queries = stack_heads(q_ref)
     grads = stack_heads(g_ref)
     saved = o_ref[...]
@@ -265,14 +268,14 @@
         dq_ref[:, i * LANES : (i + 1) * LANES] = acc[i * tok : (i + 1) * tok] * SCALE
 
 
-def attend_back(qpos_row, kpos_column, queries, grads, saved, groups):
+def attend_back(qpos_row, kpos_column, queries, grads, saved, groups, after):
     rows = queries.shape[0]
     keys = groups[0].shape[0]
     pairs = H * rows * keys * len(groups)
     heads = pl.BlockSpec((rows, GROUP * LANES), lambda g: (0, g))
     kv_block = pl.BlockSpec((keys, LANES), lambda g: (0, g))
     result = pl.pallas_call(
-        attend_back_kernel,
+        functools.partial(attend_back_kernel, count=len(groups)),
         out_shape=(jax.ShapeDtypeStruct((rows, H * LANES), F32),)
         + tuple(jax.ShapeDtypeStruct(group.shape, BF16) for group in groups),
         grid=(KVH,),
@@ -283,12 +286,13 @@
             heads,
             pl.BlockSpec((GROUP * rows, LANES), lambda g: (g, 0)),
         ]
-        + [kv_block for _ in groups],
+        + [kv_block for _ in groups]
+        + [pl.BlockSpec(memory_space=pl.ANY) for _ in after],
         out_specs=(heads,) + tuple(kv_block for _ in groups),
         compiler_params=params(40),
         cost_estimate=cost(15.2),
         name="attend_back",
-    )(qpos_row, kpos_column, queries, grads, saved, *groups)
+    )(qpos_row, kpos_column, queries, grads, saved, *groups, *after)
     return result[0], result[1:]
 
 
@@ -691,52 +695,61 @@
     def fetch_rows(part, after=()):
         if after:
             (part,) = tie((part,), after)
-        pieces = gather_wa(part)
-        mine = join(pieces)
-        other = to_sibling(mine)
-        whole = assemble(index, mine, other, wa_count, True, kept_rows, shard_rows, step)
-        return whole, mine, pieces[1:]
-
-    def gains_of(mine):
-        rows = mine.reshape(wa_count, -1, mine.shape[1])[:, kept_rows : kept_rows + 2, :shard_rows]
+        return gather_wa(part)
+
+    def placed_rows(pieces, after=()):
+        mine = join(pieces, after)
+        columns = pieces[0].shape[1]
+        return assemble(
+            index, mine, to_sibling(mine), columns, wa_count, True, kept_rows, shard_rows, step
+        )
+
+    def gains_of(pieces):
+        rows = jnp.stack([piece[kept_rows : kept_rows + 2, :shard_rows] for piece in pieces])
         return rows[wa ^ jnp.arange(wa_count)].transpose(1, 0, 2).reshape(2, 1, width)
 
     def fetch_columns(part, after):
-        pieces = send_wa(tie([at(part, wa ^ k, ff_part, 1) for k in peers], after))
-        mine = join(pieces)
-        return assemble_pair(index, mine, to_sibling(mine), shard_rows), pieces[1:]
+        return send_wa(tie([at(part, wa ^ k, ff_part, 1) for k in peers], after))
+
+    def placed_columns(pieces, after):
+        mine = join(pieces, after)
+        return assemble_pair(index, mine, to_sibling(mine), shard_rows)
 
     qkv_parts = halves(w_qkv, gain_rows)
-    qkv, mine, pieces = fetch_rows(qkv_parts[0])
+    qkv_pieces = fetch_rows(qkv_parts[0])
+    qkv = placed_rows(qkv_pieces)
     out_parts = halves(w_out)
     crossing = to_sibling(jnp.where(first, w_up, w_gate))
     wide_parts = (jnp.where(first, w_gate, crossing), jnp.where(first, crossing, w_up))
     down_other = to_sibling(w_down)
     downs = (jnp.where(first, w_down, down_other), jnp.where(first, down_other, w_down))
-    gains = [gains_of(mine)]
-    out, _, pieces = fetch_rows(out_parts[0], pieces)
-    qkv_last, mine, pieces = fetch_rows(qkv_parts[1], pieces)
-    gains.append(gains_of(mine))
-    qkvs, outs, wides = [qkv, qkv_last], [out], []
+    out_pieces = fetch_rows(out_parts[0], qkv_pieces[1:])
+    last_pieces = fetch_rows(qkv_parts[1], out_pieces[1:])
+    gains = [gains_of(qkv_pieces), gains_of(last_pieces)]
+    qkvs, outs, wides = [qkv], [], []
 
     terms = [lax.dynamic_index_in_dim(block_input, section, 0, keepdims=False)]
     cotangent = lax.dynamic_index_in_dim(out_cotangent, section, 0, keepdims=False)
     records, inputs = [], []
     for layer in range(layers):
         u, normed, queries, kv = project(terms, gains[layer][0], qkvs[layer], cosine, sine)
+        pieces = last_pieces[1:]
         if layer:
-            out, _, pieces = fetch_rows(out_parts[layer], terms[1:])
-            outs.append(out)
-            (grad_y,) = tie((cotangent,), pieces)
+            out_pieces = fetch_rows(out_parts[layer], terms[1:])
+            (grad_y,) = tie((cotangent,), out_pieces[1:])
             grad_ys = gather_wa(grad_y)
             pieces = grad_ys[1:]
-        (group,) = tie((gather_ctx(kv),), pieces)
+        group = gather_ctx(kv)
+        outs.append(placed_rows(out_pieces, (group,)))
+        (group,) = tie((group,), pieces)
         groups = gather_wa(group)
-        weight, pieces = fetch_columns(wide_parts[layer], groups[1:])
-        wides.append(weight)
+        wide_pieces = fetch_columns(wide_parts[layer], groups[1:])
         saved = attend(qpos_column, key_pos, queries, groups)
+        wides.append(placed_columns(wide_pieces, (saved,)))
+        if not layer:
+            qkvs.append(placed_rows(last_pieces, (saved,)))
         low, middle, second = close_attention(u, saved, outs[layer], gains[layer][1])
-        seconds = gather_wa(*tie((second,), pieces))
+        seconds = gather_wa(*tie((second,), wide_pieces[1:]))
         wide, hidden = widen(seconds, wides[layer])
         if layer < layers - 1:
             partial = narrow(hidden, downs[layer], wa_count, index)
@@ -754,23 +767,21 @@
 
     def rows_over_wa(blocks, after):
         half = over_cores(blocks, 1, 1)[:, 0]
-        pieces = send_wa(tie([at(half, wa ^ k, 1, 0)[0] for k in peers], after))
+        pieces = [at(half, wa ^ k, 1, 0)[0] for k in peers]
+        pieces = send_wa(tie(pieces, after) if after else pieces)
         return added(pieces).astype(BF16), pieces[1:]
 
-    def over_ctx(values, after):
-        return lax.psum(tie(values, after) if after else tuple(values), "ctx")
+    def over_ctx(values, turn):
+        order = [(i + turn) % ctx_count for i in range(ctx_count)]
+        return lax.psum(tuple(values), "ctx", axis_index_groups=[order])
 
     input_grads, gain_grads = [None] * layers, []
     sums, pending = {}, ()
-    done = ()
     for layer in reversed(range(layers)):
         u, normed, queries, groups, saved, low, middle, seconds, wide, hidden = records[layer]
         if layer < layers - 1:
-            (grad_y,) = tie((grad_y,), square_pieces)
             grad_ys = gather_wa(grad_y)
         grad_wide, partial = mlp_back(grad_ys, wide, wides[layer], downs[layer])
-        if layer < layers - 1:
-            partial = tie(partial, (sums["wide", layer + 1],))
         terms = send_wa(partial)
         grad_middle, grad_low, grad_heads, gain_two_grad = open_back(
             terms, middle, gains[layer][1], grad_y, outs[layer]
@@ -781,36 +792,38 @@
         wide_half = over_cores(wide_grad, ff_part, 1)
         down_half = over_cores(down_grad, width // 2, 0)
         pieces = [at(wide_half, wa ^ k, shard_rows, 0) for k in peers]
-        pieces = send_wa(tie(pieces, (grad_heads,)))
+        pieces = send_wa(pieces)
         wide_rows = join(pieces)
         wide_pieces = pieces[1:]
+        before = (wide_rows, down_half)
         if pending:
-            key_half, key_pieces = rows_over_wa(pending[0], (grad_heads,))
-            wide_pieces = wide_pieces + key_pieces
-
-        dq, dkv = attend_back(qpos_row, key_pos_column, queries, grad_heads, saved, groups)
-        dkv = send_wa(tie(dkv, wide_pieces))
+            key_half, _ = rows_over_wa(pending[0], ())
+            before = (wide_rows, key_half)
+
+        dq, dkv = attend_back(
+            qpos_row, key_pos_column, queries, grad_heads, saved, groups, before
+        )
+        if layer < layers - 1:
+            dkv = tie(dkv, done)
+        dkv = send_wa(dkv)
         gathered = added(dkv).astype(BF16)
         if layer == layers - 1:
-            done = over_ctx((wide_rows,), done)
-            sums["wide", layer] = done[0]
+            done = over_ctx((wide_rows, down_half), 0)
+            sums["wide", layer], sums["down", layer] = done
         else:
-            (gathered,) = tie((gathered,), (sums["square", layer + 1],))
-            done = over_ctx((wide_rows, down_half, key_half), done)
-            sums["wide", layer], sums["down", layer], sums["key", layer + 1] = done
+            done = over_ctx((key_half, wide_rows, down_half), 1)
+            sums["key", layer + 1], sums["wide", layer], sums["down", layer] = done
+            last_square = square_half
 
         terms = scatter_ctx(gathered)
         grad_query, part = query_back(dq, cosine, sine, qkvs[layer])
         out_grad = dot_tn(low, grad_low).astype(BF16)
         query_grad = dot_tn(normed, grad_query).astype(BF16)
         square_grad = jnp.concatenate([blocked(out_grad), blocked(query_grad)], axis=2)
-        square_half, square_pieces = rows_over_wa(square_grad, dkv[1:])
-        if layer == layers - 1:
-            done = over_ctx((down_half, square_half), done)
-            sums["down", layer], sums["square", layer] = done
-        else:
-            done = over_ctx((square_half,), done)
-            sums["square", layer] = done[0]
+        square_half, square_pieces = rows_over_wa(square_grad, ())
+        if layer == 0:
+            done = over_ctx(tie((last_square, square_half), done), 2)
+            sums["square", layer + 1], sums["square", layer] = done
 
         grad_key, grad_u, gain_one_grad = key_back(
             terms, part, cosine, sine, qkvs[layer], u, gains[layer][0], grad_middle

time: 722 us -> 691 us (0.957)
  local copies, waits for them, and re-layouts: 125 us -> 85.5 us
  waiting for transfers between devices: 271 us -> 287 us
    unnamed x501 -> x418, local copies, waits for them, and re-layouts: 83.5 us -> 59.6 us
    ppermute x6, waiting for transfers between devices: 21.4 us -> 36.8 us  [scatter_ctx(): lax.ppermute(piece, 'ctx', [(i, (i - k) % count) for i in range(count)])]
    ppermute x72, waiting for transfers between devices: 186 us -> 177 us  [to_peer(): return lax.ppermute(value, 'wa', [(i, i ^ k) for i in range(count)])]
    psum x4 -> x3, waiting for transfers between devices: 40.5 us -> 47.9 us  [over_ctx(): return lax.psum(tuple(values), 'ctx', axis_index_groups=[order])]
  transfers between devices with their start and end apart: 115 -> 114, of which waited for: 46 -> 45; matrix products, arithmetic and copies ran while one was open for 16% -> 12% of each run, Pallas kernels for 12% -> 11%
where the time goes in v3:
time: 691 us; the launch traced here: 685 us
  waiting for transfers between devices  287 us (42%)
  starting transfers between devices  134 us (19%)
  Pallas kernels  97.7 us (14%)
  local copies, waits for them, and re-layouts  85.5 us (12%)
  other arithmetic  52.2 us (8%)
  between operations  16.3 us (2%)
  matrix products  12.6 us (2%)
    ppermute x72, waiting for transfers between devices, to_peer(): return lax.ppermute(value, 'wa', [(i, i ^ k) for i in range(count)])  177 us
    ppermute x72, starting transfers between devices, to_peer(): return lax.ppermute(value, 'wa', [(i, i ^ k) for i in range(count)])  68.4 us
    unnamed x418, local copies, waits for them, and re-layouts  59.6 us
    psum x3, waiting for transfers between devices, over_ctx(): return lax.psum(tuple(values), 'ctx', axis_index_groups=[order])  47.9 us
    ppermute x24, starting transfers between devices, to_sibling(): return lax.ppermute(value, 'section', [(0, 1), (1, 0)])  44.9 us
    ppermute x6, waiting for transfers between devices, scatter_ctx(): lax.ppermute(piece, 'ctx', [(i, (i - k) % count) for i in range(count)])  36.8 us
    pallas_call x2, Pallas kernels, attend_back(): pl.pallas_call(functools.partial(attend_back_kernel, count=len(groups)),...  28.9 us
    ppermute x9, waiting for transfers between devices, gather_ctx(): lax.ppermute(value, 'ctx', [(i, (i + k) % count) for i in range(count)])  23.8 us
  transfers between devices with their start and end apart: 114, of which 45 were waited for; matrix products, arithmetic and copies ran while one was open for 12% of the time, Pallas kernels for 11%

profile of v3, /device:TPU:1, one launch (start us, length us, event | category | flops | bytes accessed | tf_op | source)
XLA Modules:
  0.0 685.5 jit_solution(11970114236324794028)
XLA Ops:
  18.7 3.6 collective-permute-start.3
  23.3 10.4 %collective-permute-done.3.refs_3_ = bf16[144,1600]{1,0:T(8,128)(2,1)S(1)} collective-permute-done((bf16[144,1600]{1,0:T(8,128)(2,1)S(1)}, bf16[144,1600]{1,0:T(8,128)(2,1)S(1)}, u32[]{:S(2)}, u32[]{:S(2)}) %collective-permute-start.3) | collective-permute-done | bytes 460832 | tf_op jit(solution)/shard_map/ppermute | solution.py:582
  33.7 10.3 %collective-permute-done.2.refs_2_ = bf16[144,1600]{1,0:T(8,128)(2,1)S(1)} collective-permute-done((bf16[144,1600]{1,0:T(8,128)(2,1)S(1)}, bf16[144,1600]{1,0:T(8,128)(2,1)S(1)}, u32[]{:S(2)}, u32[]{:S(2)}) %collective-permute-start.2) | collective-permute-done | bytes 460832 | tf_op jit(solution)/shard_map/ppermute | solution.py:582
  54.1 2.4 assemble.4.refs_2_.w_ref.refs_7_
  69.9 4.8 collective-permute-done.6.refs_2_
  77.6 3.3 collective-permute-done.7.refs_3_
  90.7 3.3 bitcast_select_fusion
  95.0 4.0 collective-permute-start.18
  99.0 2.8 collective-permute-done.15.refs_1_.refs_4_
  101.9 2.5 collective-permute-done.16.refs_2_.refs_5_
  104.4 12.6 %collective-permute-done.17.refs_3_.refs_6_ = bf16[512,640]{1,0:T(8,128)(2,1)S(1)} collective-permute-done((bf16[512,640]{1,0:T(8,128)(2,1)}, bf16[512,640]{1,0:T(8,128)(2,1)S(1)}, u32[]{:S(2)}, u32[]{:S(2)}) %collective-permute-start.17) | collective-permute-done | bytes 655392 | tf_op jit(solution)/shard_map/ppermute | solution.py:582
  124.8 8.8 %attend.2.saved_ref.refs_4_.o_ref = f32[1920,128]{1,0:T(8,128)S(1)} custom-call(s32[128,1]{1,0:T(8,128)S(1)} %copy.102.qpos_ref, s32[4,512]{1,0:T(4,128)S(1)} %pad_add_fusion.kpos_ref, bf16[128,1920]{1,0:T(8,128)(2,1)S(1)} %copy-done.172, bf16[512,640]{1,0:T(8,128)(2,1)S(1)} %copy-done.39, bf16[512,640]{1,0:T(8,128)(2,1)S(1)} %copy-done.26, ...), custom_call_target="tpu_custom_call" | custom-call | flops 11040000000 | tf_op jit(solution)/shard_map/attend/pallas_call | solution.py:227
  135.0 4.8 collective-permute-start.26
  139.8 3.0 broadcast_select_fusion.2
  153.1 3.6 collective-permute-done.23.refs_1_
  156.6 5.8 collective-permute-done.25.refs_3_
  164.1 2.4 narrow.2
  171.3 3.2 collective-permute-done.28.refs_2_
  174.9 5.8 collective-permute-done.30.refs_4_
  185.3 2.5 project.3
  189.3 2.5 collective-permute-start.33
  197.0 5.8 collective-permute-done.33.refs_2_
  210.4 5.5 collective-permute-start.44
  215.9 2.8 collective-permute-done.41.refs_1_.refs_4_
  218.6 14.7 %collective-permute-done.43.refs_3_.refs_6_ = bf16[512,640]{1,0:T(8,128)(2,1)} collective-permute-done((bf16[512,640]{1,0:T(8,128)(2,1)}, bf16[512,640]{1,0:T(8,128)(2,1)}, u32[]{:S(2)}, u32[]{:S(2)}) %collective-permute-start.43) | collective-permute-done | bytes 655392 | tf_op jit(solution)/shard_map/ppermute | solution.py:582
  237.1 9.9 %attend.3.saved_ref.refs_4_.o_ref = f32[1920,128]{1,0:T(8,128)S(1)} custom-call(s32[128,1]{1,0:T(8,128)S(1)} %copy-done.99, s32[4,512]{1,0:T(4,128)S(1)} %pad_add_fusion.kpos_ref, bf16[128,1920]{1,0:T(8,128)(2,1)S(1)} %copy-done.162, bf16[512,640]{1,0:T(8,128)(2,1)S(1)} %copy-done.24, bf16[512,640]{1,0:T(8,128)(2,1)S(1)} %copy-done.35, ...), custom_call_target="tpu_custom_call" | custom-call | flops 11040000000 | tf_op jit(solution)/shard_map/attend/pallas_call | solution.py:227
  248.7 7.7 %collective-permute-start.51 = (bf16[960,640]{1,0:T(8,128)(2,1)}, bf16[960,640]{1,0:T(8,128)(2,1)}, u32[]{:S(2)}, u32[]{:S(2)}) collective-permute-start(bf16[960,640]{1,0:T(8,128)(2,1)} %join.18.mine_ref), channel_id=1, source_target_pairs={{0,16},{16,0},{1,17},{17,1},{2,18},{18,2},{3,19},{19,3},{4,20},{20... | collective-permute-start | bytes 3686408 | tf_op jit(solution)/shard_map/ppermute | solution.py:577
  266.7 3.8 collective-permute-done.48.refs_1_
  270.5 6.5 collective-permute-done.49.refs_2_
  279.4 2.5 mlp_back.2
  290.1 2.4 convolution_convert_fusion.9
  298.1 2.9 collective-permute-done.54.refs_3_
  303.0 4.8 collective-permute-done.56.refs_1_
  307.8 6.8 collective-permute-done.57.refs_2_
  321.1 14.7 %attend_back.2 = (f32[128,1920]{1,0:T(8,128)S(1)}, bf16[512,640]{1,0:T(8,128)(2,1)S(1)}, bf16[512,640]{1,0:T(8,128)(2,1)S(1)}, bf16[512,640]{1,0:T(8,128)(2,1)S(1)}, bf16[512,640]{1,0:T(8,128)(2,1)S(1)}) custom-call(s32[1,128]{1,0:T(1,128)S(1)} %add.542.qpos_ref, s32[512,4]{1,0:T(8,128)S(1)} %bitcast.156, bf16[128,1920]{1,0:T(8,128)(2,1)S(1)} %copy-done.163, ...), custom_call_target="tpu_custom_call" | custom-call | flops 17479999488 | tf_op jit(solution)/shard_map/attend_back/pallas_call | solution.py:277
  342.9 14.2 %collective-permute-done.62 = bf16[512,640]{1,0:T(8,128)(2,1)S(1)} collective-permute-done((bf16[512,640]{1,0:T(8,128)(2,1)}, bf16[512,640]{1,0:T(8,128)(2,1)S(1)}, u32[]{:S(2)}, u32[]{:S(2)}) %collective-permute-start.62) | collective-permute-done | bytes 655392 | tf_op jit(solution)/shard_map/ppermute | solution.py:582
  357.1 15.0 %collective-permute-done.61 = bf16[512,640]{1,0:T(8,128)(2,1)} collective-permute-done((bf16[512,640]{1,0:T(8,128)(2,1)}, bf16[512,640]{1,0:T(8,128)(2,1)}, u32[]{:S(2)}, u32[]{:S(2)}) %collective-permute-start.61) | collective-permute-done | bytes 655392 | tf_op jit(solution)/shard_map/ppermute | solution.py:582
  375.5 2.5 collective-permute-start.64
  386.6 11.8 %collective-permute-done.64.refs_2_ = bf16[128,640]{1,0:T(8,128)(2,1)S(1)} collective-permute-done((bf16[128,640]{1,0:T(8,128)(2,1)}, bf16[128,640]{1,0:T(8,128)(2,1)S(1)}, u32[]{:S(2)}, u32[]{:S(2)}) %collective-permute-start.64) | collective-permute-done | bytes 163872 | tf_op jit(solution)/shard_map/ppermute | solution.py:616
  407.5 2.9 collective-permute-done.67.refs_2_
  410.4 2.5 mlp_back.3
  414.6 7.3 %collective-permute-start.72 = (bf16[960,640]{1,0:T(8,128)(2,1)S(1)}, bf16[960,640]{1,0:T(8,128)(2,1)S(1)}, u32[]{:S(2)}, u32[]{:S(2)}) collective-permute-start(bf16[960,640]{1,0:T(8,128)(2,1)S(1)} %constant_dynamic-slice_fusion.10), channel_id=1, source_target_pairs={{0,16},{16,0},{1,17},{17,1},{2,18},{18,2},{3,19},{19,3},{4,20},{20... | collective-permute-start | bytes 3686408 | tf_op jit(solution)/shard_map/ppermute | solution.py:577
  427.3 2.8 collective-permute-done.69.refs_1_
  430.1 5.4 collective-permute-done.71.refs_3_
  446.6 3.2 collective-permute-start.102
  450.0 2.4 collective-permute-done.73.refs_1_
  454.5 3.8 collective-permute-done.75.refs_3_
  460.8 14.2 %attend_back.3 = (f32[128,1920]{1,0:T(8,128)S(1)}, bf16[512,640]{1,0:T(8,128)(2,1)S(1)}, bf16[512,640]{1,0:T(8,128)(2,1)S(1)}, bf16[512,640]{1,0:T(8,128)(2,1)S(1)}, bf16[512,640]{1,0:T(8,128)(2,1)S(1)}) custom-call(s32[1,128]{1,0:T(1,128)S(1)} %add.542.qpos_ref, s32[512,4]{1,0:T(8,128)S(1)} %bitcast.157, bf16[128,1920]{1,0:T(8,128)(2,1)S(1)} %copy-done.173, ...), custom_call_target="tpu_custom_call" | custom-call | flops 17479999488 | tf_op jit(solution)/shard_map/attend_back/pallas_call | solution.py:277
  484.6 3.0 add_convert_fusion
  496.7 17.3 %collective-permute-done.81 = bf16[512,640]{1,0:T(8,128)(2,1)} collective-permute-done((bf16[512,640]{1,0:T(8,128)(2,1)}, bf16[512,640]{1,0:T(8,128)(2,1)}, u32[]{:S(2)}, u32[]{:S(2)}) %collective-permute-start.81) | collective-permute-done | bytes 655392 | tf_op jit(solution)/shard_map/ppermute | solution.py:582
  516.0 3.8 collective-permute-start.84
  523.8 6.2 collective-permute-done.83.refs_1_
  531.1 18.9 %collective-permute-done.84.refs_2_ = bf16[128,640]{1,0:T(8,128)(2,1)S(1)} collective-permute-done((bf16[128,640]{1,0:T(8,128)(2,1)S(1)}, bf16[128,640]{1,0:T(8,128)(2,1)S(1)}, u32[]{:S(2)}, u32[]{:S(2)}) %collective-permute-start.84) | collective-permute-done | bytes 163872 | tf_op jit(solution)/shard_map/ppermute | solution.py:616
  554.5 2.4 fusion.39.refs_0_
  562.2 2.8 add_convert_fusion.1
  570.0 23.9 %all-reduce.11.cloned.1.call-done = (bf16[120,640]{1,0:T(8,128)(2,1)}, bf16[960,640]{1,0:T(8,128)(2,1)}, bf16[480,640]{1,0:T(8,128)(2,1)}) async-done(((bf16[120,640]{1,0:T(8,128)(2,1)}, bf16[960,640]{1,0:T(8,128)(2,1)}, bf16[480,640]{1,0:T(8,128)(2,1)}), (bf16[120,640]{1,0:T(8,128)(2,1)}, bf16[960,640]{1,0:T(8,128)(2,1)}, bf16[480,640]{1,0:T(8,128)(2,1)})) %all-reduce.11.cloned.1.call-update) | async-done | bytes 1996816 | tf_op jit(solution)/shard_map/psum | solution.py:776
  594.0 3.0 broadcast_select_fusion
  602.0 2.6 fusion.36.refs_1_
  605.7 4.4 collective-permute-done.98
  615.7 2.3 narrow.3
  623.3 9.4 %collective-permute-done.100.refs_2_ = bf16[128,640]{1,0:T(8,128)(2,1)S(1)} collective-permute-done((bf16[128,640]{1,0:T(8,128)(2,1)S(1)}, bf16[128,640]{1,0:T(8,128)(2,1)S(1)}, u32[]{:S(2)}, u32[]{:S(2)}) %collective-permute-start.100) | collective-permute-done | bytes 163872 | tf_op jit(solution)/shard_map/ppermute | solution.py:603
  636.2 3.2 collective-permute-done.92
  644.2 24.0 %all-reduce.13.cloned.1.call-done = (bf16[240,960]{1,0:T(8,128)(2,1)}, bf16[240,960]{1,0:T(8,128)(2,1)}) async-done(((bf16[240,960]{1,0:T(8,128)(2,1)}, bf16[240,960]{1,0:T(8,128)(2,1)}), (bf16[240,960]{1,0:T(8,128)(2,1)}, bf16[240,960]{1,0:T(8,128)(2,1)})) %all-reduce.13.cloned.1.call-update) | async-done | bytes 921616 | tf_op jit(solution)/shard_map/psum | solution.py:776
  670.9 4.1 finish.1
  (791 shorter events, 256.5 us)
Async XLA Ops:
  10.9 35.9 %collective-permute-start.8 = (bf16[128,960]{1,0:T(8,128)(2,1)}, bf16[128,960]{1,0:T(8,128)(2,1)}, u32[]{:S(2)}, u32[]{:S(2)}) collective-permute-start(bf16[128,960]{1,0:T(8,128)(2,1)} %dynamic-slice_bitcast_fusion.8), channel_id=1, source_target_pairs={{0,16},{16,0},{1,17},{17,1},{2,18},{18,2},{3,19},{19,3},{4,20},{20... | collective-permute-start | bytes 737288 | tf_op jit(solution)/shard_map/ppermute | solution.py:577
  12.5 78.2 %collective-permute-start.19 = (bf16[240,2560]{1,0:T(8,128)(2,1)}, bf16[240,2560]{1,0:T(8,128)(2,1)}, u32[]{:S(2)}, u32[]{:S(2)}) collective-permute-start(bf16[240,2560]{1,0:T(8,128)(2,1)} %bitcast_select_fusion.1), channel_id=1, source_target_pairs={{0,16},{16,0},{1,17},{17,1},{2,18},{18,2},{3,19},{19,3},{4,20},{20... | collective-permute-start | bytes 3686408 | tf_op jit(solution)/shard_map/ppermute | solution.py:577
  18.7 15.0 %collective-permute-start.3 = (bf16[144,1600]{1,0:T(8,128)(2,1)S(1)}, bf16[144,1600]{1,0:T(8,128)(2,1)S(1)}, u32[]{:S(2)}, u32[]{:S(2)}) collective-permute-start(bf16[144,1600]{1,0:T(8,128)(2,1)S(1)} %get-tuple-element.270.refs_0_), channel_id=1, source_target_pairs={{0,3},{1,2},{2,1},{3,0},{4,7},{5,6},{6,5},{7,4},{8,11},{9,10},{10,... | collective-permute-start | bytes 1382408 | tf_op jit(solution)/shard_map/ppermute | solution.py:582
  22.3 21.7 %collective-permute-start.2 = (bf16[144,1600]{1,0:T(8,128)(2,1)S(1)}, bf16[144,1600]{1,0:T(8,128)(2,1)S(1)}, u32[]{:S(2)}, u32[]{:S(2)}) collective-permute-start(bf16[144,1600]{1,0:T(8,128)(2,1)S(1)} %get-tuple-element.270.refs_0_), channel_id=1, source_target_pairs={{0,2},{1,3},{2,0},{3,1},{4,6},{5,7},{6,4},{7,5},{8,10},{9,11},{10,... | collective-permute-start | bytes 1382408 | tf_op jit(solution)/shard_map/ppermute | solution.py:582
  22.5 21.5 %collective-permute-start.1 = (bf16[144,1600]{1,0:T(8,128)(2,1)S(1)}, bf16[144,1600]{1,0:T(8,128)(2,1)S(1)}, u32[]{:S(2)}, u32[]{:S(2)}) collective-permute-start(bf16[144,1600]{1,0:T(8,128)(2,1)S(1)} %get-tuple-element.270.refs_0_), channel_id=1, source_target_pairs={{0,1},{1,0},{2,3},{3,2},{4,5},{5,4},{6,7},{7,6},{8,9},{9,8},{10,11... | collective-permute-start | bytes 1382408 | tf_op jit(solution)/shard_map/ppermute | solution.py:582
  49.9 13.8 %collective-permute-start.10 = (bf16[128,960]{1,0:T(8,128)(2,1)}, bf16[128,960]{1,0:T(8,128)(2,1)S(1)}, u32[]{:S(2)}, u32[]{:S(2)}) collective-permute-start(bf16[128,960]{1,0:T(8,128)(2,1)} %tie.13.refs_0_), channel_id=1, source_target_pairs={{0,2},{1,3},{2,0},{3,1},{4,6},{5,7},{6,4},{7,5},{8,10},{9,11},{10,... | collective-permute-start | bytes 737288 | tf_op jit(solution)/shard_map/ppermute | solution.py:582
  50.3 13.5 %collective-permute-start.11 = (bf16[128,960]{1,0:T(8,128)(2,1)}, bf16[128,960]{1,0:T(8,128)(2,1)S(1)}, u32[]{:S(2)}, u32[]{:S(2)}) collective-permute-start(bf16[128,960]{1,0:T(8,128)(2,1)} %tie.13.refs_0_), channel_id=1, source_target_pairs={{0,3},{1,2},{2,1},{3,0},{4,7},{5,6},{6,5},{7,4},{8,11},{9,10},{10,... | collective-permute-start | bytes 737288 | tf_op jit(solution)/shard_map/ppermute | solution.py:582
  61.1 13.7 %collective-permute-start.6 = (bf16[128,640]{1,0:T(8,128)(2,1)S(1)}, bf16[128,640]{1,0:T(8,128)(2,1)S(1)}, u32[]{:S(2)}, u32[]{:S(2)}) collective-permute-start(bf16[128,640]{1,0:T(8,128)(2,1)S(1)} %get-tuple-element.95.refs_0_), channel_id=1, source_target_pairs={{0,8},{4,12},{8,0},{12,4},{1,9},{5,13},{9,1},{13,5},{2,10},{6,14},... | collective-permute-start | bytes 491528 | tf_op jit(solution)/shard_map/ppermute | solution.py:603
  64.6 21.7 %collective-permute-start.12 = (bf16[144,1600]{1,0:T(8,128)(2,1)}, bf16[144,1600]{1,0:T(8,128)(2,1)S(1)}, u32[]{:S(2)}, u32[]{:S(2)}) collective-permute-start(bf16[144,1600]{1,0:T(8,128)(2,1)} %tie.14.refs_0_), channel_id=1, source_target_pairs={{0,1},{1,0},{2,3},{3,2},{4,5},{5,4},{6,7},{7,6},{8,9},{9,8},{10,11... | collective-permute-start | bytes 1382408 | tf_op jit(solution)/shard_map/ppermute | solution.py:582
  65.8 20.5 %collective-permute-start.13 = (bf16[144,1600]{1,0:T(8,128)(2,1)}, bf16[144,1600]{1,0:T(8,128)(2,1)S(1)}, u32[]{:S(2)}, u32[]{:S(2)}) collective-permute-start(bf16[144,1600]{1,0:T(8,128)(2,1)} %tie.14.refs_0_), channel_id=1, source_target_pairs={{0,2},{1,3},{2,0},{3,1},{4,6},{5,7},{6,4},{7,5},{8,10},{9,11},{10,... | collective-permute-start | bytes 1382408 | tf_op jit(solution)/shard_map/ppermute | solution.py:582
  67.3 19.7 %collective-permute-start.14 = (bf16[144,1600]{1,0:T(8,128)(2,1)}, bf16[144,1600]{1,0:T(8,128)(2,1)S(1)}, u32[]{:S(2)}, u32[]{:S(2)}) collective-permute-start(bf16[144,1600]{1,0:T(8,128)(2,1)} %tie.14.refs_0_), channel_id=1, source_target_pairs={{0,3},{1,2},{2,1},{3,0},{4,7},{5,6},{6,5},{7,4},{8,11},{9,10},{10,... | collective-permute-start | bytes 1382408 | tf_op jit(solution)/shard_map/ppermute | solution.py:582
  80.9 59.0 %collective-permute-start.27 = (bf16[960,640]{1,0:T(8,128)(2,1)}, bf16[960,640]{1,0:T(8,128)(2,1)}, u32[]{:S(2)}, u32[]{:S(2)}) collective-permute-start(bf16[960,640]{1,0:T(8,128)(2,1)} %bitcast.170), channel_id=1, source_target_pairs={{0,16},{16,0},{1,17},{17,1},{2,18},{18,2},{3,19},{19,3},{4,20},{20... | collective-permute-start | bytes 3686408 | tf_op jit(solution)/shard_map/ppermute | solution.py:577
  88.0 13.9 %collective-permute-start.15 = (bf16[512,640]{1,0:T(8,128)(2,1)}, bf16[512,640]{1,0:T(8,128)(2,1)S(1)}, u32[]{:S(2)}, u32[]{:S(2)}) collective-permute-start(bf16[512,640]{1,0:T(8,128)(2,1)} %tie.15.refs_0_), channel_id=1, source_target_pairs={{0,1},{1,0},{2,3},{3,2},{4,5},{5,4},{6,7},{7,6},{8,9},{9,8},{10,11... | collective-permute-start | bytes 1966088 | tf_op jit(solution)/shard_map/ppermute | solution.py:582
  89.2 15.2 %collective-permute-start.16 = (bf16[512,640]{1,0:T(8,128)(2,1)}, bf16[512,640]{1,0:T(8,128)(2,1)S(1)}, u32[]{:S(2)}, u32[]{:S(2)}) collective-permute-start(bf16[512,640]{1,0:T(8,128)(2,1)} %tie.15.refs_0_), channel_id=1, source_target_pairs={{0,2},{1,3},{2,0},{3,1},{4,6},{5,7},{6,4},{7,5},{8,10},{9,11},{10,... | collective-permute-start | bytes 1966088 | tf_op jit(solution)/shard_map/ppermute | solution.py:582
  89.7 27.2 %collective-permute-start.17 = (bf16[512,640]{1,0:T(8,128)(2,1)}, bf16[512,640]{1,0:T(8,128)(2,1)S(1)}, u32[]{:S(2)}, u32[]{:S(2)}) collective-permute-start(bf16[512,640]{1,0:T(8,128)(2,1)} %tie.15.refs_0_), channel_id=1, source_target_pairs={{0,3},{1,2},{2,1},{3,0},{4,7},{5,6},{6,5},{7,4},{8,11},{9,10},{10,... | collective-permute-start | bytes 1966088 | tf_op jit(solution)/shard_map/ppermute | solution.py:582
  95.0 48.9 %collective-permute-start.18 = (bf16[512,1024]{1,0:T(8,128)(2,1)}, bf16[512,1024]{1,0:T(8,128)(2,1)}, u32[]{:S(2)}, u32[]{:S(2)}) collective-permute-start(bf16[512,1024]{1,0:T(8,128)(2,1)} %join.13.mine_ref), channel_id=1, source_target_pairs={{0,16},{16,0},{1,17},{17,1},{2,18},{18,2},{3,19},{19,3},{4,20},{20... | collective-permute-start | bytes 3145736 | tf_op jit(solution)/shard_map/ppermute | solution.py:577
  117.8 15.8 %collective-permute-start.20 = (bf16[240,640]{1,0:T(8,128)(2,1)}, bf16[240,640]{1,0:T(8,128)(2,1)S(1)}, u32[]{:S(2)}, u32[]{:S(2)}) collective-permute-start(bf16[240,640]{1,0:T(8,128)(2,1)} %get-tuple-element.98), channel_id=1, source_target_pairs={{0,1},{1,0},{2,3},{3,2},{4,5},{5,4},{6,7},{7,6},{8,9},{9,8},{10,11... | collective-permute-start | bytes 921608 | tf_op jit(solution)/shard_map/ppermute | solution.py:582
  117.9 15.8 %collective-permute-start.21 = (bf16[240,640]{1,0:T(8,128)(2,1)}, bf16[240,640]{1,0:T(8,128)(2,1)S(1)}, u32[]{:S(2)}, u32[]{:S(2)}) collective-permute-start(bf16[240,640]{1,0:T(8,128)(2,1)} %get-tuple-element.99), channel_id=1, source_target_pairs={{0,2},{1,3},{2,0},{3,1},{4,6},{5,7},{6,4},{7,5},{8,10},{9,11},{10,... | collective-permute-start | bytes 921608 | tf_op jit(solution)/shard_map/ppermute | solution.py:582
  120.1 13.6 %collective-permute-start.22 = (bf16[240,640]{1,0:T(8,128)(2,1)}, bf16[240,640]{1,0:T(8,128)(2,1)S(1)}, u32[]{:S(2)}, u32[]{:S(2)}) collective-permute-start(bf16[240,640]{1,0:T(8,128)(2,1)} %get-tuple-element.100), channel_id=1, source_target_pairs={{0,3},{1,2},{2,1},{3,0},{4,7},{5,6},{6,5},{7,4},{8,11},{9,10},{10,... | collective-permute-start | bytes 921608 | tf_op jit(solution)/shard_map/ppermute | solution.py:582
  135.0 16.2 %collective-permute-start.26 = (bf16[960,640]{1,0:T(8,128)(2,1)}, bf16[960,640]{1,0:T(8,128)(2,1)}, u32[]{:S(2)}, u32[]{:S(2)}) collective-permute-start(bf16[960,640]{1,0:T(8,128)(2,1)} %join.14.mine_ref), channel_id=1, source_target_pairs={{0,16},{16,0},{1,17},{17,1},{2,18},{18,2},{3,19},{19,3},{4,20},{20... | collective-permute-start | bytes 3686408 | tf_op jit(solution)/shard_map/ppermute | solution.py:577
  143.0 40.5 %collective-permute-start.31 = (bf16[576,1664]{1,0:T(8,128)(2,1)S(1)}, bf16[576,1664]{1,0:T(8,128)(2,1)}, u32[]{:S(2)}, u32[]{:S(2)}) collective-permute-start(bf16[576,1664]{1,0:T(8,128)(2,1)S(1)} %join.15.mine_ref), channel_id=1, source_target_pairs={{0,16},{16,0},{1,17},{17,1},{2,18},{18,2},{3,19},{19,3},{4,20},{20... | collective-permute-start | bytes 5750792 | tf_op jit(solution)/shard_map/ppermute | solution.py:577
  189.3 13.6 %collective-permute-start.33 = (bf16[128,640]{1,0:T(8,128)(2,1)S(1)}, bf16[128,640]{1,0:T(8,128)(2,1)}, u32[]{:S(2)}, u32[]{:S(2)}) collective-permute-start(bf16[128,640]{1,0:T(8,128)(2,1)S(1)} %get-tuple-element.109.refs_0_), channel_id=1, source_target_pairs={{0,8},{4,12},{8,0},{12,4},{1,9},{5,13},{9,1},{13,5},{2,10},{6,14},... | collective-permute-start | bytes 491528 | tf_op jit(solution)/shard_map/ppermute | solution.py:603
  208.3 25.1 %collective-permute-start.43 = (bf16[512,640]{1,0:T(8,128)(2,1)}, bf16[512,640]{1,0:T(8,128)(2,1)}, u32[]{:S(2)}, u32[]{:S(2)}) collective-permute-start(bf16[512,640]{1,0:T(8,128)(2,1)} %tie.20.refs_0_), channel_id=1, source_target_pairs={{0,3},{1,2},{2,1},{3,0},{4,7},{5,6},{6,5},{7,4},{8,11},{9,10},{10,... | collective-permute-start | bytes 1966088 | tf_op jit(solution)/shard_map/ppermute | solution.py:582
  210.4 46.1 %collective-permute-start.44 = (bf16[512,1024]{1,0:T(8,128)(2,1)}, bf16[512,1024]{1,0:T(8,128)(2,1)}, u32[]{:S(2)}, u32[]{:S(2)}) collective-permute-start(bf16[512,1024]{1,0:T(8,128)(2,1)} %join.17.mine_ref), channel_id=1, source_target_pairs={{0,16},{16,0},{1,17},{17,1},{2,18},{18,2},{3,19},{19,3},{4,20},{20... | collective-permute-start | bytes 3145736 | tf_op jit(solution)/shard_map/ppermute | solution.py:577
  233.4 13.7 %collective-permute-start.45 = (bf16[240,640]{1,0:T(8,128)(2,1)}, bf16[240,640]{1,0:T(8,128)(2,1)S(1)}, u32[]{:S(2)}, u32[]{:S(2)}) collective-permute-start(bf16[240,640]{1,0:T(8,128)(2,1)} %get-tuple-element.112), channel_id=1, source_target_pairs={{0,1},{1,0},{2,3},{3,2},{4,5},{5,4},{6,7},{7,6},{8,9},{9,8},{10,11... | collective-permute-start | bytes 921608 | tf_op jit(solution)/shard_map/ppermute | solution.py:582
  234.1 12.9 %collective-permute-start.46 = (bf16[240,640]{1,0:T(8,128)(2,1)}, bf16[240,640]{1,0:T(8,128)(2,1)S(1)}, u32[]{:S(2)}, u32[]{:S(2)}) collective-permute-start(bf16[240,640]{1,0:T(8,128)(2,1)} %get-tuple-element.113), channel_id=1, source_target_pairs={{0,2},{1,3},{2,0},{3,1},{4,6},{5,7},{6,4},{7,5},{8,10},{9,11},{10,... | collective-permute-start | bytes 921608 | tf_op jit(solution)/shard_map/ppermute | solution.py:582
  234.2 13.0 %collective-permute-start.47 = (bf16[240,640]{1,0:T(8,128)(2,1)}, bf16[240,640]{1,0:T(8,128)(2,1)S(1)}, u32[]{:S(2)}, u32[]{:S(2)}) collective-permute-start(bf16[240,640]{1,0:T(8,128)(2,1)} %get-tuple-element.114), channel_id=1, source_target_pairs={{0,3},{1,2},{2,1},{3,0},{4,7},{5,6},{6,5},{7,4},{8,11},{9,10},{10,... | collective-permute-start | bytes 921608 | tf_op jit(solution)/shard_map/ppermute | solution.py:582
  248.7 16.0 %collective-permute-start.51 = (bf16[960,640]{1,0:T(8,128)(2,1)}, bf16[960,640]{1,0:T(8,128)(2,1)}, u32[]{:S(2)}, u32[]{:S(2)}) collective-permute-start(bf16[960,640]{1,0:T(8,128)(2,1)} %join.18.mine_ref), channel_id=1, source_target_pairs={{0,16},{16,0},{1,17},{17,1},{2,18},{18,2},{3,19},{19,3},{4,20},{20... | collective-permute-start | bytes 3686408 | tf_op jit(solution)/shard_map/ppermute | solution.py:577
  263.5 13.4 %collective-permute-start.49 = (bf16[128,960]{1,0:T(8,128)(2,1)}, bf16[128,960]{1,0:T(8,128)(2,1)S(1)}, u32[]{:S(2)}, u32[]{:S(2)}) collective-permute-start(bf16[128,960]{1,0:T(8,128)(2,1)} %tie.22.refs_0_), channel_id=1, source_target_pairs={{0,2},{1,3},{2,0},{3,1},{4,6},{5,7},{6,4},{7,5},{8,10},{9,11},{10,... | collective-permute-start | bytes 737288 | tf_op jit(solution)/shard_map/ppermute | solution.py:582
  263.5 13.4 %collective-permute-start.50 = (bf16[128,960]{1,0:T(8,128)(2,1)}, bf16[128,960]{1,0:T(8,128)(2,1)S(1)}, u32[]{:S(2)}, u32[]{:S(2)}) collective-permute-start(bf16[128,960]{1,0:T(8,128)(2,1)} %tie.22.refs_0_), channel_id=1, source_target_pairs={{0,3},{1,2},{2,1},{3,0},{4,7},{5,6},{6,5},{7,4},{8,11},{9,10},{10,... | collective-permute-start | bytes 737288 | tf_op jit(solution)/shard_map/ppermute | solution.py:582
  295.6 19.1 %collective-permute-start.57 = (bf16[240,640]{1,0:T(8,128)(2,1)S(1)}, bf16[240,640]{1,0:T(8,128)(2,1)S(1)}, u32[]{:S(2)}, u32[]{:S(2)}) collective-permute-start(bf16[240,640]{1,0:T(8,128)(2,1)S(1)} %get-tuple-element.256), channel_id=1, source_target_pairs={{0,2},{1,3},{2,0},{3,1},{4,6},{5,7},{6,4},{7,5},{8,10},{9,11},{10,... | collective-permute-start | bytes 921608 | tf_op jit(solution)/shard_map/ppermute | solution.py:582
  296.6 18.0 %collective-permute-start.58 = (bf16[240,640]{1,0:T(8,128)(2,1)S(1)}, bf16[240,640]{1,0:T(8,128)(2,1)S(1)}, u32[]{:S(2)}, u32[]{:S(2)}) collective-permute-start(bf16[240,640]{1,0:T(8,128)(2,1)S(1)} %get-tuple-element.255), channel_id=1, source_target_pairs={{0,3},{1,2},{2,1},{3,0},{4,7},{5,6},{6,5},{7,4},{8,11},{9,10},{10,... | collective-permute-start | bytes 921608 | tf_op jit(solution)/shard_map/ppermute | solution.py:582
  340.2 139.2 %all-reduce.9.cloned.1.call-start = ((), (), s32[]{:S(2)}) async-start(), calls=%async_computation | async-start | bytes 3686400 | tf_op jit(solution)/shard_map/psum | solution.py:776
  340.2 16.9 %collective-permute-start.62 = (bf16[512,640]{1,0:T(8,128)(2,1)}, bf16[512,640]{1,0:T(8,128)(2,1)S(1)}, u32[]{:S(2)}, u32[]{:S(2)}) collective-permute-start(bf16[512,640]{1,0:T(8,128)(2,1)} %copy-done.108), channel_id=1, source_target_pairs={{0,3},{1,2},{2,1},{3,0},{4,7},{5,6},{6,5},{7,4},{8,11},{9,10},{10,... | collective-permute-start | bytes 1966088 | tf_op jit(solution)/shard_map/ppermute | solution.py:582
  341.4 30.7 %collective-permute-start.61 = (bf16[512,640]{1,0:T(8,128)(2,1)}, bf16[512,640]{1,0:T(8,128)(2,1)}, u32[]{:S(2)}, u32[]{:S(2)}) collective-permute-start(bf16[512,640]{1,0:T(8,128)(2,1)} %copy-done.107), channel_id=1, source_target_pairs={{0,2},{1,3},{2,0},{3,1},{4,6},{5,7},{6,4},{7,5},{8,10},{9,11},{10,... | collective-permute-start | bytes 1966088 | tf_op jit(solution)/shard_map/ppermute | solution.py:582
  342.5 29.6 %collective-permute-start.60 = (bf16[512,640]{1,0:T(8,128)(2,1)}, bf16[512,640]{1,0:T(8,128)(2,1)}, u32[]{:S(2)}, u32[]{:S(2)}) collective-permute-start(bf16[512,640]{1,0:T(8,128)(2,1)} %copy-done.106), channel_id=1, source_target_pairs={{0,1},{1,0},{2,3},{3,2},{4,5},{5,4},{6,7},{7,6},{8,9},{9,8},{10,11... | collective-permute-start | bytes 1966088 | tf_op jit(solution)/shard_map/ppermute | solution.py:582
  375.5 22.8 %collective-permute-start.64 = (bf16[128,640]{1,0:T(8,128)(2,1)}, bf16[128,640]{1,0:T(8,128)(2,1)S(1)}, u32[]{:S(2)}, u32[]{:S(2)}) collective-permute-start(bf16[128,640]{1,0:T(8,128)(2,1)} %get-tuple-element.288), channel_id=1, source_target_pairs={{0,8},{4,12},{8,0},{12,4},{1,9},{5,13},{9,1},{13,5},{2,10},{6,14},... | collective-permute-start | bytes 491528 | tf_op jit(solution)/shard_map/ppermute | solution.py:616
  378.1 21.0 %collective-permute-start.65 = (bf16[128,640]{1,0:T(8,128)(2,1)}, bf16[128,640]{1,0:T(8,128)(2,1)}, u32[]{:S(2)}, u32[]{:S(2)}) collective-permute-start(bf16[128,640]{1,0:T(8,128)(2,1)} %get-tuple-element.287), channel_id=1, source_target_pairs={{0,4},{4,8},{8,12},{12,0},{1,5},{5,9},{9,13},{13,1},{2,6},{6,10},{... | collective-permute-start | bytes 491528 | tf_op jit(solution)/shard_map/ppermute | solution.py:616
  414.6 25.1 %collective-permute-start.72 = (bf16[960,640]{1,0:T(8,128)(2,1)S(1)}, bf16[960,640]{1,0:T(8,128)(2,1)S(1)}, u32[]{:S(2)}, u32[]{:S(2)}) collective-permute-start(bf16[960,640]{1,0:T(8,128)(2,1)S(1)} %constant_dynamic-slice_fusion.10), channel_id=1, source_target_pairs={{0,16},{16,0},{1,17},{17,1},{2,18},{18,2},{3,19},{19,3},{4,20},{20... | collective-permute-start | bytes 3686408 | tf_op jit(solution)/shard_map/ppermute | solution.py:577
  422.5 14.2 %collective-permute-start.76 = (bf16[4,1,120,640]{3,2,1,0:T(8,128)(2,1)S(1)}, bf16[4,1,120,640]{3,2,1,0:T(8,128)(2,1)S(1)}, u32[]{:S(2)}, u32[]{:S(2)}) collective-permute-start(bf16[4,1,120,640]{3,2,1,0:T(8,128)(2,1)S(1)} %constant_dynamic-slice_fusion.5), channel_id=1, source_target_pairs={{0,16},{16,0},{1,17},{17,1},{2,18},{18,2},{3,19},{19,3},{4,20},{20... | collective-permute-start | bytes 1843208 | tf_op jit(solution)/shard_map/ppermute | solution.py:577
  441.6 12.9 %collective-permute-start.74 = (bf16[240,640]{1,0:T(8,128)(2,1)S(1)}, bf16[240,640]{1,0:T(8,128)(2,1)S(1)}, u32[]{:S(2)}, u32[]{:S(2)}) collective-permute-start(bf16[240,640]{1,0:T(8,128)(2,1)S(1)} %get-tuple-element.252), channel_id=1, source_target_pairs={{0,2},{1,3},{2,0},{3,1},{4,6},{5,7},{6,4},{7,5},{8,10},{9,11},{10,... | collective-permute-start | bytes 921608 | tf_op jit(solution)/shard_map/ppermute | solution.py:582
  442.3 16.0 %collective-permute-start.75 = (bf16[240,640]{1,0:T(8,128)(2,1)S(1)}, bf16[240,640]{1,0:T(8,128)(2,1)S(1)}, u32[]{:S(2)}, u32[]{:S(2)}) collective-permute-start(bf16[240,640]{1,0:T(8,128)(2,1)S(1)} %get-tuple-element.251), channel_id=1, source_target_pairs={{0,3},{1,2},{2,1},{3,0},{4,7},{5,6},{6,5},{7,4},{8,11},{9,10},{10,... | collective-permute-start | bytes 921608 | tf_op jit(solution)/shard_map/ppermute | solution.py:582
  446.6 38.1 %collective-permute-start.102 = (bf16[4,1,240,960]{3,2,1,0:T(8,128)(2,1)}, bf16[4,1,240,960]{3,2,1,0:T(8,128)(2,1)}, u32[]{:S(2)}, u32[]{:S(2)}) collective-permute-start(bf16[4,1,240,960]{3,2,1,0:T(8,128)(2,1)} %fusion.1), channel_id=1, source_target_pairs={{0,16},{16,0},{1,17},{17,1},{2,18},{18,2},{3,19},{19,3},{4,20},{20... | collective-permute-start | bytes 5529608 | tf_op jit(solution)/shard_map/ppermute | solution.py:577
  449.8 32.6 %collective-permute-start.106 = (bf16[480,640]{1,0:T(8,128)(2,1)}, bf16[480,640]{1,0:T(8,128)(2,1)}, u32[]{:S(2)}, u32[]{:S(2)}) collective-permute-start(bf16[480,640]{1,0:T(8,128)(2,1)} %constant_dynamic-slice_fusion.1), channel_id=1, source_target_pairs={{0,16},{16,0},{1,17},{17,1},{2,18},{18,2},{3,19},{19,3},{4,20},{20... | collective-permute-start | bytes 1843208 | tf_op jit(solution)/shard_map/ppermute | solution.py:577
  479.4 114.6 %all-reduce.11.cloned.1.call-start = ((), (), s32[]{:S(2)}) async-start(), calls=%async_computation.1 | async-start | bytes 3993600 | tf_op jit(solution)/shard_map/psum | solution.py:776
  479.4 17.3 %collective-permute-start.82 = (bf16[512,640]{1,0:T(8,128)(2,1)}, bf16[512,640]{1,0:T(8,128)(2,1)}, u32[]{:S(2)}, u32[]{:S(2)}) collective-permute-start(bf16[512,640]{1,0:T(8,128)(2,1)} %get-tuple-element.149), channel_id=1, source_target_pairs={{0,3},{1,2},{2,1},{3,0},{4,7},{5,6},{6,5},{7,4},{8,11},{9,10},{10,... | collective-permute-start | bytes 1966088 | tf_op jit(solution)/shard_map/ppermute | solution.py:582
  480.9 33.2 %collective-permute-start.81 = (bf16[512,640]{1,0:T(8,128)(2,1)}, bf16[512,640]{1,0:T(8,128)(2,1)}, u32[]{:S(2)}, u32[]{:S(2)}) collective-permute-start(bf16[512,640]{1,0:T(8,128)(2,1)} %get-tuple-element.148), channel_id=1, source_target_pairs={{0,2},{1,3},{2,0},{3,1},{4,6},{5,7},{6,4},{7,5},{8,10},{9,11},{10,... | collective-permute-start | bytes 1966088 | tf_op jit(solution)/shard_map/ppermute | solution.py:582
  482.0 32.0 %collective-permute-start.80 = (bf16[512,640]{1,0:T(8,128)(2,1)}, bf16[512,640]{1,0:T(8,128)(2,1)}, u32[]{:S(2)}, u32[]{:S(2)}) collective-permute-start(bf16[512,640]{1,0:T(8,128)(2,1)} %get-tuple-element.147), channel_id=1, source_target_pairs={{0,1},{1,0},{2,3},{3,2},{4,5},{5,4},{6,7},{7,6},{8,9},{9,8},{10,11... | collective-permute-start | bytes 1966088 | tf_op jit(solution)/shard_map/ppermute | solution.py:582
  490.2 63.8 %collective-permute-start.105 = (bf16[240,960]{1,0:T(8,128)(2,1)}, bf16[240,960]{1,0:T(8,128)(2,1)S(1)}, u32[]{:S(2)}, u32[]{:S(2)}) collective-permute-start(bf16[240,960]{1,0:T(8,128)(2,1)} %get-tuple-element.242), channel_id=1, source_target_pairs={{0,3},{1,2},{2,1},{3,0},{4,7},{5,6},{6,5},{7,4},{8,11},{9,10},{10,... | collective-permute-start | bytes 1382408 | tf_op jit(solution)/shard_map/ppermute | solution.py:582
  491.3 63.2 %collective-permute-start.104 = (bf16[240,960]{1,0:T(8,128)(2,1)}, bf16[240,960]{1,0:T(8,128)(2,1)}, u32[]{:S(2)}, u32[]{:S(2)}) collective-permute-start(bf16[240,960]{1,0:T(8,128)(2,1)} %get-tuple-element.243), channel_id=1, source_target_pairs={{0,2},{1,3},{2,0},{3,1},{4,6},{5,7},{6,4},{7,5},{8,10},{9,11},{10,... | collective-permute-start | bytes 1382408 | tf_op jit(solution)/shard_map/ppermute | solution.py:582
  492.4 175.8 %all-reduce.13.cloned.1.call-start = ((), (), s32[]{:S(2)}) async-start(), calls=%async_computation.2 | async-start | bytes 1966080 | tf_op jit(solution)/shard_map/psum | solution.py:776
  515.9 14.1 %collective-permute-start.83 = (bf16[128,640]{1,0:T(8,128)(2,1)S(1)}, bf16[128,640]{1,0:T(8,128)(2,1)S(1)}, u32[]{:S(2)}, u32[]{:S(2)}) collective-permute-start(bf16[128,640]{1,0:T(8,128)(2,1)S(1)} %get-tuple-element.285), channel_id=1, source_target_pairs={{0,12},{4,0},{8,4},{12,8},{1,13},{5,1},{9,5},{13,9},{2,14},{6,2},{... | collective-permute-start | bytes 491528 | tf_op jit(solution)/shard_map/ppermute | solution.py:616
  516.0 34.0 %collective-permute-start.84 = (bf16[128,640]{1,0:T(8,128)(2,1)S(1)}, bf16[128,640]{1,0:T(8,128)(2,1)S(1)}, u32[]{:S(2)}, u32[]{:S(2)}) collective-permute-start(bf16[128,640]{1,0:T(8,128)(2,1)S(1)} %get-tuple-element.284), channel_id=1, source_target_pairs={{0,8},{4,12},{8,0},{12,4},{1,9},{5,13},{9,1},{13,5},{2,10},{6,14},... | collective-permute-start | bytes 491528 | tf_op jit(solution)/shard_map/ppermute | solution.py:616
  519.7 31.3 %collective-permute-start.85 = (bf16[128,640]{1,0:T(8,128)(2,1)S(1)}, bf16[128,640]{1,0:T(8,128)(2,1)S(1)}, u32[]{:S(2)}, u32[]{:S(2)}) collective-permute-start(bf16[128,640]{1,0:T(8,128)(2,1)S(1)} %get-tuple-element.283), channel_id=1, source_target_pairs={{0,4},{4,8},{8,12},{12,0},{1,5},{5,9},{9,13},{13,1},{2,6},{6,10},{... | collective-permute-start | bytes 491528 | tf_op jit(solution)/shard_map/ppermute | solution.py:616
  530.0 24.5 %collective-permute-start.103 = (bf16[240,960]{1,0:T(8,128)(2,1)}, bf16[240,960]{1,0:T(8,128)(2,1)}, u32[]{:S(2)}, u32[]{:S(2)}) collective-permute-start(bf16[240,960]{1,0:T(8,128)(2,1)} %get-tuple-element.241), channel_id=1, source_target_pairs={{0,1},{1,0},{2,3},{3,2},{4,5},{5,4},{6,7},{7,6},{8,9},{9,8},{10,11... | collective-permute-start | bytes 1382408 | tf_op jit(solution)/shard_map/ppermute | solution.py:582
  567.4 31.2 %collective-permute-start.88 = (bf16[240,960]{1,0:T(8,128)(2,1)}, bf16[240,960]{1,0:T(8,128)(2,1)S(1)}, u32[]{:S(2)}, u32[]{:S(2)}) collective-permute-start(bf16[240,960]{1,0:T(8,128)(2,1)} %get-tuple-element.246), channel_id=1, source_target_pairs={{0,1},{1,0},{2,3},{3,2},{4,5},{5,4},{6,7},{7,6},{8,9},{9,8},{10,11... | collective-permute-start | bytes 1382408 | tf_op jit(solution)/shard_map/ppermute | solution.py:582
  568.6 30.0 %collective-permute-start.89 = (bf16[240,960]{1,0:T(8,128)(2,1)}, bf16[240,960]{1,0:T(8,128)(2,1)}, u32[]{:S(2)}, u32[]{:S(2)}) collective-permute-start(bf16[240,960]{1,0:T(8,128)(2,1)} %get-tuple-element.245), channel_id=1, source_target_pairs={{0,2},{1,3},{2,0},{3,1},{4,6},{5,7},{6,4},{7,5},{8,10},{9,11},{10,... | collective-permute-start | bytes 1382408 | tf_op jit(solution)/shard_map/ppermute | solution.py:582
  569.2 29.4 %collective-permute-start.90 = (bf16[240,960]{1,0:T(8,128)(2,1)}, bf16[240,960]{1,0:T(8,128)(2,1)}, u32[]{:S(2)}, u32[]{:S(2)}) collective-permute-start(bf16[240,960]{1,0:T(8,128)(2,1)} %get-tuple-element.244), channel_id=1, source_target_pairs={{0,3},{1,2},{2,1},{3,0},{4,7},{5,6},{6,5},{7,4},{8,11},{9,10},{10,... | collective-permute-start | bytes 1382408 | tf_op jit(solution)/shard_map/ppermute | solution.py:582
  597.0 73.9 %collective-permute-start.109 = (bf16[960,640]{1,0:T(8,128)(2,1)}, bf16[960,640]{1,0:T(8,128)(2,1)}, u32[]{:S(2)}, u32[]{:S(2)}) collective-permute-start(bf16[960,640]{1,0:T(8,128)(2,1)} %get-tuple-element.237), channel_id=1, source_target_pairs={{0,16},{16,0},{1,17},{17,1},{2,18},{18,2},{3,19},{19,3},{4,20},{20... | collective-permute-start | bytes 3686408 | tf_op jit(solution)/shard_map/ppermute | solution.py:577
  598.6 19.5 %collective-permute-start.110 = (bf16[480,640]{1,0:T(8,128)(2,1)}, bf16[480,640]{1,0:T(8,128)(2,1)}, u32[]{:S(2)}, u32[]{:S(2)}) collective-permute-start(bf16[480,640]{1,0:T(8,128)(2,1)} %broadcast_select_fusion.6), channel_id=1, source_target_pairs={{0,16},{16,0},{1,17},{17,1},{2,18},{18,2},{3,19},{19,3},{4,20},{20... | collective-permute-start | bytes 1843208 | tf_op jit(solution)/shard_map/ppermute | solution.py:577
  610.3 22.4 %collective-permute-start.100 = (bf16[128,640]{1,0:T(8,128)(2,1)S(1)}, bf16[128,640]{1,0:T(8,128)(2,1)S(1)}, u32[]{:S(2)}, u32[]{:S(2)}) collective-permute-start(bf16[128,640]{1,0:T(8,128)(2,1)S(1)} %add_convert_fusion.11.refs_0_), channel_id=1, source_target_pairs={{0,8},{4,12},{8,0},{12,4},{1,9},{5,13},{9,1},{13,5},{2,10},{6,14},... | collective-permute-start | bytes 491528 | tf_op jit(solution)/shard_map/ppermute | solution.py:603
  611.8 22.1 %collective-permute-start.101 = (bf16[128,640]{1,0:T(8,128)(2,1)S(1)}, bf16[128,640]{1,0:T(8,128)(2,1)S(1)}, u32[]{:S(2)}, u32[]{:S(2)}) collective-permute-start(bf16[128,640]{1,0:T(8,128)(2,1)S(1)} %add_convert_fusion.11.refs_0_), channel_id=1, source_target_pairs={{0,12},{4,0},{8,4},{12,8},{1,13},{5,1},{9,5},{13,9},{2,14},{6,2},{... | collective-permute-start | bytes 491528 | tf_op jit(solution)/shard_map/ppermute | solution.py:603
  618.0 18.2 %collective-permute-start.94 = (bf16[128,960]{1,0:T(8,128)(2,1)}, bf16[128,960]{1,0:T(8,128)(2,1)}, u32[]{:S(2)}, u32[]{:S(2)}) collective-permute-start(bf16[128,960]{1,0:T(8,128)(2,1)} %get-tuple-element.165), channel_id=1, source_target_pairs={{0,3},{1,2},{2,1},{3,0},{4,7},{5,6},{6,5},{7,4},{8,11},{9,10},{10,... | collective-permute-start | bytes 737288 | tf_op jit(solution)/shard_map/ppermute | solution.py:582
  621.7 14.5 %collective-permute-start.93 = (bf16[128,960]{1,0:T(8,128)(2,1)}, bf16[128,960]{1,0:T(8,128)(2,1)}, u32[]{:S(2)}, u32[]{:S(2)}) collective-permute-start(bf16[128,960]{1,0:T(8,128)(2,1)} %get-tuple-element.164), channel_id=1, source_target_pairs={{0,2},{1,3},{2,0},{3,1},{4,6},{5,7},{6,4},{7,5},{8,10},{9,11},{10,... | collective-permute-start | bytes 737288 | tf_op jit(solution)/shard_map/ppermute | solution.py:582
  (258 other events, 1792.9 us)
Sparse Core Ops, SparseCore 0:
  382.4 80.0 all-reduce.8
  492.5 101.3 all-reduce.10
  604.7 63.4 all-reduce.12

commit v4 on v3

--- a/solution.py
+++ b/solution.py
@@ -822,7 +822,7 @@
         square_grad = jnp.concatenate([blocked(out_grad), blocked(query_grad)], axis=2)
         square_half, square_pieces = rows_over_wa(square_grad, ())
         if layer == 0:
-            done = over_ctx(tie((last_square, square_half), done), 2)
+            done = over_ctx((last_square, square_half), 2)
             sums["square", layer + 1], sums["square", layer] = done
 
         grad_key, grad_u, gain_one_grad = key_back(

time: 691 us -> 694 us (level)
  waiting for transfers between devices: 287 us -> 294 us
    unnamed x418 -> x412, local copies, waits for them, and re-layouts: 59.6 us -> 58.2 us
  transfers between devices with their start and end apart: 114 -> 114, of which waited for: 45 -> 46; matrix products, arithmetic and copies ran while one was open for 12% -> 12% of each run, Pallas kernels for 11% -> 11%
where the time goes in v4:
time: 694 us; the launch traced here: 689 us
  waiting for transfers between devices  294 us (42%)
  starting transfers between devices  131 us (19%)
  Pallas kernels  98.6 us (14%)
  local copies, waits for them, and re-layouts  84.7 us (12%)
  other arithmetic  51.6 us (7%)
  between operations  16.2 us (2%)
  matrix products  12.6 us (2%)
    ppermute x72, waiting for transfers between devices, to_peer(): return lax.ppermute(value, 'wa', [(i, i ^ k) for i in range(count)])  181 us
    ppermute x72, starting transfers between devices, to_peer(): return lax.ppermute(value, 'wa', [(i, i ^ k) for i in range(count)])  67.2 us
    unnamed x412, local copies, waits for them, and re-layouts  58.2 us
    psum x3, waiting for transfers between devices, over_ctx(): return lax.psum(tuple(values), 'ctx', axis_index_groups=[order])  46.5 us
    ppermute x24, starting transfers between devices, to_sibling(): return lax.ppermute(value, 'section', [(0, 1), (1, 0)])  41.3 us
    ppermute x6, waiting for transfers between devices, scatter_ctx(): lax.ppermute(piece, 'ctx', [(i, (i - k) % count) for i in range(count)])  39.5 us
    pallas_call x2, Pallas kernels, attend_back(): pl.pallas_call(functools.partial(attend_back_kernel, count=len(groups)),...  28.9 us
    ppermute x9, waiting for transfers between devices, gather_ctx(): lax.ppermute(value, 'ctx', [(i, (i + k) % count) for i in range(count)])  25.7 us
  transfers between devices with their start and end apart: 114, of which 46 were waited for; matrix products, arithmetic and copies ran while one was open for 12% of the time, Pallas kernels for 11%

profile of v4, /device:TPU:1, one launch (start us, length us, event | category | flops | bytes accessed | tf_op | source)
XLA Modules:
  0.0 688.6 jit_solution(17716408867397395409)
XLA Ops:
  18.7 3.6 collective-permute-start.3
  23.3 10.4 %collective-permute-done.3.refs_3_ = bf16[144,1600]{1,0:T(8,128)(2,1)S(1)} collective-permute-done((bf16[144,1600]{1,0:T(8,128)(2,1)S(1)}, bf16[144,1600]{1,0:T(8,128)(2,1)S(1)}, u32[]{:S(2)}, u32[]{:S(2)}) %collective-permute-start.3) | collective-permute-done | bytes 460832 | tf_op jit(solution)/shard_map/ppermute | solution.py:582
  33.7 10.3 %collective-permute-done.2.refs_2_ = bf16[144,1600]{1,0:T(8,128)(2,1)S(1)} collective-permute-done((bf16[144,1600]{1,0:T(8,128)(2,1)S(1)}, bf16[144,1600]{1,0:T(8,128)(2,1)S(1)}, u32[]{:S(2)}, u32[]{:S(2)}) %collective-permute-start.2) | collective-permute-done | bytes 460832 | tf_op jit(solution)/shard_map/ppermute | solution.py:582
  54.1 2.4 assemble.4.refs_2_.w_ref.refs_7_
  61.1 2.3 collective-permute-start.6
  69.9 4.9 collective-permute-done.6.refs_2_
  76.9 3.9 collective-permute-done.7.refs_3_
  84.5 2.5 collective-permute-done.14.refs_3_
  90.5 2.9 bitcast_select_fusion
  94.5 4.2 collective-permute-start.18
  103.0 11.8 %collective-permute-done.17.refs_3_.refs_6_ = bf16[512,640]{1,0:T(8,128)(2,1)S(1)} collective-permute-done((bf16[512,640]{1,0:T(8,128)(2,1)}, bf16[512,640]{1,0:T(8,128)(2,1)S(1)}, u32[]{:S(2)}, u32[]{:S(2)}) %collective-permute-start.17) | collective-permute-done | bytes 655392 | tf_op jit(solution)/shard_map/ppermute | solution.py:582
  123.4 8.9 %attend.2.saved_ref.refs_4_.o_ref = f32[1920,128]{1,0:T(8,128)S(1)} custom-call(s32[128,1]{1,0:T(8,128)S(1)} %copy-done.95, s32[4,512]{1,0:T(4,128)S(1)} %pad_add_fusion.kpos_ref, bf16[128,1920]{1,0:T(8,128)(2,1)S(1)} %copy-done.168, bf16[512,640]{1,0:T(8,128)(2,1)S(1)} %copy-done.39, bf16[512,640]{1,0:T(8,128)(2,1)S(1)} %copy-done.26, ...), custom_call_target="tpu_custom_call" | custom-call | flops 11040000000 | tf_op jit(solution)/shard_map/attend/pallas_call | solution.py:227
  133.6 6.1 collective-permute-start.26
  139.8 3.0 broadcast_select_fusion.2
  153.0 3.6 collective-permute-done.23.refs_1_
  157.3 5.5 collective-permute-done.25.refs_3_
  164.5 2.4 narrow.2
  171.7 2.8 collective-permute-done.28.refs_2_
  174.5 6.2 collective-permute-done.30.refs_4_
  185.4 2.5 project.3
  190.1 2.3 collective-permute-start.33
  197.9 5.9 collective-permute-done.33.refs_2_
  212.1 4.2 collective-permute-start.44
  216.3 5.2 collective-permute-done.41.refs_1_.refs_4_
  221.6 15.5 %collective-permute-done.43.refs_3_.refs_6_ = bf16[512,640]{1,0:T(8,128)(2,1)} collective-permute-done((bf16[512,640]{1,0:T(8,128)(2,1)}, bf16[512,640]{1,0:T(8,128)(2,1)}, u32[]{:S(2)}, u32[]{:S(2)}) %collective-permute-start.43) | collective-permute-done | bytes 655392 | tf_op jit(solution)/shard_map/ppermute | solution.py:582
  237.1 2.6 collective-permute-start.47
  241.9 9.9 %attend.3.saved_ref.refs_4_.o_ref = f32[1920,128]{1,0:T(8,128)S(1)} custom-call(s32[128,1]{1,0:T(8,128)S(1)} %copy-done.96, s32[4,512]{1,0:T(4,128)S(1)} %pad_add_fusion.kpos_ref, bf16[128,1920]{1,0:T(8,128)(2,1)S(1)} %copy-done.158, bf16[512,640]{1,0:T(8,128)(2,1)S(1)} %copy-done.24, bf16[512,640]{1,0:T(8,128)(2,1)S(1)} %copy-done.35, ...), custom_call_target="tpu_custom_call" | custom-call | flops 11040000000 | tf_op jit(solution)/shard_map/attend/pallas_call | solution.py:227
  253.4 5.0 collective-permute-start.51
  268.4 3.6 collective-permute-done.48.refs_1_
  272.0 5.5 collective-permute-done.50.refs_3_
  279.9 3.4 mlp_back.2
  291.5 2.4 convolution_convert_fusion.9
  299.5 4.1 collective-permute-done.54.refs_3_
  305.7 3.6 collective-permute-done.56.refs_1_
  309.3 8.1 %collective-permute-done.57.refs_2_ = bf16[240,640]{1,0:T(8,128)(2,1)S(1)} collective-permute-done((bf16[240,640]{1,0:T(8,128)(2,1)S(1)}, bf16[240,640]{1,0:T(8,128)(2,1)S(1)}, u32[]{:S(2)}, u32[]{:S(2)}) %collective-permute-start.57) | collective-permute-done | bytes 307232 | tf_op jit(solution)/shard_map/ppermute | solution.py:582
  323.8 14.7 %attend_back.2 = (f32[128,1920]{1,0:T(8,128)S(1)}, bf16[512,640]{1,0:T(8,128)(2,1)S(1)}, bf16[512,640]{1,0:T(8,128)(2,1)S(1)}, bf16[512,640]{1,0:T(8,128)(2,1)S(1)}, bf16[512,640]{1,0:T(8,128)(2,1)S(1)}) custom-call(s32[1,128]{1,0:T(1,128)S(1)} %add.542.qpos_ref, s32[512,4]{1,0:T(8,128)S(1)} %bitcast.156, bf16[128,1920]{1,0:T(8,128)(2,1)S(1)} %copy-done.159, ...), custom_call_target="tpu_custom_call" | custom-call | flops 17479999488 | tf_op jit(solution)/shard_map/attend_back/pallas_call | solution.py:277
  345.6 14.3 %collective-permute-done.62 = bf16[512,640]{1,0:T(8,128)(2,1)S(1)} collective-permute-done((bf16[512,640]{1,0:T(8,128)(2,1)}, bf16[512,640]{1,0:T(8,128)(2,1)S(1)}, u32[]{:S(2)}, u32[]{:S(2)}) %collective-permute-start.62) | collective-permute-done | bytes 655392 | tf_op jit(solution)/shard_map/ppermute | solution.py:582
  359.9 15.0 %collective-permute-done.61 = bf16[512,640]{1,0:T(8,128)(2,1)} collective-permute-done((bf16[512,640]{1,0:T(8,128)(2,1)}, bf16[512,640]{1,0:T(8,128)(2,1)}, u32[]{:S(2)}, u32[]{:S(2)}) %collective-permute-start.61) | collective-permute-done | bytes 655392 | tf_op jit(solution)/shard_map/ppermute | solution.py:582
  388.3 13.0 %collective-permute-done.64.refs_2_ = bf16[128,640]{1,0:T(8,128)(2,1)S(1)} collective-permute-done((bf16[128,640]{1,0:T(8,128)(2,1)}, bf16[128,640]{1,0:T(8,128)(2,1)S(1)}, u32[]{:S(2)}, u32[]{:S(2)}) %collective-permute-start.64) | collective-permute-done | bytes 163872 | tf_op jit(solution)/shard_map/ppermute | solution.py:616
  405.0 2.6 collective-permute-start.68
  410.5 2.9 collective-permute-done.67.refs_2_
  413.5 2.5 mlp_back.3
  417.6 6.5 collective-permute-start.72
  429.8 3.0 collective-permute-done.69.refs_1_
  434.2 4.7 collective-permute-done.71.refs_3_
  449.6 3.7 collective-permute-start.102
  457.0 5.1 collective-permute-done.75.refs_3_
  464.6 14.2 %attend_back.3 = (f32[128,1920]{1,0:T(8,128)S(1)}, bf16[512,640]{1,0:T(8,128)(2,1)S(1)}, bf16[512,640]{1,0:T(8,128)(2,1)S(1)}, bf16[512,640]{1,0:T(8,128)(2,1)S(1)}, bf16[512,640]{1,0:T(8,128)(2,1)S(1)}) custom-call(s32[1,128]{1,0:T(1,128)S(1)} %add.542.qpos_ref, s32[512,4]{1,0:T(8,128)S(1)} %bitcast.157, bf16[128,1920]{1,0:T(8,128)(2,1)S(1)} %copy-done.169, ...), custom_call_target="tpu_custom_call" | custom-call | flops 17479999488 | tf_op jit(solution)/shard_map/attend_back/pallas_call | solution.py:277
  488.1 3.0 add_convert_fusion
  499.7 18.0 %collective-permute-done.81 = bf16[512,640]{1,0:T(8,128)(2,1)} collective-permute-done((bf16[512,640]{1,0:T(8,128)(2,1)}, bf16[512,640]{1,0:T(8,128)(2,1)}, u32[]{:S(2)}, u32[]{:S(2)}) %collective-permute-start.81) | collective-permute-done | bytes 655392 | tf_op jit(solution)/shard_map/ppermute | solution.py:582
  519.7 5.1 collective-permute-start.84
  528.9 6.2 collective-permute-done.83.refs_1_
  535.1 20.2 %collective-permute-done.84.refs_2_ = bf16[128,640]{1,0:T(8,128)(2,1)S(1)} collective-permute-done((bf16[128,640]{1,0:T(8,128)(2,1)S(1)}, bf16[128,640]{1,0:T(8,128)(2,1)S(1)}, u32[]{:S(2)}, u32[]{:S(2)}) %collective-permute-start.84) | collective-permute-done | bytes 163872 | tf_op jit(solution)/shard_map/ppermute | solution.py:616
  559.1 2.5 fusion.36
  566.8 2.8 add_convert_fusion.1
  574.6 22.7 %all-reduce.11.cloned.1.call-done = (bf16[120,640]{1,0:T(8,128)(2,1)}, bf16[960,640]{1,0:T(8,128)(2,1)}, bf16[480,640]{1,0:T(8,128)(2,1)}) async-done(((bf16[120,640]{1,0:T(8,128)(2,1)}, bf16[960,640]{1,0:T(8,128)(2,1)}, bf16[480,640]{1,0:T(8,128)(2,1)}), (bf16[120,640]{1,0:T(8,128)(2,1)}, bf16[960,640]{1,0:T(8,128)(2,1)}, bf16[480,640]{1,0:T(8,128)(2,1)})) %all-reduce.11.cloned.1.call-update) | async-done | bytes 1996816 | tf_op jit(solution)/shard_map/psum | solution.py:776
  597.3 3.0 broadcast_select_fusion
  605.4 2.6 fusion.39
  609.1 4.4 collective-permute-done.98
  618.2 2.4 narrow.3
  625.8 10.3 %collective-permute-done.100.refs_2_ = bf16[128,640]{1,0:T(8,128)(2,1)S(1)} collective-permute-done((bf16[128,640]{1,0:T(8,128)(2,1)S(1)}, bf16[128,640]{1,0:T(8,128)(2,1)S(1)}, u32[]{:S(2)}, u32[]{:S(2)}) %collective-permute-start.100) | collective-permute-done | bytes 163872 | tf_op jit(solution)/shard_map/ppermute | solution.py:603
  639.6 3.4 collective-permute-done.92
  647.9 23.7 %all-reduce.13.cloned.1.call-done = (bf16[240,960]{1,0:T(8,128)(2,1)}, bf16[240,960]{1,0:T(8,128)(2,1)}) async-done(((bf16[240,960]{1,0:T(8,128)(2,1)}, bf16[240,960]{1,0:T(8,128)(2,1)}), (bf16[240,960]{1,0:T(8,128)(2,1)}, bf16[240,960]{1,0:T(8,128)(2,1)})) %all-reduce.13.cloned.1.call-update) | async-done | bytes 921616 | tf_op jit(solution)/shard_map/psum | solution.py:776
  675.0 4.1 finish.1
  (784 shorter events, 254.1 us)
Async XLA Ops:
  10.9 35.9 %collective-permute-start.8 = (bf16[128,960]{1,0:T(8,128)(2,1)}, bf16[128,960]{1,0:T(8,128)(2,1)}, u32[]{:S(2)}, u32[]{:S(2)}) collective-permute-start(bf16[128,960]{1,0:T(8,128)(2,1)} %dynamic-slice_bitcast_fusion.8), channel_id=1, source_target_pairs={{0,16},{16,0},{1,17},{17,1},{2,18},{18,2},{3,19},{19,3},{4,20},{20... | collective-permute-start | bytes 737288 | tf_op jit(solution)/shard_map/ppermute | solution.py:577
  12.5 78.0 %collective-permute-start.19 = (bf16[240,2560]{1,0:T(8,128)(2,1)}, bf16[240,2560]{1,0:T(8,128)(2,1)}, u32[]{:S(2)}, u32[]{:S(2)}) collective-permute-start(bf16[240,2560]{1,0:T(8,128)(2,1)} %bitcast_select_fusion.1), channel_id=1, source_target_pairs={{0,16},{16,0},{1,17},{17,1},{2,18},{18,2},{3,19},{19,3},{4,20},{20... | collective-permute-start | bytes 3686408 | tf_op jit(solution)/shard_map/ppermute | solution.py:577
  18.7 15.0 %collective-permute-start.3 = (bf16[144,1600]{1,0:T(8,128)(2,1)S(1)}, bf16[144,1600]{1,0:T(8,128)(2,1)S(1)}, u32[]{:S(2)}, u32[]{:S(2)}) collective-permute-start(bf16[144,1600]{1,0:T(8,128)(2,1)S(1)} %get-tuple-element.266.refs_0_), channel_id=1, source_target_pairs={{0,3},{1,2},{2,1},{3,0},{4,7},{5,6},{6,5},{7,4},{8,11},{9,10},{10,... | collective-permute-start | bytes 1382408 | tf_op jit(solution)/shard_map/ppermute | solution.py:582
  22.3 21.7 %collective-permute-start.2 = (bf16[144,1600]{1,0:T(8,128)(2,1)S(1)}, bf16[144,1600]{1,0:T(8,128)(2,1)S(1)}, u32[]{:S(2)}, u32[]{:S(2)}) collective-permute-start(bf16[144,1600]{1,0:T(8,128)(2,1)S(1)} %get-tuple-element.266.refs_0_), channel_id=1, source_target_pairs={{0,2},{1,3},{2,0},{3,1},{4,6},{5,7},{6,4},{7,5},{8,10},{9,11},{10,... | collective-permute-start | bytes 1382408 | tf_op jit(solution)/shard_map/ppermute | solution.py:582
  22.5 21.5 %collective-permute-start.1 = (bf16[144,1600]{1,0:T(8,128)(2,1)S(1)}, bf16[144,1600]{1,0:T(8,128)(2,1)S(1)}, u32[]{:S(2)}, u32[]{:S(2)}) collective-permute-start(bf16[144,1600]{1,0:T(8,128)(2,1)S(1)} %get-tuple-element.266.refs_0_), channel_id=1, source_target_pairs={{0,1},{1,0},{2,3},{3,2},{4,5},{5,4},{6,7},{7,6},{8,9},{9,8},{10,11... | collective-permute-start | bytes 1382408 | tf_op jit(solution)/shard_map/ppermute | solution.py:582
  49.9 13.8 %collective-permute-start.10 = (bf16[128,960]{1,0:T(8,128)(2,1)}, bf16[128,960]{1,0:T(8,128)(2,1)S(1)}, u32[]{:S(2)}, u32[]{:S(2)}) collective-permute-start(bf16[128,960]{1,0:T(8,128)(2,1)} %tie.12.refs_0_), channel_id=1, source_target_pairs={{0,2},{1,3},{2,0},{3,1},{4,6},{5,7},{6,4},{7,5},{8,10},{9,11},{10,... | collective-permute-start | bytes 737288 | tf_op jit(solution)/shard_map/ppermute | solution.py:582
  50.3 13.5 %collective-permute-start.11 = (bf16[128,960]{1,0:T(8,128)(2,1)}, bf16[128,960]{1,0:T(8,128)(2,1)S(1)}, u32[]{:S(2)}, u32[]{:S(2)}) collective-permute-start(bf16[128,960]{1,0:T(8,128)(2,1)} %tie.12.refs_0_), channel_id=1, source_target_pairs={{0,3},{1,2},{2,1},{3,0},{4,7},{5,6},{6,5},{7,4},{8,11},{9,10},{10,... | collective-permute-start | bytes 737288 | tf_op jit(solution)/shard_map/ppermute | solution.py:582
  61.1 13.7 %collective-permute-start.6 = (bf16[128,640]{1,0:T(8,128)(2,1)S(1)}, bf16[128,640]{1,0:T(8,128)(2,1)S(1)}, u32[]{:S(2)}, u32[]{:S(2)}) collective-permute-start(bf16[128,640]{1,0:T(8,128)(2,1)S(1)} %get-tuple-element.93.refs_0_), channel_id=1, source_target_pairs={{0,8},{4,12},{8,0},{12,4},{1,9},{5,13},{9,1},{13,5},{2,10},{6,14},... | collective-permute-start | bytes 491528 | tf_op jit(solution)/shard_map/ppermute | solution.py:603
  64.6 19.9 %collective-permute-start.12 = (bf16[144,1600]{1,0:T(8,128)(2,1)}, bf16[144,1600]{1,0:T(8,128)(2,1)S(1)}, u32[]{:S(2)}, u32[]{:S(2)}) collective-permute-start(bf16[144,1600]{1,0:T(8,128)(2,1)} %tie.13.refs_0_), channel_id=1, source_target_pairs={{0,1},{1,0},{2,3},{3,2},{4,5},{5,4},{6,7},{7,6},{8,9},{9,8},{10,11... | collective-permute-start | bytes 1382408 | tf_op jit(solution)/shard_map/ppermute | solution.py:582
  65.8 18.7 %collective-permute-start.13 = (bf16[144,1600]{1,0:T(8,128)(2,1)}, bf16[144,1600]{1,0:T(8,128)(2,1)S(1)}, u32[]{:S(2)}, u32[]{:S(2)}) collective-permute-start(bf16[144,1600]{1,0:T(8,128)(2,1)} %tie.13.refs_0_), channel_id=1, source_target_pairs={{0,2},{1,3},{2,0},{3,1},{4,6},{5,7},{6,4},{7,5},{8,10},{9,11},{10,... | collective-permute-start | bytes 1382408 | tf_op jit(solution)/shard_map/ppermute | solution.py:582
  66.6 20.4 %collective-permute-start.14 = (bf16[144,1600]{1,0:T(8,128)(2,1)}, bf16[144,1600]{1,0:T(8,128)(2,1)S(1)}, u32[]{:S(2)}, u32[]{:S(2)}) collective-permute-start(bf16[144,1600]{1,0:T(8,128)(2,1)} %tie.13.refs_0_), channel_id=1, source_target_pairs={{0,3},{1,2},{2,1},{3,0},{4,7},{5,6},{6,5},{7,4},{8,11},{9,10},{10,... | collective-permute-start | bytes 1382408 | tf_op jit(solution)/shard_map/ppermute | solution.py:582
  80.9 58.9 %collective-permute-start.27 = (bf16[960,640]{1,0:T(8,128)(2,1)}, bf16[960,640]{1,0:T(8,128)(2,1)}, u32[]{:S(2)}, u32[]{:S(2)}) collective-permute-start(bf16[960,640]{1,0:T(8,128)(2,1)} %bitcast.170), channel_id=1, source_target_pairs={{0,16},{16,0},{1,17},{17,1},{2,18},{18,2},{3,19},{19,3},{4,20},{20... | collective-permute-start | bytes 3686408 | tf_op jit(solution)/shard_map/ppermute | solution.py:577
  87.8 13.1 %collective-permute-start.15 = (bf16[512,640]{1,0:T(8,128)(2,1)}, bf16[512,640]{1,0:T(8,128)(2,1)S(1)}, u32[]{:S(2)}, u32[]{:S(2)}) collective-permute-start(bf16[512,640]{1,0:T(8,128)(2,1)} %tie.14.refs_0_), channel_id=1, source_target_pairs={{0,1},{1,0},{2,3},{3,2},{4,5},{5,4},{6,7},{7,6},{8,9},{9,8},{10,11... | collective-permute-start | bytes 1966088 | tf_op jit(solution)/shard_map/ppermute | solution.py:582
  88.3 14.7 %collective-permute-start.16 = (bf16[512,640]{1,0:T(8,128)(2,1)}, bf16[512,640]{1,0:T(8,128)(2,1)S(1)}, u32[]{:S(2)}, u32[]{:S(2)}) collective-permute-start(bf16[512,640]{1,0:T(8,128)(2,1)} %tie.14.refs_0_), channel_id=1, source_target_pairs={{0,2},{1,3},{2,0},{3,1},{4,6},{5,7},{6,4},{7,5},{8,10},{9,11},{10,... | collective-permute-start | bytes 1966088 | tf_op jit(solution)/shard_map/ppermute | solution.py:582
  89.3 25.4 %collective-permute-start.17 = (bf16[512,640]{1,0:T(8,128)(2,1)}, bf16[512,640]{1,0:T(8,128)(2,1)S(1)}, u32[]{:S(2)}, u32[]{:S(2)}) collective-permute-start(bf16[512,640]{1,0:T(8,128)(2,1)} %tie.14.refs_0_), channel_id=1, source_target_pairs={{0,3},{1,2},{2,1},{3,0},{4,7},{5,6},{6,5},{7,4},{8,11},{9,10},{10,... | collective-permute-start | bytes 1966088 | tf_op jit(solution)/shard_map/ppermute | solution.py:582
  94.5 49.4 %collective-permute-start.18 = (bf16[512,1024]{1,0:T(8,128)(2,1)}, bf16[512,1024]{1,0:T(8,128)(2,1)}, u32[]{:S(2)}, u32[]{:S(2)}) collective-permute-start(bf16[512,1024]{1,0:T(8,128)(2,1)} %join.13.mine_ref), channel_id=1, source_target_pairs={{0,16},{16,0},{1,17},{17,1},{2,18},{18,2},{3,19},{19,3},{4,20},{20... | collective-permute-start | bytes 3145736 | tf_op jit(solution)/shard_map/ppermute | solution.py:577
  115.6 16.7 %collective-permute-start.20 = (bf16[240,640]{1,0:T(8,128)(2,1)}, bf16[240,640]{1,0:T(8,128)(2,1)S(1)}, u32[]{:S(2)}, u32[]{:S(2)}) collective-permute-start(bf16[240,640]{1,0:T(8,128)(2,1)} %get-tuple-element.96), channel_id=1, source_target_pairs={{0,1},{1,0},{2,3},{3,2},{4,5},{5,4},{6,7},{7,6},{8,9},{9,8},{10,11... | collective-permute-start | bytes 921608 | tf_op jit(solution)/shard_map/ppermute | solution.py:582
  117.1 15.2 %collective-permute-start.21 = (bf16[240,640]{1,0:T(8,128)(2,1)}, bf16[240,640]{1,0:T(8,128)(2,1)S(1)}, u32[]{:S(2)}, u32[]{:S(2)}) collective-permute-start(bf16[240,640]{1,0:T(8,128)(2,1)} %get-tuple-element.97), channel_id=1, source_target_pairs={{0,2},{1,3},{2,0},{3,1},{4,6},{5,7},{6,4},{7,5},{8,10},{9,11},{10,... | collective-permute-start | bytes 921608 | tf_op jit(solution)/shard_map/ppermute | solution.py:582
  118.3 14.1 %collective-permute-start.22 = (bf16[240,640]{1,0:T(8,128)(2,1)}, bf16[240,640]{1,0:T(8,128)(2,1)S(1)}, u32[]{:S(2)}, u32[]{:S(2)}) collective-permute-start(bf16[240,640]{1,0:T(8,128)(2,1)} %get-tuple-element.98), channel_id=1, source_target_pairs={{0,3},{1,2},{2,1},{3,0},{4,7},{5,6},{6,5},{7,4},{8,11},{9,10},{10,... | collective-permute-start | bytes 921608 | tf_op jit(solution)/shard_map/ppermute | solution.py:582
  133.6 17.4 %collective-permute-start.26 = (bf16[960,640]{1,0:T(8,128)(2,1)}, bf16[960,640]{1,0:T(8,128)(2,1)}, u32[]{:S(2)}, u32[]{:S(2)}) collective-permute-start(bf16[960,640]{1,0:T(8,128)(2,1)} %join.14.mine_ref), channel_id=1, source_target_pairs={{0,16},{16,0},{1,17},{17,1},{2,18},{18,2},{3,19},{19,3},{4,20},{20... | collective-permute-start | bytes 3686408 | tf_op jit(solution)/shard_map/ppermute | solution.py:577
  142.9 40.6 %collective-permute-start.31 = (bf16[576,1664]{1,0:T(8,128)(2,1)S(1)}, bf16[576,1664]{1,0:T(8,128)(2,1)}, u32[]{:S(2)}, u32[]{:S(2)}) collective-permute-start(bf16[576,1664]{1,0:T(8,128)(2,1)S(1)} %join.15.mine_ref), channel_id=1, source_target_pairs={{0,16},{16,0},{1,17},{17,1},{2,18},{18,2},{3,19},{19,3},{4,20},{20... | collective-permute-start | bytes 5750792 | tf_op jit(solution)/shard_map/ppermute | solution.py:577
  149.5 13.4 %collective-permute-start.25 = (bf16[128,960]{1,0:T(8,128)(2,1)}, bf16[128,960]{1,0:T(8,128)(2,1)S(1)}, u32[]{:S(2)}, u32[]{:S(2)}) collective-permute-start(bf16[128,960]{1,0:T(8,128)(2,1)} %tie.16.refs_0_), channel_id=1, source_target_pairs={{0,3},{1,2},{2,1},{3,0},{4,7},{5,6},{6,5},{7,4},{8,11},{9,10},{10,... | collective-permute-start | bytes 737288 | tf_op jit(solution)/shard_map/ppermute | solution.py:582
  190.1 13.7 %collective-permute-start.33 = (bf16[128,640]{1,0:T(8,128)(2,1)S(1)}, bf16[128,640]{1,0:T(8,128)(2,1)S(1)}, u32[]{:S(2)}, u32[]{:S(2)}) collective-permute-start(bf16[128,640]{1,0:T(8,128)(2,1)S(1)} %get-tuple-element.107.refs_0_), channel_id=1, source_target_pairs={{0,8},{4,12},{8,0},{12,4},{1,9},{5,13},{9,1},{13,5},{2,10},{6,14},... | collective-permute-start | bytes 491528 | tf_op jit(solution)/shard_map/ppermute | solution.py:603
  208.4 13.2 %collective-permute-start.41 = (bf16[512,640]{1,0:T(8,128)(2,1)}, bf16[512,640]{1,0:T(8,128)(2,1)S(1)}, u32[]{:S(2)}, u32[]{:S(2)}) collective-permute-start(bf16[512,640]{1,0:T(8,128)(2,1)} %tie.19.refs_0_), channel_id=1, source_target_pairs={{0,1},{1,0},{2,3},{3,2},{4,5},{5,4},{6,7},{7,6},{8,9},{9,8},{10,11... | collective-permute-start | bytes 1966088 | tf_op jit(solution)/shard_map/ppermute | solution.py:582
  208.4 13.2 %collective-permute-start.42 = (bf16[512,640]{1,0:T(8,128)(2,1)}, bf16[512,640]{1,0:T(8,128)(2,1)}, u32[]{:S(2)}, u32[]{:S(2)}) collective-permute-start(bf16[512,640]{1,0:T(8,128)(2,1)} %tie.19.refs_0_), channel_id=1, source_target_pairs={{0,2},{1,3},{2,0},{3,1},{4,6},{5,7},{6,4},{7,5},{8,10},{9,11},{10,... | collective-permute-start | bytes 1966088 | tf_op jit(solution)/shard_map/ppermute | solution.py:582
  209.4 27.7 %collective-permute-start.43 = (bf16[512,640]{1,0:T(8,128)(2,1)}, bf16[512,640]{1,0:T(8,128)(2,1)}, u32[]{:S(2)}, u32[]{:S(2)}) collective-permute-start(bf16[512,640]{1,0:T(8,128)(2,1)} %tie.19.refs_0_), channel_id=1, source_target_pairs={{0,3},{1,2},{2,1},{3,0},{4,7},{5,6},{6,5},{7,4},{8,11},{9,10},{10,... | collective-permute-start | bytes 1966088 | tf_op jit(solution)/shard_map/ppermute | solution.py:582
  212.1 46.4 %collective-permute-start.44 = (bf16[512,1024]{1,0:T(8,128)(2,1)}, bf16[512,1024]{1,0:T(8,128)(2,1)}, u32[]{:S(2)}, u32[]{:S(2)}) collective-permute-start(bf16[512,1024]{1,0:T(8,128)(2,1)} %join.17.mine_ref), channel_id=1, source_target_pairs={{0,16},{16,0},{1,17},{17,1},{2,18},{18,2},{3,19},{19,3},{4,20},{20... | collective-permute-start | bytes 3145736 | tf_op jit(solution)/shard_map/ppermute | solution.py:577
  237.1 14.7 %collective-permute-start.45 = (bf16[240,640]{1,0:T(8,128)(2,1)}, bf16[240,640]{1,0:T(8,128)(2,1)S(1)}, u32[]{:S(2)}, u32[]{:S(2)}) collective-permute-start(bf16[240,640]{1,0:T(8,128)(2,1)} %get-tuple-element.110), channel_id=1, source_target_pairs={{0,1},{1,0},{2,3},{3,2},{4,5},{5,4},{6,7},{7,6},{8,9},{9,8},{10,11... | collective-permute-start | bytes 921608 | tf_op jit(solution)/shard_map/ppermute | solution.py:582
  237.1 14.8 %collective-permute-start.46 = (bf16[240,640]{1,0:T(8,128)(2,1)}, bf16[240,640]{1,0:T(8,128)(2,1)S(1)}, u32[]{:S(2)}, u32[]{:S(2)}) collective-permute-start(bf16[240,640]{1,0:T(8,128)(2,1)} %get-tuple-element.111), channel_id=1, source_target_pairs={{0,2},{1,3},{2,0},{3,1},{4,6},{5,7},{6,4},{7,5},{8,10},{9,11},{10,... | collective-permute-start | bytes 921608 | tf_op jit(solution)/shard_map/ppermute | solution.py:582
  237.1 14.8 %collective-permute-start.47 = (bf16[240,640]{1,0:T(8,128)(2,1)}, bf16[240,640]{1,0:T(8,128)(2,1)S(1)}, u32[]{:S(2)}, u32[]{:S(2)}) collective-permute-start(bf16[240,640]{1,0:T(8,128)(2,1)} %get-tuple-element.112), channel_id=1, source_target_pairs={{0,3},{1,2},{2,1},{3,0},{4,7},{5,6},{6,5},{7,4},{8,11},{9,10},{10,... | collective-permute-start | bytes 921608 | tf_op jit(solution)/shard_map/ppermute | solution.py:582
  290.2 13.4 %collective-permute-start.54 = (bf16[128,960]{1,0:T(8,128)(2,1)}, bf16[128,960]{1,0:T(8,128)(2,1)S(1)}, u32[]{:S(2)}, u32[]{:S(2)}) collective-permute-start(bf16[128,960]{1,0:T(8,128)(2,1)} %copy-done.112), channel_id=1, source_target_pairs={{0,3},{1,2},{2,1},{3,0},{4,7},{5,6},{6,5},{7,4},{8,11},{9,10},{10,... | collective-permute-start | bytes 737288 | tf_op jit(solution)/shard_map/ppermute | solution.py:582
  298.2 19.2 %collective-permute-start.57 = (bf16[240,640]{1,0:T(8,128)(2,1)S(1)}, bf16[240,640]{1,0:T(8,128)(2,1)S(1)}, u32[]{:S(2)}, u32[]{:S(2)}) collective-permute-start(bf16[240,640]{1,0:T(8,128)(2,1)S(1)} %get-tuple-element.252), channel_id=1, source_target_pairs={{0,2},{1,3},{2,0},{3,1},{4,6},{5,7},{6,4},{7,5},{8,10},{9,11},{10,... | collective-permute-start | bytes 921608 | tf_op jit(solution)/shard_map/ppermute | solution.py:582
  298.3 19.0 %collective-permute-start.58 = (bf16[240,640]{1,0:T(8,128)(2,1)S(1)}, bf16[240,640]{1,0:T(8,128)(2,1)S(1)}, u32[]{:S(2)}, u32[]{:S(2)}) collective-permute-start(bf16[240,640]{1,0:T(8,128)(2,1)S(1)} %get-tuple-element.251), channel_id=1, source_target_pairs={{0,3},{1,2},{2,1},{3,0},{4,7},{5,6},{6,5},{7,4},{8,11},{9,10},{10,... | collective-permute-start | bytes 921608 | tf_op jit(solution)/shard_map/ppermute | solution.py:582
  342.9 140.3 %all-reduce.9.cloned.1.call-start = ((), (), s32[]{:S(2)}) async-start(), calls=%async_computation | async-start | bytes 3686400 | tf_op jit(solution)/shard_map/psum | solution.py:776
  342.9 16.9 %collective-permute-start.62 = (bf16[512,640]{1,0:T(8,128)(2,1)}, bf16[512,640]{1,0:T(8,128)(2,1)S(1)}, u32[]{:S(2)}, u32[]{:S(2)}) collective-permute-start(bf16[512,640]{1,0:T(8,128)(2,1)} %copy-done.105), channel_id=1, source_target_pairs={{0,3},{1,2},{2,1},{3,0},{4,7},{5,6},{6,5},{7,4},{8,11},{9,10},{10,... | collective-permute-start | bytes 1966088 | tf_op jit(solution)/shard_map/ppermute | solution.py:582
  344.1 30.7 %collective-permute-start.61 = (bf16[512,640]{1,0:T(8,128)(2,1)}, bf16[512,640]{1,0:T(8,128)(2,1)}, u32[]{:S(2)}, u32[]{:S(2)}) collective-permute-start(bf16[512,640]{1,0:T(8,128)(2,1)} %copy-done.104), channel_id=1, source_target_pairs={{0,2},{1,3},{2,0},{3,1},{4,6},{5,7},{6,4},{7,5},{8,10},{9,11},{10,... | collective-permute-start | bytes 1966088 | tf_op jit(solution)/shard_map/ppermute | solution.py:582
  344.1 30.7 %collective-permute-start.60 = (bf16[512,640]{1,0:T(8,128)(2,1)}, bf16[512,640]{1,0:T(8,128)(2,1)}, u32[]{:S(2)}, u32[]{:S(2)}) collective-permute-start(bf16[512,640]{1,0:T(8,128)(2,1)} %copy-done.103), channel_id=1, source_target_pairs={{0,1},{1,0},{2,3},{3,2},{4,5},{5,4},{6,7},{7,6},{8,9},{9,8},{10,11... | collective-permute-start | bytes 1966088 | tf_op jit(solution)/shard_map/ppermute | solution.py:582
  379.6 21.8 %collective-permute-start.64 = (bf16[128,640]{1,0:T(8,128)(2,1)}, bf16[128,640]{1,0:T(8,128)(2,1)S(1)}, u32[]{:S(2)}, u32[]{:S(2)}) collective-permute-start(bf16[128,640]{1,0:T(8,128)(2,1)} %get-tuple-element.284), channel_id=1, source_target_pairs={{0,8},{4,12},{8,0},{12,4},{1,9},{5,13},{9,1},{13,5},{2,10},{6,14},... | collective-permute-start | bytes 491528 | tf_op jit(solution)/shard_map/ppermute | solution.py:616
  381.1 20.9 %collective-permute-start.65 = (bf16[128,640]{1,0:T(8,128)(2,1)}, bf16[128,640]{1,0:T(8,128)(2,1)}, u32[]{:S(2)}, u32[]{:S(2)}) collective-permute-start(bf16[128,640]{1,0:T(8,128)(2,1)} %get-tuple-element.283), channel_id=1, source_target_pairs={{0,4},{4,8},{8,12},{12,0},{1,5},{5,9},{9,13},{13,1},{2,6},{6,10},{... | collective-permute-start | bytes 491528 | tf_op jit(solution)/shard_map/ppermute | solution.py:616
  417.6 25.4 %collective-permute-start.72 = (bf16[960,640]{1,0:T(8,128)(2,1)S(1)}, bf16[960,640]{1,0:T(8,128)(2,1)S(1)}, u32[]{:S(2)}, u32[]{:S(2)}) collective-permute-start(bf16[960,640]{1,0:T(8,128)(2,1)S(1)} %constant_dynamic-slice_fusion.10), channel_id=1, source_target_pairs={{0,16},{16,0},{1,17},{17,1},{2,18},{18,2},{3,19},{19,3},{4,20},{20... | collective-permute-start | bytes 3686408 | tf_op jit(solution)/shard_map/ppermute | solution.py:577
  424.7 15.3 %collective-permute-start.76 = (bf16[4,1,120,640]{3,2,1,0:T(8,128)(2,1)S(1)}, bf16[4,1,120,640]{3,2,1,0:T(8,128)(2,1)S(1)}, u32[]{:S(2)}, u32[]{:S(2)}) collective-permute-start(bf16[4,1,120,640]{3,2,1,0:T(8,128)(2,1)S(1)} %constant_dynamic-slice_fusion.5), channel_id=1, source_target_pairs={{0,16},{16,0},{1,17},{17,1},{2,18},{18,2},{3,19},{19,3},{4,20},{20... | collective-permute-start | bytes 1843208 | tf_op jit(solution)/shard_map/ppermute | solution.py:577
  445.7 16.4 %collective-permute-start.75 = (bf16[240,640]{1,0:T(8,128)(2,1)S(1)}, bf16[240,640]{1,0:T(8,128)(2,1)S(1)}, u32[]{:S(2)}, u32[]{:S(2)}) collective-permute-start(bf16[240,640]{1,0:T(8,128)(2,1)S(1)} %get-tuple-element.247), channel_id=1, source_target_pairs={{0,3},{1,2},{2,1},{3,0},{4,7},{5,6},{6,5},{7,4},{8,11},{9,10},{10,... | collective-permute-start | bytes 921608 | tf_op jit(solution)/shard_map/ppermute | solution.py:582
  449.6 38.4 %collective-permute-start.102 = (bf16[4,1,240,960]{3,2,1,0:T(8,128)(2,1)}, bf16[4,1,240,960]{3,2,1,0:T(8,128)(2,1)}, u32[]{:S(2)}, u32[]{:S(2)}) collective-permute-start(bf16[4,1,240,960]{3,2,1,0:T(8,128)(2,1)} %fusion.1), channel_id=1, source_target_pairs={{0,16},{16,0},{1,17},{17,1},{2,18},{18,2},{3,19},{19,3},{4,20},{20... | collective-permute-start | bytes 5529608 | tf_op jit(solution)/shard_map/ppermute | solution.py:577
  453.4 32.4 %collective-permute-start.109 = (bf16[480,640]{1,0:T(8,128)(2,1)}, bf16[480,640]{1,0:T(8,128)(2,1)}, u32[]{:S(2)}, u32[]{:S(2)}) collective-permute-start(bf16[480,640]{1,0:T(8,128)(2,1)} %constant_dynamic-slice_fusion.1), channel_id=1, source_target_pairs={{0,16},{16,0},{1,17},{17,1},{2,18},{18,2},{3,19},{19,3},{4,20},{20... | collective-permute-start | bytes 1843208 | tf_op jit(solution)/shard_map/ppermute | solution.py:577
  483.2 114.2 %all-reduce.11.cloned.1.call-start = ((), (), s32[]{:S(2)}) async-start(), calls=%async_computation.1 | async-start | bytes 3993600 | tf_op jit(solution)/shard_map/psum | solution.py:776
  483.2 16.5 %collective-permute-start.82 = (bf16[512,640]{1,0:T(8,128)(2,1)}, bf16[512,640]{1,0:T(8,128)(2,1)}, u32[]{:S(2)}, u32[]{:S(2)}) collective-permute-start(bf16[512,640]{1,0:T(8,128)(2,1)} %get-tuple-element.147), channel_id=1, source_target_pairs={{0,3},{1,2},{2,1},{3,0},{4,7},{5,6},{6,5},{7,4},{8,11},{9,10},{10,... | collective-permute-start | bytes 1966088 | tf_op jit(solution)/shard_map/ppermute | solution.py:582
  485.0 32.8 %collective-permute-start.81 = (bf16[512,640]{1,0:T(8,128)(2,1)}, bf16[512,640]{1,0:T(8,128)(2,1)}, u32[]{:S(2)}, u32[]{:S(2)}) collective-permute-start(bf16[512,640]{1,0:T(8,128)(2,1)} %get-tuple-element.146), channel_id=1, source_target_pairs={{0,2},{1,3},{2,0},{3,1},{4,6},{5,7},{6,4},{7,5},{8,10},{9,11},{10,... | collective-permute-start | bytes 1966088 | tf_op jit(solution)/shard_map/ppermute | solution.py:582
  485.0 32.8 %collective-permute-start.80 = (bf16[512,640]{1,0:T(8,128)(2,1)}, bf16[512,640]{1,0:T(8,128)(2,1)}, u32[]{:S(2)}, u32[]{:S(2)}) collective-permute-start(bf16[512,640]{1,0:T(8,128)(2,1)} %get-tuple-element.145), channel_id=1, source_target_pairs={{0,1},{1,0},{2,3},{3,2},{4,5},{5,4},{6,7},{7,6},{8,9},{9,8},{10,11... | collective-permute-start | bytes 1966088 | tf_op jit(solution)/shard_map/ppermute | solution.py:582
  493.6 65.1 %collective-permute-start.105 = (bf16[240,960]{1,0:T(8,128)(2,1)}, bf16[240,960]{1,0:T(8,128)(2,1)S(1)}, u32[]{:S(2)}, u32[]{:S(2)}) collective-permute-start(bf16[240,960]{1,0:T(8,128)(2,1)} %get-tuple-element.238), channel_id=1, source_target_pairs={{0,3},{1,2},{2,1},{3,0},{4,7},{5,6},{6,5},{7,4},{8,11},{9,10},{10,... | collective-permute-start | bytes 1382408 | tf_op jit(solution)/shard_map/ppermute | solution.py:582
  495.4 63.7 %collective-permute-start.104 = (bf16[240,960]{1,0:T(8,128)(2,1)}, bf16[240,960]{1,0:T(8,128)(2,1)}, u32[]{:S(2)}, u32[]{:S(2)}) collective-permute-start(bf16[240,960]{1,0:T(8,128)(2,1)} %get-tuple-element.239), channel_id=1, source_target_pairs={{0,2},{1,3},{2,0},{3,1},{4,6},{5,7},{6,4},{7,5},{8,10},{9,11},{10,... | collective-permute-start | bytes 1382408 | tf_op jit(solution)/shard_map/ppermute | solution.py:582
  495.4 176.2 %all-reduce.13.cloned.1.call-start = ((), (), s32[]{:S(2)}) async-start(), calls=%async_computation.2 | async-start | bytes 1966080 | tf_op jit(solution)/shard_map/psum | solution.py:776
  519.7 15.5 %collective-permute-start.83 = (bf16[128,640]{1,0:T(8,128)(2,1)S(1)}, bf16[128,640]{1,0:T(8,128)(2,1)S(1)}, u32[]{:S(2)}, u32[]{:S(2)}) collective-permute-start(bf16[128,640]{1,0:T(8,128)(2,1)S(1)} %get-tuple-element.281), channel_id=1, source_target_pairs={{0,12},{4,0},{8,4},{12,8},{1,13},{5,1},{9,5},{13,9},{2,14},{6,2},{... | collective-permute-start | bytes 491528 | tf_op jit(solution)/shard_map/ppermute | solution.py:616
  519.7 35.6 %collective-permute-start.84 = (bf16[128,640]{1,0:T(8,128)(2,1)S(1)}, bf16[128,640]{1,0:T(8,128)(2,1)S(1)}, u32[]{:S(2)}, u32[]{:S(2)}) collective-permute-start(bf16[128,640]{1,0:T(8,128)(2,1)S(1)} %get-tuple-element.280), channel_id=1, source_target_pairs={{0,8},{4,12},{8,0},{12,4},{1,9},{5,13},{9,1},{13,5},{2,10},{6,14},... | collective-permute-start | bytes 491528 | tf_op jit(solution)/shard_map/ppermute | solution.py:616
  524.8 30.8 %collective-permute-start.85 = (bf16[128,640]{1,0:T(8,128)(2,1)S(1)}, bf16[128,640]{1,0:T(8,128)(2,1)S(1)}, u32[]{:S(2)}, u32[]{:S(2)}) collective-permute-start(bf16[128,640]{1,0:T(8,128)(2,1)S(1)} %get-tuple-element.279), channel_id=1, source_target_pairs={{0,4},{4,8},{8,12},{12,0},{1,5},{5,9},{9,13},{13,1},{2,6},{6,10},{... | collective-permute-start | bytes 491528 | tf_op jit(solution)/shard_map/ppermute | solution.py:616
  535.1 24.0 %collective-permute-start.103 = (bf16[240,960]{1,0:T(8,128)(2,1)}, bf16[240,960]{1,0:T(8,128)(2,1)}, u32[]{:S(2)}, u32[]{:S(2)}) collective-permute-start(bf16[240,960]{1,0:T(8,128)(2,1)} %get-tuple-element.237), channel_id=1, source_target_pairs={{0,1},{1,0},{2,3},{3,2},{4,5},{5,4},{6,7},{7,6},{8,9},{9,8},{10,11... | collective-permute-start | bytes 1382408 | tf_op jit(solution)/shard_map/ppermute | solution.py:582
  572.0 30.0 %collective-permute-start.88 = (bf16[240,960]{1,0:T(8,128)(2,1)}, bf16[240,960]{1,0:T(8,128)(2,1)S(1)}, u32[]{:S(2)}, u32[]{:S(2)}) collective-permute-start(bf16[240,960]{1,0:T(8,128)(2,1)} %get-tuple-element.242), channel_id=1, source_target_pairs={{0,1},{1,0},{2,3},{3,2},{4,5},{5,4},{6,7},{7,6},{8,9},{9,8},{10,11... | collective-permute-start | bytes 1382408 | tf_op jit(solution)/shard_map/ppermute | solution.py:582
  572.8 29.2 %collective-permute-start.89 = (bf16[240,960]{1,0:T(8,128)(2,1)}, bf16[240,960]{1,0:T(8,128)(2,1)}, u32[]{:S(2)}, u32[]{:S(2)}) collective-permute-start(bf16[240,960]{1,0:T(8,128)(2,1)} %get-tuple-element.241), channel_id=1, source_target_pairs={{0,2},{1,3},{2,0},{3,1},{4,6},{5,7},{6,4},{7,5},{8,10},{9,11},{10,... | collective-permute-start | bytes 1382408 | tf_op jit(solution)/shard_map/ppermute | solution.py:582
  574.5 27.4 %collective-permute-start.90 = (bf16[240,960]{1,0:T(8,128)(2,1)}, bf16[240,960]{1,0:T(8,128)(2,1)}, u32[]{:S(2)}, u32[]{:S(2)}) collective-permute-start(bf16[240,960]{1,0:T(8,128)(2,1)} %get-tuple-element.240), channel_id=1, source_target_pairs={{0,3},{1,2},{2,1},{3,0},{4,7},{5,6},{6,5},{7,4},{8,11},{9,10},{10,... | collective-permute-start | bytes 1382408 | tf_op jit(solution)/shard_map/ppermute | solution.py:582
  600.4 74.6 %collective-permute-start.108 = (bf16[960,640]{1,0:T(8,128)(2,1)}, bf16[960,640]{1,0:T(8,128)(2,1)}, u32[]{:S(2)}, u32[]{:S(2)}) collective-permute-start(bf16[960,640]{1,0:T(8,128)(2,1)} %get-tuple-element.233), channel_id=1, source_target_pairs={{0,16},{16,0},{1,17},{17,1},{2,18},{18,2},{3,19},{19,3},{4,20},{20... | collective-permute-start | bytes 3686408 | tf_op jit(solution)/shard_map/ppermute | solution.py:577
  601.9 18.6 %collective-permute-start.110 = (bf16[480,640]{1,0:T(8,128)(2,1)}, bf16[480,640]{1,0:T(8,128)(2,1)}, u32[]{:S(2)}, u32[]{:S(2)}) collective-permute-start(bf16[480,640]{1,0:T(8,128)(2,1)} %broadcast_select_fusion.6), channel_id=1, source_target_pairs={{0,16},{16,0},{1,17},{17,1},{2,18},{18,2},{3,19},{19,3},{4,20},{20... | collective-permute-start | bytes 1843208 | tf_op jit(solution)/shard_map/ppermute | solution.py:577
  613.6 22.4 %collective-permute-start.100 = (bf16[128,640]{1,0:T(8,128)(2,1)S(1)}, bf16[128,640]{1,0:T(8,128)(2,1)S(1)}, u32[]{:S(2)}, u32[]{:S(2)}) collective-permute-start(bf16[128,640]{1,0:T(8,128)(2,1)S(1)} %add_convert_fusion.11.refs_0_), channel_id=1, source_target_pairs={{0,8},{4,12},{8,0},{12,4},{1,9},{5,13},{9,1},{13,5},{2,10},{6,14},... | collective-permute-start | bytes 491528 | tf_op jit(solution)/shard_map/ppermute | solution.py:603
  615.2 22.1 %collective-permute-start.101 = (bf16[128,640]{1,0:T(8,128)(2,1)S(1)}, bf16[128,640]{1,0:T(8,128)(2,1)S(1)}, u32[]{:S(2)}, u32[]{:S(2)}) collective-permute-start(bf16[128,640]{1,0:T(8,128)(2,1)S(1)} %add_convert_fusion.11.refs_0_), channel_id=1, source_target_pairs={{0,12},{4,0},{8,4},{12,8},{1,13},{5,1},{9,5},{13,9},{2,14},{6,2},{... | collective-permute-start | bytes 491528 | tf_op jit(solution)/shard_map/ppermute | solution.py:603
  620.5 19.1 %collective-permute-start.94 = (bf16[128,960]{1,0:T(8,128)(2,1)}, bf16[128,960]{1,0:T(8,128)(2,1)S(1)}, u32[]{:S(2)}, u32[]{:S(2)}) collective-permute-start(bf16[128,960]{1,0:T(8,128)(2,1)} %get-tuple-element.163), channel_id=1, source_target_pairs={{0,3},{1,2},{2,1},{3,0},{4,7},{5,6},{6,5},{7,4},{8,11},{9,10},{10,... | collective-permute-start | bytes 737288 | tf_op jit(solution)/shard_map/ppermute | solution.py:582
  624.4 15.2 %collective-permute-start.93 = (bf16[128,960]{1,0:T(8,128)(2,1)}, bf16[128,960]{1,0:T(8,128)(2,1)}, u32[]{:S(2)}, u32[]{:S(2)}) collective-permute-start(bf16[128,960]{1,0:T(8,128)(2,1)} %get-tuple-element.162), channel_id=1, source_target_pairs={{0,2},{1,3},{2,0},{3,1},{4,6},{5,7},{6,4},{7,5},{8,10},{9,11},{10,... | collective-permute-start | bytes 737288 | tf_op jit(solution)/shard_map/ppermute | solution.py:582
  (255 other events, 1730.1 us)
Sparse Core Ops, SparseCore 0:
  384.2 82.1 all-reduce.8
  495.5 101.7 all-reduce.10
  608.1 63.4 all-reduce.12
